TPU v7x, 768 devices: a whole 4x8x12 slice. The times are simulated.
768 devices in a mesh: seq: 96 (over y, z), head: 8 (over x, core).
Axes of the slice: x: 4, y: 8, z: 12, core: 2. Of those that a mesh axis runs over, the one named last changes fastest.
Arguments:
- hidden: bfloat16 [12288, 2048], P('seq', 'head'), may hold values from -6 to 6
- beta_weight: bfloat16 [2048, 16], P('head'), may hold values from -0.125 to 0.125
- beta_bias: float32 [16], P('head'), as said below
- queries: bfloat16 [12288, 2048], P('seq', 'head'), may hold values from -6 to 6
- keys: bfloat16 [12288, 2048], P('seq', 'head'), may hold values from -6 to 6
- values: bfloat16 [12288, 2048], P('seq', 'head'), may hold values from -6 to 6
- cotangent: bfloat16 [12288, 2048], P('seq', 'head'), may hold values from -6 to 6
Outputs:
- layer_out: bfloat16 [12288, 2048], P('seq', 'head')
- d_queries: bfloat16 [12288, 2048], P('seq', 'head')
- d_keys: bfloat16 [12288, 2048], P('seq', 'head')
- d_values: bfloat16 [12288, 2048], P('seq', 'head')
- d_hidden: bfloat16 [12288, 2048], P('seq', 'head')
- d_weight: float32 [2048, 16], P('head')
- d_bias: float32 [16], P('head')
Inputs may be any that keep to these rules, and one draw needn't show every extreme that they name: `beta_bias`: at most ln(768) + 1.
All inputs are finite; a program needn't handle non-finite values.
Results may differ from a plain program's by a relative error of at most 0.006.
Values may be sent and summed in bfloat16 or wider, within the bound.
No kernel may reach another device: no remote copies, remote signals or barrier semaphores. Data moves between devices by JAX's collectives and lax.ppermute only.
A program may use at most 128 MiB of HBM per device.

v0:
```python
import math

import jax
import jax.numpy as jnp
from jax import lax
from jax.sharding import PartitionSpec as P

HIGHEST = lax.Precision.HIGHEST


def entering(part, axis, combine, identity, reverse):
    count = lax.axis_size(axis)
    place = lax.axis_index(axis)
    ahead = count - 1 - place if reverse else place
    gathered = jax.tree.map(lambda a: lax.all_gather(a, axis), part)
    state = jax.tree.map(lambda a, e: jnp.zeros_like(a) + jnp.asarray(e, a.dtype), part, identity)

    def one(turn, state):
        source = count - 1 - turn if reverse else turn
        return combine(
            state, jax.tree.map(lambda a: lax.dynamic_index_in_dim(a, source, 0, False), gathered)
        )

    return lax.fori_loop(0, ahead, one, state)


def normalize(vectors):
    return vectors / jnp.sqrt(jnp.sum(vectors * vectors, axis=-1, keepdims=True) + 1e-06)


def prepare(queries_f, keys_f, logits):
    return (normalize(queries_f), normalize(keys_f), 2.0 * jax.nn.sigmoid(logits))


def split_blocks(array, block_len):
    return array.reshape((array.shape[0] // block_len, block_len) + array.shape[1:])


def block_update(carried, keys_c, values_c, betas_c):
    length = keys_c.shape[0]
    inner_gram = jnp.einsum("chd,ehd->hce", keys_c, keys_c, precision=HIGHEST)
    strictly = jnp.tril(jnp.ones((length, length), jnp.float32), -1)
    weights = jnp.transpose(betas_c)
    system = jnp.eye(length, dtype=jnp.float32) + inner_gram * weights[:, None, :] * strictly
    misfit = jnp.swapaxes(values_c, 0, 1) - jnp.einsum(
        "chd,hrd->hcr", keys_c, carried, precision=HIGHEST
    )
    errors = jax.scipy.linalg.solve_triangular(system, misfit, lower=True, unit_diagonal=True)
    scaled = errors * weights[:, :, None]
    updated = carried + jnp.einsum("hcr,chd->hrd", scaled, keys_c, precision=HIGHEST)
    return (updated, scaled)


def transitions(keys_n, values_f, betas):
    tokens, head_count, head_size = keys_n.shape
    block_len = math.gcd(tokens, 128)
    start_state = jnp.concatenate(
        [
            jnp.broadcast_to(
                jnp.eye(head_size, dtype=jnp.float32), (head_count, head_size, head_size)
            ),
            jnp.zeros((head_count, values_f.shape[2], head_size), jnp.float32),
        ],
        axis=1,
    )
    padded_values = jnp.concatenate(
        [jnp.zeros((tokens, head_count, head_size), jnp.float32), values_f], axis=2
    )

    def transitions_advance(carried, pieces):
        updated, unused = block_update(carried, pieces[0], pieces[1], pieces[2])
        return (updated, None)

    final_state, unused = lax.scan(
        transitions_advance,
        start_state,
        (
            split_blocks(keys_n, block_len),
            split_blocks(padded_values, block_len),
            split_blocks(betas, block_len),
        ),
    )
    return (final_state[:, :head_size], final_state[:, head_size:])


def layer_states(start_state, queries_n, keys_n, values_f, betas):
    tokens, head_count, head_size = keys_n.shape
    block_len = math.gcd(tokens, 128)

    def layer_advance(carried, pieces):
        query_c, keys_c, values_c, betas_c = pieces
        updated, scaled = block_update(carried, keys_c, values_c, betas_c)
        causal = jnp.tril(jnp.ones((keys_c.shape[0], keys_c.shape[0]), jnp.float32))
        scores = jnp.einsum("chd,ehd->hce", query_c, keys_c, precision=HIGHEST) * causal
        outputs = jnp.einsum("chd,hrd->chr", query_c, carried, precision=HIGHEST) + jnp.einsum(
            "hce,her->chr", scores, scaled, precision=HIGHEST
        )
        return (updated, outputs)

    final_state, outputs = lax.scan(
        layer_advance,
        start_state,
        (
            split_blocks(queries_n, block_len),
            split_blocks(keys_n, block_len),
            split_blocks(values_f, block_len),
            split_blocks(betas, block_len),
        ),
    )
    raw_out = outputs.reshape(tokens, head_count, values_f.shape[2])
    normed = raw_out / jnp.sqrt(jnp.mean(raw_out * raw_out, axis=-1, keepdims=True) + 1e-05)
    return (normed, final_state)


def compose(earlier, later_pair):
    return (
        jnp.einsum("hij,hjk->hik", earlier[0], later_pair[0], precision=HIGHEST),
        jnp.einsum("hij,hjk->hik", earlier[1], later_pair[0], precision=HIGHEST) + later_pair[1],
    )


def unit_pairs(pair_set):
    return (
        jnp.broadcast_to(jnp.eye(pair_set[0].shape[1], dtype=jnp.float32), pair_set[0].shape),
        jnp.zeros_like(pair_set[1]),
    )


def process(queries_n, keys_n, values_f, betas, cotan_f, forward_scan, reverse_scan):
    moving, local_state = transitions(keys_n, values_f, betas)
    prefix = forward_scan((moving, local_state))
    (normed, final_state), pullback = jax.vjp(
        layer_states, prefix[1], queries_n, keys_n, values_f, betas
    )
    start_grad = pullback((cotan_f, jnp.zeros_like(final_state)))[0]
    suffix = reverse_scan((jnp.swapaxes(moving, 1, 2), start_grad))
    grads_n = pullback((cotan_f, suffix[1]))
    return (normed, grads_n[1], grads_n[2], grads_n[3], grads_n[4])


def per_device(hidden, beta_weight, beta_bias, queries, keys, values, cotangent):
    tokens = hidden.shape[0]
    head_count = beta_bias.shape[0]
    head_size = queries.shape[1] // head_count
    logit_part = lax.psum_scatter(
        lax.dot_general(
            beta_weight, hidden, (((0,), (1,)), ((), ())), preferred_element_type=jnp.float32
        ),
        "head",
        scatter_dimension=0,
        tiled=True,
    )
    logits = jnp.transpose(logit_part) + beta_bias[None, :]

    def shaped(array):
        return array.astype(jnp.float32).reshape(tokens, head_count, head_size)

    (queries_n, keys_n, betas), prep_pullback = jax.vjp(
        prepare, shaped(queries), shaped(keys), logits
    )
    values_f = shaped(values)
    cotan_f = shaped(cotangent)
    normed, dq_unit, dk_unit, grad_values, grad_betas = process(
        queries_n,
        keys_n,
        values_f,
        betas,
        cotan_f,
        lambda pair_set: entering(pair_set, "seq", compose, unit_pairs(pair_set), False),
        lambda pair_set: entering(pair_set, "seq", compose, unit_pairs(pair_set), True),
    )
    d_queries_f, d_keys_f, d_logits = prep_pullback((dq_unit, dk_unit, grad_betas))
    grad_rows = jnp.transpose(d_logits).astype(jnp.bfloat16)
    all_grads = lax.all_gather(grad_rows, "head", axis=0, tiled=True)
    d_hidden = lax.dot_general(
        all_grads, beta_weight, (((0,), (1,)), ((), ())), preferred_element_type=jnp.float32
    )
    weight_part = lax.dot_general(
        hidden, all_grads, (((0,), (1,)), ((), ())), preferred_element_type=jnp.float32
    )
    bias_part = jnp.sum(d_logits, axis=0)
    d_weight, d_bias = lax.psum((weight_part, bias_part), "seq")

    def flatten_out(array):
        return array.reshape(tokens, -1).astype(jnp.bfloat16)

    return (
        flatten_out(normed),
        flatten_out(d_queries_f),
        flatten_out(d_keys_f),
        flatten_out(grad_values),
        d_hidden.astype(jnp.bfloat16),
        d_weight,
        d_bias,
    )


def solution(mesh):
    return jax.shard_map(
        per_device,
        mesh=mesh,
        in_specs=(
            P("seq", "head"),
            P("head", None),
            P("head"),
            P("seq", "head"),
            P("seq", "head"),
            P("seq", "head"),
            P("seq", "head"),
        ),
        out_specs=(
            P("seq", "head"),
            P("seq", "head"),
            P("seq", "head"),
            P("seq", "head"),
            P("seq", "head"),
            P("head", None),
            P("head"),
        ),
        check_vma=False,
    )
```

profile of v0, /device:TPU:2, one launch (start us, length us, event | category | flops | bytes accessed | tf_op | source)
XLA Modules:
  0.0 1393.7 jit_solution(4284741213604059584)
XLA Ops:
  12.0 18.7 %all-reduce.2 = f32[16,128]{1,0:T(8,128)S(1)} all-reduce(f32[16,128]{1,0:T(8,128)S(1)} %fusion.67), channel_id=6, replica_groups=mesh['seq'=96,'head'=8] {'head'}, use_global_device_ids=true, to_apply=%region_1.0.clone | all-reduce | flops 2048 | bytes 16384
  33.4 19.7 %custom-call.12 = f32[2,1,128,128]{2,3,1,0:T(8,128)S(1)} custom-call(f32[2,1,128,128]{3,2,1,0:T(8,128)S(1)} %add_bitcast_fusion), custom_call_target="InvertDiagBlocksLowerTriangular" | custom-call | tf_op jit(solution)/shard_map/while/body/eval_jaxpr/jit(_solve_triangular)/vmap()/triangular_solve | solution.py:48
  58.2 151.2 %all-gather.10.cloned.1.call-done = f32[192,128,128]{2,1,0:T(8,128)} async-done(((f32[2,128,128]{2,1,0:T(8,128)}), f32[192,128,128]{2,1,0:T(8,128)}) %all-gather.10.cloned.1.call-update) | async-done | bytes 12582928 | tf_op jit(solution)/shard_map/all_gather | solution.py:15
  209.5 153.4 %all-gather.12.cloned.1.call-done = f32[192,128,128]{2,1,0:T(8,128)} async-done(((f32[2,128,128]{2,1,0:T(8,128)}), f32[192,128,128]{2,1,0:T(8,128)}) %all-gather.12.cloned.1.call-update) | async-done | bytes 12582928 | tf_op jit(solution)/shard_map/all_gather | solution.py:15
  369.6 146.9 %all-gather.14.cloned.1.call-done = f32[192,128,128]{2,1,0:T(8,128)} async-done(((f32[2,128,128]{2,1,0:T(8,128)}), f32[192,128,128]{2,1,0:T(8,128)}) %all-gather.14.cloned.1.call-update) | async-done | bytes 12582928 | tf_op jit(solution)/shard_map/all_gather | solution.py:15
  516.4 220.6 %all-gather.16.cloned.1.call-done = f32[192,128,128]{2,1,0:T(8,128)} async-done(((f32[2,128,128]{2,1,0:T(8,128)}), f32[192,128,128]{2,1,0:T(8,128)}) %all-gather.16.cloned.1.call-update) | async-done | bytes 12582928 | tf_op jit(solution)/shard_map/all_gather | solution.py:15
  737.0 225.5 %while.17 = (s32[]{:T(128)}, f32[2,128,128]{1,2,0:T(8,128)S(1)}, s32[]{:T(128)}, f32[96,2,128,128]{3,2,1,0:T(8,128)}, f32[96,2,128,128]{3,2,1,0:T(8,128)}, /*index=5*/s32[]{:T(128)}, s32[]{:T(128)}, s32[]{:T(128)}, s32[]{:T(128)}) while((s32[]{:T(128)}, f32[2,128,128]{1,2,0:T(8,128)S(1)}, s32[]{:T(128)}, f32[96,2,128,128]{3,2,1,0:T(8,128)}, ...), condition=%wide.region_9.11_spmd, body=%wide.region_8.10_spmd.sunk | while | flops 50364420 | bytes 1310875 | solution.py:24
  742.9 1.3 fusion.109
  745.2 1.3 fusion.109
  747.6 1.3 fusion.109
  750.0 1.3 fusion.109
  759.5 1.3 fusion.109
  761.9 1.3 fusion.109
  764.2 1.3 fusion.109
  766.6 1.3 fusion.109
  773.7 1.3 fusion.109
  776.1 1.3 fusion.109
  778.5 1.3 fusion.109
  780.8 1.3 fusion.109
  783.2 1.3 fusion.109
  790.3 1.3 fusion.109
  792.7 1.3 fusion.109
  795.1 1.3 fusion.109
  797.5 1.3 fusion.109
  799.8 1.3 fusion.109
  807.0 1.3 fusion.109
  809.3 1.3 fusion.109
  811.7 1.3 fusion.109
  814.1 1.3 fusion.109
  816.4 1.3 fusion.109
  823.6 1.3 fusion.109
  825.9 1.3 fusion.109
  828.3 1.3 fusion.109
  830.7 1.3 fusion.109
  833.1 1.3 fusion.109
  840.2 1.3 fusion.109
  842.6 1.3 fusion.109
  844.9 1.3 fusion.109
  847.3 1.3 fusion.109
  849.7 1.3 fusion.109
  856.8 1.3 fusion.109
  859.2 1.3 fusion.109
  861.5 1.3 fusion.109
  863.9 1.3 fusion.109
  866.3 1.3 fusion.109
  873.4 1.3 fusion.109
  875.8 1.3 fusion.109
  878.2 1.3 fusion.109
  880.5 1.3 fusion.109
  882.9 1.3 fusion.109
  890.0 1.3 fusion.109
  892.4 1.3 fusion.109
  894.8 1.3 fusion.109
  897.1 1.3 fusion.109
  899.5 1.3 fusion.109
  906.6 1.3 fusion.109
  909.0 1.3 fusion.109
  911.4 1.3 fusion.109
  913.8 1.3 fusion.109
  916.1 1.3 fusion.109
  923.3 1.3 fusion.109
  925.6 1.3 fusion.109
  965.0 8.6 all-gather.4
  976.9 410.2 %all-reduce.3 = (f32[256,16]{0,1:T(8,128)}, f32[2]{0:T(128)}) all-reduce(f32[256,16]{0,1:T(8,128)S(1)} %convolution_bitcast_fusion.7, f32[2]{0:T(128)S(1)} %fusion.53), channel_id=1, replica_groups=mesh['seq'=96,'head'=8] {'seq'}, use_global_device_ids=true, to_apply=%region_13.15 | all-reduce | flops 4098 | bytes 32784 | tf_op jit(solution)/shard_map/psum | solution.py:182
  (403 shorter events, 173.2 us)
Async XLA Ops:
  7.2 4.0 copy-start
  7.2 202.3 %all-gather.10.cloned.1.call-start = ((), (), s32[]{:S(2)}) async-start(), calls=%async_computation | async-start | bytes 12713984 | tf_op jit(solution)/shard_map/all_gather | solution.py:15
  55.1 307.8 %all-gather.12.cloned.1.call-start = ((), (), s32[]{:S(2)}) async-start(), calls=%async_computation.1 | async-start | bytes 12713984 | tf_op jit(solution)/shard_map/all_gather | solution.py:15
  55.9 460.6 %all-gather.14.cloned.1.call-start = ((), (), s32[]{:S(2)}) async-start(), calls=%async_computation.2 | async-start | bytes 12713984 | tf_op jit(solution)/shard_map/all_gather | solution.py:15
  56.7 680.4 %all-gather.16.cloned.1.call-start = ((), (), s32[]{:S(2)}) async-start(), calls=%async_computation.3 | async-start | bytes 12713984 | tf_op jit(solution)/shard_map/all_gather | solution.py:15
  57.8 915.8 %copy-start.1 = (bf16[256,16]{0,1:T(8,128)(2,1)S(1)}, bf16[256,16]{0,1:T(8,128)(2,1)}, u32[]{:S(2)}) copy-start(bf16[256,16]{0,1:T(8,128)(2,1)} %param.14) | copy-start | bytes 24580
Sparse Core Ops, SparseCore 0:
  55.2 154.1 all-gather.9
  213.2 149.6 all-gather.11
  366.6 149.7 all-gather.13
  520.0 216.9 all-gather.15
where the time goes:
time: 1400 us; the launch traced here: 1390 us
  waiting for transfers between devices  673 us (48%)
  blocking collectives  438 us (31%)
  matrix products  135 us (10%)
  local copies, waits for them, and re-layouts  107 us (8%)
  other arithmetic  21.3 us (2%)
  between operations  14.8 us (1%)
    all_gather x4, waiting for transfers between devices, entering(): gathered = jax.tree.map(lambda a: lax.all_gather(a, axis), part)  672 us
    psum x1, blocking collectives, per_device(): d_weight, d_bias = lax.psum((weight_part, bias_part), 'seq')  410 us
    dot_general x95, matrix products, compose(): jnp.einsum('hij,hjk->hik', earlier[1], later_pair[0], precision=HIGHEST)  123 us
    dynamic_slice x190, local copies, waits for them, and re-layouts, one(): lax.dynamic_index_in_dim(a, source, 0, False)  96.2 us
  transfers between devices with their start and end apart: 4, of which 4 were waited for; matrix products, arithmetic and copies ran while one was open for 1% of the time, Pallas kernels for 0%

commit v1 on v0

v1 whole, which is shorter than its diff:
```python
import functools

import jax
import jax.numpy as jnp
from jax import lax
from jax.experimental import pallas as pl
from jax.experimental.pallas import tpu as pltpu
from jax.sharding import Mesh, PartitionSpec as P

F32 = jnp.float32
BF16 = jnp.bfloat16
L = 128
D = 128
NN = (((1,), (0,)), ((), ()))
NT = (((1,), (1,)), ((), ()))
TN = (((0,), (0,)), ((), ()))


def dot1(a, b, dims=NN):
    return lax.dot_general(a, b, dims, preferred_element_type=F32)


def split(x):
    hi = x.astype(BF16)
    return hi, (x - hi.astype(F32)).astype(BF16)


def dot2(a, b, dims=NN):
    hi, lo = split(a)
    return dot1(hi, b, dims) + dot1(lo, b, dims)


def dot2r(a, b, dims=NN):
    hi, lo = split(b)
    return dot1(a, hi, dims) + dot1(a, lo, dims)


def dot3(a, b, dims=NN):
    ah, al = split(a)
    bh, bl = split(b)
    return dot1(ah, bh, dims) + (dot1(al, bh, dims) + dot1(ah, bl, dims))


def index_grids():
    row = lax.broadcasted_iota(jnp.int32, (L, L), 0)
    col = lax.broadcasted_iota(jnp.int32, (L, L), 1)
    return row, col


def to_col(row_vec, row, col):
    return jnp.sum(jnp.where(row == col, row_vec, 0.0), axis=1, keepdims=True)


def to_row(col_vec, row, col):
    return jnp.sum(jnp.where(row == col, col_vec, 0.0), axis=0, keepdims=True)


def inv_norm(raw):
    f = raw.astype(F32)
    return lax.rsqrt(jnp.sum(f * f, axis=1, keepdims=True) + 1e-06)


def triangle_inverse(strict, row, col):
    eye = jnp.where(row == col, 1.0, 0.0)
    diff = row ^ col
    inv = eye - jnp.where(diff == 1, strict, 0.0)
    size = 2
    while size < L:
        below = jnp.where((diff >= size) & (diff < 2 * size), strict, 0.0)
        inv = inv - dot3(inv, dot3(below, inv))
        size *= 2
    return inv


def block_prepare(kr, vr, logit_row):
    row, col = index_grids()
    beta_row = 2.0 * jax.nn.sigmoid(logit_row)
    beta = to_col(beta_row, row, col)
    rk = inv_norm(kr)
    rk_row = to_row(rk, row, col)
    gram = dot1(kr, kr, NT) * rk * rk_row
    strict = jnp.where(row > col, gram * beta_row, 0.0)
    inv = triangle_inverse(strict, row, col)
    solved_k = dot2(inv * rk_row, kr)
    solved_v = dot2(inv, vr)
    scale = beta * rk
    less = dot2(solved_k * scale, kr, TN)
    gain = dot2(solved_v * scale, kr, TN)
    back_k = dot3(inv, beta * (kr.astype(F32) * rk), TN)
    return less, gain, inv, solved_k, solved_v, back_k, gram


def block_outputs(qr, kr, ct, logit_row, start, inv, solved_k, solved_v):
    row, col = index_grids()
    beta = to_col(2.0 * jax.nn.sigmoid(logit_row), row, col)
    rk, rq = inv_norm(kr), inv_norm(qr)
    rk_row = to_row(rk, row, col)
    attend = jnp.where(row >= col, dot1(qr, kr, NT) * rq * rk_row, 0.0)
    errors = solved_v - dot3(solved_k, start, NT)
    scaled = beta * errors
    raw = rq * dot2r(qr, start, NT) + dot3(attend, scaled)
    rn = lax.rsqrt(jnp.mean(raw * raw, axis=1, keepdims=True) + 1e-05)
    normed = raw * rn
    cotan = ct.astype(F32)
    d_raw = rn * (cotan - normed * jnp.mean(normed * cotan, axis=1, keepdims=True))
    back0 = dot3(inv, beta * dot3(attend, d_raw, TN), TN)
    give = dot2(d_raw * rq, qr, TN) - dot2(back0 * rk, kr, TN)
    return normed, errors, d_raw, back0, give


def block_grads_early(qr, kr, logit_row, start, errors, d_raw):
    row, col = index_grids()
    beta = to_col(2.0 * jax.nn.sigmoid(logit_row), row, col)
    rk, rq = inv_norm(kr), inv_norm(qr)
    rk_row = to_row(rk, row, col)
    scaled = beta * errors
    d_attend = jnp.where(row >= col, dot3(d_raw, scaled, NT), 0.0)
    dq_unit = dot3(d_raw, start) + dot2(d_attend * rk_row, kr)
    dk_part = dot2(d_attend * rq, qr, TN)
    q_unit = qr.astype(F32) * rq
    dq = rq * (dq_unit - q_unit * jnp.sum(q_unit * dq_unit, axis=1, keepdims=True))
    return dq, dk_part


def block_grads(kr, logit_row, start, end_grad, errors, back0, back_k, dk_part):
    row, col = index_grids()
    beta = to_col(2.0 * jax.nn.sigmoid(logit_row), row, col)
    keep = to_col(jax.nn.sigmoid(-logit_row), row, col)
    rk = inv_norm(kr)
    rk_row = to_row(rk, row, col)
    scaled = beta * errors
    back = back0 + dot3(back_k, end_grad, NT)
    d_logit = to_row(jnp.sum(errors * back, axis=1, keepdims=True) * keep, row, col)
    d_gram = jnp.where(row > col, -dot3(back, scaled, NT), 0.0)
    d_gram = d_gram + jnp.where(row < col, -dot3(scaled, back, NT), 0.0)
    dk_unit = dk_part - dot3(back, start) + dot3(scaled, end_grad) + dot2(d_gram * rk_row, kr)
    k_unit = kr.astype(F32) * rk
    dk = rk * (dk_unit - k_unit * jnp.sum(k_unit * dk_unit, axis=1, keepdims=True))
    return dk, back, d_logit


def level_of(x):
    top = jnp.max(jnp.max(jnp.abs(x), axis=1, keepdims=True), axis=0, keepdims=True)
    return jnp.ceil(jnp.log2(jnp.maximum(top, 1e-30)))


def packed(x):
    level = level_of(x)
    return x * jnp.exp2(-level), jnp.broadcast_to(level, (16, D))


def scaled_back(x, level):
    return x * jnp.exp2(level[0:1])


def step(state, less, dims=NN):
    return state - dot3(state, less, dims)


def chain_forward(less, gain, place, count):
    eye = jnp.where(index_grids()[0] == index_grids()[1], 1.0, 0.0)
    zero = jnp.zeros((D, D), F32)
    state = jnp.concatenate([eye, zero], axis=0)
    own = state
    for j in range(count):
        own = jnp.where(place == j, state, own)
        if j == 0:
            state = jnp.concatenate([eye - less(j), gain(j)], axis=0)
        else:
            state = step(state, less(j)) + jnp.concatenate([zero, gain(j)], axis=0)
    return state, own


def chain_state(less, gain, place, count):
    state = jnp.zeros((D, D), F32)
    own = state
    for j in range(count - 1):
        state = gain(j) if j == 0 else step(state, less(j)) + gain(j)
        own = jnp.where(place == j + 1, state, own)
    return own


def chain_back_matrix(less, place, count):
    state = jnp.where(index_grids()[0] == index_grids()[1], 1.0, 0.0)
    own = state
    for j in range(count - 1, 0, -1):
        state = step(state, less(j), NT)
        own = jnp.where(place == j - 1, state, own)
    return own


def chain_back(less, give, place, count, total=True):
    state = jnp.zeros((D, D), F32)
    own = state
    for j in range(count - 1, -1 if total else 0, -1):
        own = jnp.where(place == j, state, own)
        state = give(j) if j == count - 1 else step(state, less(j), NT) + give(j)
    if not total:
        own = jnp.where(place == 0, state, own)
    return state, own


def put(send, less, gain):
    send[0:D] = less
    send[D : 2 * D], send[2 * D : 2 * D + 16] = packed(gain)


def less_of(got):
    return lambda j: got[j, 0:D]


def gain_of(got):
    return lambda j: scaled_back(got[j, D : 2 * D], got[j, 2 * D : 2 * D + 8])


def give_of(got):
    return lambda j: scaled_back(got[j, 0:D], got[j, D : D + 8])


def kernel_prepare(lg, kv, send, less, gain, inv, sk, sv, bk):
    moves = []
    for b in range(2):
        w, n, *rest, _ = block_prepare(kv[b, 0], kv[b, 1], lg[b : b + 1, :])
        less[b], gain[b] = w, n
        inv[b], sk[b], sv[b], bk[b] = rest
        moves.append((w, n))
    (w0, n0), (w1, n1) = moves
    both = step(jnp.concatenate([w0, n0], axis=0), w1)
    put(send, both[:D] + w1, both[D:] + n1)


def kernel_row_forward(count, place, got, send, own):
    state, before = chain_forward(less_of(got), gain_of(got), place[0], count)
    row, col = index_grids()
    put(send, jnp.where(row == col, 1.0, 0.0) - state[:D], state[D:])
    own[...] = before


def kernel_row_matrix(count, place, got, own):
    own[...] = chain_back_matrix(less_of(got), place[0], count)


def kernel_outputs(count, place, got, own, lg, kv, qc, less, gain, inv, sk, sv,
                   out, start, err, draw, back0, give, send):
    first = chain_state(less_of(got), gain_of(got), place[0], count)
    before = dot3(first, own[:D]) + own[D:]
    gives = []
    for b in range(2):
        if b == 1:
            before = step(before, less[0]) + gain[0]
        normed, e, dr, b0, g = block_outputs(
            qc[b, 0], kv[b, 0], qc[b, 1], lg[b : b + 1, :], before, inv[b], sk[b], sv[b]
        )
        out[b] = normed.astype(BF16)
        start[b], err[b], draw[b], back0[b] = before, e, dr, b0
        gives.append(g)
    give[...] = gives[1]
    send[0:D], send[D : D + 16] = packed(step(gives[1], less[0], NT) + gives[0])


def kernel_early(lg, kv, qc, start, err, draw, dq, dkp):
    for b in range(2):
        x, y = block_grads_early(
            qc[b, 0], kv[b, 0], lg[b : b + 1, :], start[b], err[b], draw[b]
        )
        dq[b] = x.astype(BF16)
        dkp[b] = y


def kernel_row_back(count, place, got, gives, send, own):
    state, after = chain_back(less_of(got), give_of(gives), place[0], count)
    send[0:D], send[D : D + 16] = packed(state)
    own[...] = after


def kernel_grads(count, place, got, gives, matrix, own, lg, kv, less, give, start, err,
                 back0, bk, dkp, dkv, dlog):
    _, row_after = chain_back(less_of(got), give_of(gives), place[0], count, total=False)
    end_grad = dot3(row_after, matrix[...]) + own[...]
    for b in (1, 0):
        if b == 0:
            end_grad = step(end_grad, less[1], NT) + give[...]
        x, y, z = block_grads(
            kv[b, 0], lg[b : b + 1, :], start[b], end_grad, err[b], back0[b], bk[b], dkp[b]
        )
        dkv[b, 0], dkv[b, 1] = x.astype(BF16), y.astype(BF16)
        dlog[b : b + 1, :] = z


VM = pl.BlockSpec(memory_space=pltpu.VMEM)
SM = pl.BlockSpec(memory_space=pltpu.SMEM)


def call(body, outs, *args, flops=1e8):
    specs = [SM if a.dtype == jnp.int32 else VM for a in args]
    total = sum(a.size * a.dtype.itemsize for a in args)
    return pl.pallas_call(
        body,
        out_shape=[jax.ShapeDtypeStruct(s, t) for s, t in outs],
        in_specs=specs,
        out_specs=[VM] * len(outs),
        compiler_params=pltpu.CompilerParams(vmem_limit_bytes=40 * 2**20),
        cost_estimate=pl.CostEstimate(flops=int(flops), bytes_accessed=total, transcendentals=0),
    )(*args)


def copies(x, axis):
    count = lax.axis_size(axis)
    return lax.all_to_all(jnp.broadcast_to(x[None], (count,) + x.shape), axis, 0, 0)


def spread(x, axis):
    return copies(x.astype(jnp.float16), axis).astype(F32)


def to_heads(*arrays):
    parts = jnp.stack([a.reshape(L, 2, D).transpose(1, 0, 2) for a in arrays], axis=1)
    return lax.all_to_all(parts, "zl", 0, 0)


def to_blocks(parts):
    heads = lax.all_to_all(parts, "zl", 0, 0)
    return [heads[:, i].transpose(1, 0, 2).reshape(L, 2 * D) for i in range(heads.shape[1])]


HALF = ((D, D), F32)
PAIR = ((2, D, D), F32)
ALL = ("zl", "head")


def per_device(hidden, beta_weight, beta_bias, queries, keys, values, cotangent):
    rows, pairs = lax.axis_size("y"), lax.axis_size("zh")
    side = lax.axis_index("zl")
    at_y = lax.axis_index("y").astype(jnp.int32).reshape(1)
    at_z = lax.axis_index("zh").astype(jnp.int32).reshape(1)

    part = lax.dot_general(
        beta_weight, hidden, (((0,), (1,)), ((), ())), preferred_element_type=F32
    )
    part = part.reshape(8, 2, L).transpose(1, 0, 2).reshape(16, L)
    part = lax.all_to_all(part, ALL, 0, 0, tiled=True)
    bias = jnp.where(side == 0, beta_bias[0], beta_bias[1])
    logits = jnp.sum(part.reshape(2, 8, L), axis=1) + bias
    kv = to_heads(keys, values)
    qc = to_heads(queries, cotangent)

    send1, less, gain, inv, sk, sv, bk = call(
        kernel_prepare, [((2 * D + 16, D), F32)] + [PAIR] * 6, logits, kv
    )
    got1 = spread(send1, "zh")
    send2, own1 = call(
        functools.partial(kernel_row_forward, pairs),
        [((2 * D + 16, D), F32), ((2 * D, D), F32)], at_z, got1,
    )
    got2 = spread(send2, "y")
    (matrix,) = call(functools.partial(kernel_row_matrix, pairs), [HALF], at_z, got1)
    out, start, err, draw, back0, give, send3 = call(
        functools.partial(kernel_outputs, rows),
        [((2, L, D), BF16)] + [PAIR] * 4 + [HALF, ((D + 16, D), F32)],
        at_y, got2, own1, logits, kv, qc, less, gain, inv, sk, sv,
    )
    got3 = spread(send3, "zh")
    dq, dkp = call(
        kernel_early, [((2, L, D), BF16), PAIR], logits, kv, qc, start, err, draw
    )
    send4, own2 = call(
        functools.partial(kernel_row_back, pairs), [((D + 16, D), F32), HALF], at_z, got1, got3
    )
    got4 = spread(send4, "y")
    out, dq = to_blocks(jnp.stack([out, dq], axis=1))
    dkv, d_logits = call(
        functools.partial(kernel_grads, rows), [((2, 2, L, D), BF16), ((2, L), F32)],
        at_y, got2, got4, matrix, own2, logits, kv, less, give, start, err, back0, bk, dkp,
    )

    grads = jnp.repeat(d_logits.astype(BF16), 8, axis=0)
    grads = lax.all_to_all(grads, ALL, 0, 0, tiled=True)
    grads, dkv = lax.optimization_barrier((grads, dkv))
    all_grads = grads.reshape(2, 8, L).transpose(1, 0, 2).reshape(16, L)
    weight_part = lax.dot_general(
        all_grads, hidden, (((1,), (0,)), ((), ())), preferred_element_type=F32
    )
    bias_part = jnp.sum(d_logits)
    slot = lax.broadcasted_iota(jnp.int32, (8, 2 * D), 0) * (2 * D) + lax.broadcasted_iota(
        jnp.int32, (8, 2 * D), 1
    )
    total = jnp.concatenate([weight_part, jnp.where(slot == side, bias_part, 0.0)], axis=0)
    total = jnp.sum(copies(total, ("zh", "zl")), axis=0)
    total = jnp.sum(copies(total, "y"), axis=0)
    dk, dv = to_blocks(dkv)
    d_hidden = lax.dot_general(
        all_grads, beta_weight, (((0,), (1,)), ((), ())), preferred_element_type=F32
    )
    return (out, dq, dk, dv, d_hidden.astype(BF16), total[:16].T, total[16, 0:2])


def solution(mesh):
    grid = Mesh(mesh.devices.reshape(8, 6, 2, 8), ("y", "zh", "zl", "head"))
    seq = P(("y", "zh", "zl"), "head")
    return jax.shard_map(
        per_device,
        mesh=grid,
        in_specs=(seq, P("head", None), P("head"), seq, seq, seq, seq),
        out_specs=(seq, seq, seq, seq, seq, P("head", None), P("head")),
        check_vma=False,
    )
```

time: 1400 us -> 204 us (0.15)
  waiting for transfers between devices: 673 us -> 66.8 us
  blocking collectives: 438 us -> 40.6 us
  matrix products: 135 us -> 1.78 us
  local copies, waits for them, and re-layouts: 107 us -> 15.4 us
  starting transfers between devices: 0.16 us -> 54.7 us
  other arithmetic: 21.3 us -> 5.01 us
  Pallas kernels: 0 us -> 16 us
    all_gather x4 -> x0, waiting for transfers between devices: 672 us -> none  [entering(): gathered = jax.tree.map(lambda a: lax.all_gather(a, axis), part)]
    psum x1 -> x0, blocking collectives: 410 us -> none  [per_device(): d_weight, d_bias = lax.psum((weight_part, bias_part), 'seq')]
    dot_general x117 -> x1, matrix products: 132 us -> 0.13 us  [per_device(): lax.dot_general(all_grads, hidden, (((1,), (0,)), ((), ())), preferred_el...]
    dynamic_slice x190 -> x0, local copies, waits for them, and re-layouts: 96.2 us -> none  [one(): lax.dynamic_index_in_dim(a, source, 0, False)]
    all_to_all x0 -> x10, waiting for transfers between devices: none -> 66.8 us  [the longest x4 48.2 us: copies(): lax.all_to_all(jnp.broadcast_to(x[None], (count,) + x.shape), axis, 0, 0)]
    all_to_all x0 -> x10, starting transfers between devices: none -> 54.7 us  [the longest x4 22.7 us: copies(): lax.all_to_all(jnp.broadcast_to(x[None], (count,) + x.shape), axis, 0, 0)]
    all_to_all x0 -> x2, blocking collectives: none -> 40.6 us  [copies(): lax.all_to_all(jnp.broadcast_to(x[None], (count,) + x.shape), axis, 0, 0)]
    unnamed x1 -> x0, blocking collectives: 18.7 us -> none
  transfers between devices with their start and end apart: 4 -> 10, of which waited for: 4 -> 9; matrix products, arithmetic and copies ran while one was open for 1% -> 6% of each run, Pallas kernels for 0% -> 1%
where the time goes in v1:
time: 204 us; the launch traced here: 203 us
  waiting for transfers between devices  66.8 us (33%)
  starting transfers between devices  54.7 us (27%)
  blocking collectives  40.6 us (20%)
  Pallas kernels  16 us (8%)
  local copies, waits for them, and re-layouts  15.4 us (8%)
  other arithmetic  5.01 us (2%)
  between operations  2.39 us (1%)
    all_to_all x4, waiting for transfers between devices, copies(): lax.all_to_all(jnp.broadcast_to(x[None], (count,) + x.shape), axis, 0, 0)  48.2 us
    all_to_all x2, blocking collectives, copies(): lax.all_to_all(jnp.broadcast_to(x[None], (count,) + x.shape), axis, 0, 0)  40.6 us
    all_to_all x4, starting transfers between devices, copies(): lax.all_to_all(jnp.broadcast_to(x[None], (count,) + x.shape), axis, 0, 0)  22.7 us
    pallas_call x7, Pallas kernels, call(): pl.pallas_call(body, out_shape=[jax.ShapeDtypeStruct(s, t) for s, t in ou...  16 us
    all_to_all x1, starting transfers between devices, per_device(): part = lax.all_to_all(part, ALL, 0, 0, tiled=True)  12.8 us
    all_to_all x2, waiting for transfers between devices, to_heads(): return lax.all_to_all(parts, 'zl', 0, 0)  7.74 us
    unnamed x37, local copies, waits for them, and re-layouts  7.15 us
    all_to_all x2, waiting for transfers between devices, to_blocks(): heads = lax.all_to_all(parts, 'zl', 0, 0)  6.97 us
  transfers between devices with their start and end apart: 10, of which 9 were waited for; matrix products, arithmetic and copies ran while one was open for 6% of the time, Pallas kernels for 1%

profile of v1, /device:TPU:2, one launch (start us, length us, event | category | flops | bytes accessed | tf_op | source)
XLA Modules:
  0.0 202.7 jit_solution(9554521686813426057)
XLA Ops:
  0.6 0.8 copy-done
  1.5 0.8 fusion.4
  2.3 0.6 copy.90
  2.9 12.8 %all-to-all-start = ((f32[16,1,128]{2,1,0:T(1,128)}), f32[16,1,128]{2,1,0:T(1,128)S(1)}, u32[]{:S(2)}, u32[]{:S(2)}) async-start(f32[16,1,128]{2,1,0:T(1,128)} %bitcast.5), calls=%async_computation | async-start | bytes 16384 | tf_op jit(solution)/shard_map/all_to_all | solution.py:341
  15.7 0.9 copy.92
  16.7 0.1 copy.93
  16.8 1.0 copy.94
  17.8 0.1 copy.95
  17.9 0.7 pad_maximum_fusion
  18.6 1.3 fusion.3
  21.2 3.4 %all-to-all-start.1 = ((bf16[2,2,128,128]{3,2,1,0:T(8,128)(2,1)}), bf16[2,2,128,128]{3,2,1,0:T(8,128)(2,1)S(1)}, u32[]{:S(2)}, u32[]{:S(2)}) async-start(bf16[2,2,128,128]{3,2,1,0:T(8,128)(2,1)} %pad_maximum_fusion), calls=%async_computation.1 | async-start | bytes 262144 | tf_op jit(solution)/shard_map/all_to_all | solution.py:318
  24.6 4.4 %all-to-all-done.1.kv = bf16[2,2,128,128]{3,2,1,0:T(8,128)(2,1)S(1)} async-done(((bf16[2,2,128,128]{3,2,1,0:T(8,128)(2,1)}), bf16[2,2,128,128]{3,2,1,0:T(8,128)(2,1)S(1)}, u32[]{:S(2)}, u32[]{:S(2)}) %all-to-all-start.1) | async-done | bytes 131104 | tf_op jit(solution)/shard_map/all_to_all | solution.py:318
  29.1 5.4 %shard_map.126 = (f32[272,128]{1,0:T(8,128)S(1)}, f32[2,128,128]{2,1,0:T(8,128)S(1)}, f32[2,128,128]{2,1,0:T(8,128)S(1)}, f32[2,128,128]{2,1,0:T(8,128)S(1)}, f3...) custom-call(f32[2,128]{1,0:T(2,128)S(1)} %broadcast_add_fusion.lg, ...), custom_call_target="tpu_custom_call" | custom-call | flops 100000000 | bytes 132096 | tf_op jit(solution)/shard_map/pallas_call | solution.py:297
  34.5 0.8 broadcast_in_dim.22
  35.4 8.1 %all-to-all-start.2 = ((f16[6,272,128]{2,1,0:T(8,128)(2,1)}), f16[6,272,128]{2,1,0:T(8,128)(2,1)S(1)}, u32[]{:S(2)}, u32[]{:S(2)}) async-start(f16[6,272,128]{2,1,0:T(8,128)(2,1)} %broadcast_in_dim.22), calls=%async_computation.2 | async-start | bytes 835584 | tf_op jit(solution)/shard_map/all_to_all | solution.py:309
  43.4 18.2 %all-to-all-done.2 = f16[6,272,128]{2,1,0:T(8,128)(2,1)S(1)} async-done(((f16[6,272,128]{2,1,0:T(8,128)(2,1)}), f16[6,272,128]{2,1,0:T(8,128)(2,1)S(1)}, u32[]{:S(2)}, u32[]{:S(2)}) %all-to-all-start.2) | async-done | bytes 417824 | tf_op jit(solution)/shard_map/all_to_all | solution.py:309
  61.7 1.1 shard_map.127
  62.8 0.9 broadcast_in_dim.23
  63.7 7.1 %all-to-all-start.3 = ((f16[8,272,128]{2,1,0:T(8,128)(2,1)}), f16[8,272,128]{2,1,0:T(8,128)(2,1)S(1)}, u32[]{:S(2)}, u32[]{:S(2)}) async-start(f16[8,272,128]{2,1,0:T(8,128)(2,1)} %broadcast_in_dim.23), calls=%async_computation.3 | async-start | bytes 1114112 | tf_op jit(solution)/shard_map/all_to_all | solution.py:309
  70.8 0.1 copy.96
  70.9 0.1 copy.97
  71.2 0.1 copy.99
  71.3 0.7 pad_maximum_fusion.1
  72.0 14.5 %all-to-all-done.3 = f16[8,272,128]{2,1,0:T(8,128)(2,1)S(1)} async-done(((f16[8,272,128]{2,1,0:T(8,128)(2,1)}), f16[8,272,128]{2,1,0:T(8,128)(2,1)S(1)}, u32[]{:S(2)}, u32[]{:S(2)}) %all-to-all-start.3) | async-done | bytes 557088 | tf_op jit(solution)/shard_map/all_to_all | solution.py:309
  86.5 3.4 %all-to-all-start.4 = ((bf16[2,2,128,128]{3,2,1,0:T(8,128)(2,1)}), bf16[2,2,128,128]{3,2,1,0:T(8,128)(2,1)S(1)}, u32[]{:S(2)}, u32[]{:S(2)}) async-start(bf16[2,2,128,128]{3,2,1,0:T(8,128)(2,1)} %pad_maximum_fusion.1), calls=%async_computation.4 | async-start | bytes 262144 | tf_op jit(solution)/shard_map/all_to_all | solution.py:318
  89.9 1.1 convert_element_type.33.got
  91.0 3.3 %all-to-all-done.4.qc = bf16[2,2,128,128]{3,2,1,0:T(8,128)(2,1)S(1)} async-done(((bf16[2,2,128,128]{3,2,1,0:T(8,128)(2,1)}), bf16[2,2,128,128]{3,2,1,0:T(8,128)(2,1)S(1)}, u32[]{:S(2)}, u32[]{:S(2)}) %all-to-all-start.4) | async-done | bytes 131104 | tf_op jit(solution)/shard_map/all_to_all | solution.py:318
  94.3 0.9 copy-done.2
  95.2 3.5 %shard_map.128 = (bf16[2,128,128]{2,1,0:T(8,128)(2,1)S(1)}, f32[2,128,128]{2,1,0:T(8,128)S(1)}, f32[2,128,128]{2,1,0:T(8,128)S(1)}, f32[2,128,128]{2,1,0:T(8,128...) custom-call(s32[1]{0:T(128)} %bitcast.place, ...), custom_call_target="tpu_custom_call" | custom-call | flops 100000000 | bytes 2163716 | tf_op jit(solution)/shard_map/pallas_call | solution.py:297
  98.8 20.9 %all_to_all.71 = f16[6,144,128]{2,1,0:T(8,128)(2,1)S(1)} all-to-all(f16[6,144,128]{2,1,0:T(8,128)(2,1)S(1)} %broadcast_in_dim.24), channel_id=1, replica_groups=mesh['y'=8,'zh'=6,'zl'=2,'head'=8] {'zh'}, dimensions={0} | all-to-all | bytes 442368 | tf_op jit(solution)/shard_map/all_to_all | solution.py:309
  119.7 1.1 shard_map.130
  120.8 0.7 broadcast_in_dim.25
  121.6 4.2 %all-to-all-start.7 = ((f16[8,144,128]{2,1,0:T(8,128)(2,1)}), f16[8,144,128]{2,1,0:T(8,128)(2,1)}, u32[]{:S(2)}, u32[]{:S(2)}) async-start(f16[8,144,128]{2,1,0:T(8,128)(2,1)} %broadcast_in_dim.25), calls=%async_computation.7 | async-start | bytes 589824 | tf_op jit(solution)/shard_map/all_to_all | solution.py:309
  125.8 1.0 shard_map.131.matrix
  126.8 0.7 shard_map.129
  127.5 0.7 copy.100
  128.2 8.4 %all-to-all-done.7 = f16[8,144,128]{2,1,0:T(8,128)(2,1)} async-done(((f16[8,144,128]{2,1,0:T(8,128)(2,1)}), f16[8,144,128]{2,1,0:T(8,128)(2,1)}, u32[]{:S(2)}, u32[]{:S(2)}) %all-to-all-start.7) | async-done | bytes 294944 | tf_op jit(solution)/shard_map/all_to_all | solution.py:309
  136.6 1.0 convert_element_type.37.gives
  137.6 3.3 %shard_map.132 = (bf16[2,2,128,128]{3,2,1,0:T(8,128)(2,1)}, f32[2,128]{1,0:T(2,128)S(1)}) custom-call(s32[1]{0:T(128)} %bitcast.place, f32[8,272,128]{2,1,0:T(8,128)S(1)} %convert_element_type.33.got, f32[8,144,128]{2,1,0:T(8,128)S(1)} %convert_element_type.37.gives, f32[128,128]{1,0:T(8,128)S(1)} %shard_map.131.matrix, ...), custom_call_target="tpu_custom_call" | custom-call | flops 100000000 | bytes 2819076 | tf_op jit(solution)/shard_map/pallas_call | solution.py:297
  140.9 0.6 fusion.2
  141.5 0.6 copy.103
  142.1 5.5 %all-to-all-start.8 = ((bf16[16,1,128]{2,1,0:T(2,128)(2,1)}), bf16[16,1,128]{2,1,0:T(2,128)(2,1)S(1)}, u32[]{:S(2)}, u32[]{:S(2)}) async-start(bf16[16,1,128]{2,1,0:T(2,128)(2,1)} %copy.103), calls=%async_computation.8 | async-start | bytes 16384 | tf_op jit(solution)/shard_map/all_to_all | solution.py:377
  147.6 0.7 fusion
  148.3 3.9 %all-to-all-done.8 = bf16[16,1,128]{2,1,0:T(2,128)(2,1)S(1)} async-done(((bf16[16,1,128]{2,1,0:T(2,128)(2,1)}), bf16[16,1,128]{2,1,0:T(2,128)(2,1)S(1)}, u32[]{:S(2)}, u32[]{:S(2)}) %all-to-all-start.8) | async-done | bytes 4128 | tf_op jit(solution)/shard_map/all_to_all | solution.py:377
  152.2 3.4 %all-to-all-start.5 = ((bf16[2,2,128,128]{3,2,1,0:T(8,128)(2,1)}), bf16[2,2,128,128]{3,2,1,0:T(8,128)(2,1)S(1)}, u32[]{:S(2)}, u32[]{:S(2)}) async-start(bf16[2,2,128,128]{3,2,1,0:T(8,128)(2,1)} %copy.100), calls=%async_computation.5 | async-start | bytes 262144 | tf_op jit(solution)/shard_map/all_to_all | solution.py:322
  155.6 0.1 fusion.5
  155.8 4.3 %all-to-all-done.5 = bf16[2,2,128,128]{3,2,1,0:T(8,128)(2,1)S(1)} async-done(((bf16[2,2,128,128]{3,2,1,0:T(8,128)(2,1)}), bf16[2,2,128,128]{3,2,1,0:T(8,128)(2,1)S(1)}, u32[]{:S(2)}, u32[]{:S(2)}) %all-to-all-start.5) | async-done | bytes 131104 | tf_op jit(solution)/shard_map/all_to_all | solution.py:322
  160.1 19.7 %all_to_all.72 = f32[12,24,256]{2,1,0:T(8,128)S(1)} all-to-all(f32[12,24,256]{2,1,0:T(8,128)S(1)} %broadcast_in_dim.54), channel_id=1, replica_groups=mesh['y'=8,'zh'=6,'zl'=2,'head'=8] {'zh','zl'}, dimensions={0} | all-to-all | bytes 589824 | tf_op jit(solution)/shard_map/all_to_all | solution.py:309
  179.8 3.5 %all-to-all-start.9 = ((bf16[2,2,128,128]{3,2,1,0:T(8,128)(2,1)}), bf16[2,2,128,128]{3,2,1,0:T(8,128)(2,1)S(1)}, u32[]{:S(2)}, u32[]{:S(2)}) async-start(bf16[2,2,128,128]{3,2,1,0:T(8,128)(2,1)} %get-tuple-element.53), calls=%async_computation.9 | async-start | bytes 262144 | tf_op jit(solution)/shard_map/all_to_all | solution.py:322
  183.4 0.1 copy.113
  183.5 0.7 copy.108
  184.2 0.1 copy.112
  184.4 0.7 copy.107
  185.1 2.7 %all-to-all-done.9 = bf16[2,2,128,128]{3,2,1,0:T(8,128)(2,1)S(1)} async-done(((bf16[2,2,128,128]{3,2,1,0:T(8,128)(2,1)}), bf16[2,2,128,128]{3,2,1,0:T(8,128)(2,1)S(1)}, u32[]{:S(2)}, u32[]{:S(2)}) %all-to-all-start.9) | async-done | bytes 131104 | tf_op jit(solution)/shard_map/all_to_all | solution.py:322
  187.8 0.7 broadcast_in_dim.55
  188.5 3.4 %all-to-all-start.11 = ((f32[8,24,256]{2,1,0:T(8,128)}), f32[8,24,256]{2,1,0:T(8,128)S(1)}, u32[]{:S(2)}, u32[]{:S(2)}) async-start(f32[8,24,256]{2,1,0:T(8,128)} %broadcast_in_dim.55), calls=%async_computation.11 | async-start | bytes 393216 | tf_op jit(solution)/shard_map/all_to_all | solution.py:309
  191.9 0.8 convolution_convert_fusion
  192.7 0.1 copy.105
  192.9 0.7 copy.110
  193.6 0.1 copy.104
  193.7 0.7 copy.109
  194.5 7.1 %all-to-all-done.11 = f32[8,24,256]{2,1,0:T(8,128)S(1)} async-done(((f32[8,24,256]{2,1,0:T(8,128)}), f32[8,24,256]{2,1,0:T(8,128)S(1)}, u32[]{:S(2)}, u32[]{:S(2)}) %all-to-all-start.11) | async-done | bytes 196640 | tf_op jit(solution)/shard_map/all_to_all | solution.py:309
  201.6 0.5 slice_bitcast_fusion.3
  202.1 0.6 slice_bitcast_fusion.2
  (46 shorter events, 0.5 us)
Async XLA Ops:
  0.6 0.8 copy-start
  2.9 18.3 %all-to-all-start = ((f32[16,1,128]{2,1,0:T(1,128)}), f32[16,1,128]{2,1,0:T(1,128)S(1)}, u32[]{:S(2)}, u32[]{:S(2)}) async-start(f32[16,1,128]{2,1,0:T(1,128)} %bitcast.5), calls=%async_computation | async-start | bytes 16384 | tf_op jit(solution)/shard_map/all_to_all | solution.py:341
  21.2 7.9 %all-to-all-start.1 = ((bf16[2,2,128,128]{3,2,1,0:T(8,128)(2,1)}), bf16[2,2,128,128]{3,2,1,0:T(8,128)(2,1)S(1)}, u32[]{:S(2)}, u32[]{:S(2)}) async-start(bf16[2,2,128,128]{3,2,1,0:T(8,128)(2,1)} %pad_maximum_fusion), calls=%async_computation.1 | async-start | bytes 262144 | tf_op jit(solution)/shard_map/all_to_all | solution.py:318
  35.4 26.2 %all-to-all-start.2 = ((f16[6,272,128]{2,1,0:T(8,128)(2,1)}), f16[6,272,128]{2,1,0:T(8,128)(2,1)S(1)}, u32[]{:S(2)}, u32[]{:S(2)}) async-start(f16[6,272,128]{2,1,0:T(8,128)(2,1)} %broadcast_in_dim.22), calls=%async_computation.2 | async-start | bytes 835584 | tf_op jit(solution)/shard_map/all_to_all | solution.py:309
  62.7 8.4 %copy-start.1 = (f32[256,128]{1,0:T(8,128)}, f32[256,128]{1,0:T(8,128)S(1)}, u32[]{:S(2)}) copy-start(f32[256,128]{1,0:T(8,128)S(1)} %get-tuple-element.33.own) | copy-start | bytes 393220
  62.7 8.0 %copy-start.10 = (bf16[128,256]{1,0:T(8,128)(2,1)S(1)}, bf16[128,256]{1,0:T(8,128)(2,1)}, u32[]{:S(2)}) copy-start(bf16[128,256]{1,0:T(8,128)(2,1)} %param.10) | copy-start | bytes 196612
  62.7 8.3 %copy-start.11 = (bf16[128,256]{1,0:T(8,128)(2,1)S(1)}, bf16[128,256]{1,0:T(8,128)(2,1)}, u32[]{:S(2)}) copy-start(bf16[128,256]{1,0:T(8,128)(2,1)} %param.13) | copy-start | bytes 196612
  63.7 22.8 %all-to-all-start.3 = ((f16[8,272,128]{2,1,0:T(8,128)(2,1)}), f16[8,272,128]{2,1,0:T(8,128)(2,1)S(1)}, u32[]{:S(2)}, u32[]{:S(2)}) async-start(f16[8,272,128]{2,1,0:T(8,128)(2,1)} %broadcast_in_dim.23), calls=%async_computation.3 | async-start | bytes 1114112 | tf_op jit(solution)/shard_map/all_to_all | solution.py:309
  86.5 3.4 %copy-start.9 = (f16[8,272,128]{2,1,0:T(8,128)(2,1)}, f16[8,272,128]{2,1,0:T(8,128)(2,1)S(1)}, u32[]{:S(2)}) copy-start(f16[8,272,128]{2,1,0:T(8,128)(2,1)S(1)} %all-to-all-done.3) | copy-start | bytes 1671172
  86.5 7.8 %all-to-all-start.4 = ((bf16[2,2,128,128]{3,2,1,0:T(8,128)(2,1)}), bf16[2,2,128,128]{3,2,1,0:T(8,128)(2,1)S(1)}, u32[]{:S(2)}, u32[]{:S(2)}) async-start(bf16[2,2,128,128]{3,2,1,0:T(8,128)(2,1)} %pad_maximum_fusion.1), calls=%async_computation.4 | async-start | bytes 262144 | tf_op jit(solution)/shard_map/all_to_all | solution.py:318
  94.3 0.9 copy-start.2
  98.7 22.1 %copy-start.3 = (f32[2,128,128]{2,1,0:T(8,128)}, f32[2,128,128]{2,1,0:T(8,128)S(1)}, u32[]{:S(2)}) copy-start(f32[2,128,128]{2,1,0:T(8,128)S(1)} %get-tuple-element.42.draw) | copy-start | bytes 393220
  98.7 22.1 %copy-start.5 = (f32[128,128]{1,0:T(8,128)}, f32[128,128]{1,0:T(8,128)S(1)}, u32[]{:S(2)}) copy-start(f32[128,128]{1,0:T(8,128)S(1)} %get-tuple-element.47.give) | copy-start | bytes 196612
  98.7 22.1 %copy-start.7 = (bf16[2,128,128]{2,1,0:T(8,128)(2,1)}, bf16[2,128,128]{2,1,0:T(8,128)(2,1)S(1)}, u32[]{:S(2)}) copy-start(bf16[2,128,128]{2,1,0:T(8,128)(2,1)S(1)} %get-tuple-element.39) | copy-start | bytes 196612
  120.8 6.0 %copy-start.4 = (f32[2,128,128]{2,1,0:T(8,128)S(1)}, f32[2,128,128]{2,1,0:T(8,128)}, u32[]{:S(2)}) copy-start(f32[2,128,128]{2,1,0:T(8,128)} %copy-done.3) | copy-start | bytes 393220
  121.6 5.9 %copy-start.8 = (bf16[2,128,128]{2,1,0:T(8,128)(2,1)S(1)}, bf16[2,128,128]{2,1,0:T(8,128)(2,1)}, u32[]{:S(2)}) copy-start(bf16[2,128,128]{2,1,0:T(8,128)(2,1)} %copy-done.7) | copy-start | bytes 196612
  121.6 15.0 %all-to-all-start.7 = ((f16[8,144,128]{2,1,0:T(8,128)(2,1)}), f16[8,144,128]{2,1,0:T(8,128)(2,1)}, u32[]{:S(2)}, u32[]{:S(2)}) async-start(f16[8,144,128]{2,1,0:T(8,128)(2,1)} %broadcast_in_dim.25), calls=%async_computation.7 | async-start | bytes 589824 | tf_op jit(solution)/shard_map/all_to_all | solution.py:309
  126.8 10.9 %copy-start.6 = (f32[128,128]{1,0:T(8,128)S(1)}, f32[128,128]{1,0:T(8,128)}, u32[]{:S(2)}) copy-start(f32[128,128]{1,0:T(8,128)} %copy-done.5) | copy-start | bytes 196612
  142.1 10.1 %all-to-all-start.8 = ((bf16[16,1,128]{2,1,0:T(2,128)(2,1)}), bf16[16,1,128]{2,1,0:T(2,128)(2,1)S(1)}, u32[]{:S(2)}, u32[]{:S(2)}) async-start(bf16[16,1,128]{2,1,0:T(2,128)(2,1)} %copy.103), calls=%async_computation.8 | async-start | bytes 16384 | tf_op jit(solution)/shard_map/all_to_all | solution.py:377
  152.2 7.8 %all-to-all-start.5 = ((bf16[2,2,128,128]{3,2,1,0:T(8,128)(2,1)}), bf16[2,2,128,128]{3,2,1,0:T(8,128)(2,1)S(1)}, u32[]{:S(2)}, u32[]{:S(2)}) async-start(bf16[2,2,128,128]{3,2,1,0:T(8,128)(2,1)} %copy.100), calls=%async_computation.5 | async-start | bytes 262144 | tf_op jit(solution)/shard_map/all_to_all | solution.py:322
  179.8 12.1 %copy-start.12 = (bf16[256,16]{0,1:T(8,128)(2,1)S(1)}, bf16[256,16]{0,1:T(8,128)(2,1)}, u32[]{:S(2)}) copy-start(bf16[256,16]{0,1:T(8,128)(2,1)} %param.8) | copy-start | bytes 24580
  179.8 8.0 %all-to-all-start.9 = ((bf16[2,2,128,128]{3,2,1,0:T(8,128)(2,1)}), bf16[2,2,128,128]{3,2,1,0:T(8,128)(2,1)S(1)}, u32[]{:S(2)}, u32[]{:S(2)}) async-start(bf16[2,2,128,128]{3,2,1,0:T(8,128)(2,1)} %get-tuple-element.53), calls=%async_computation.9 | async-start | bytes 262144 | tf_op jit(solution)/shard_map/all_to_all | solution.py:322
  188.5 13.1 %all-to-all-start.11 = ((f32[8,24,256]{2,1,0:T(8,128)}), f32[8,24,256]{2,1,0:T(8,128)S(1)}, u32[]{:S(2)}, u32[]{:S(2)}) async-start(f32[8,24,256]{2,1,0:T(8,128)} %broadcast_in_dim.55), calls=%async_computation.11 | async-start | bytes 393216 | tf_op jit(solution)/shard_map/all_to_all | solution.py:309

commit v2 on v1

--- a/solution.py
+++ b/solution.py
@@ -217,10 +217,20 @@
     return lambda j: scaled_back(got[j, 0:D], got[j, D : D + 8])
 
 
-def kernel_prepare(lg, kv, send, less, gain, inv, sk, sv, bk):
+def in_order(side, mine, theirs):
+    first = side[0] == 0
+    return jnp.where(first, mine, theirs), jnp.where(first, theirs, mine)
+
+
+def blocks_of(side, own, swapped):
+    return in_order(side, jnp.where(side[0] == 0, own[:, :D], own[:, D:]), swapped)
+
+
+def kernel_prepare(side, lg, k, v, swapped, send, less, gain, inv, sk, sv, bk):
     moves = []
+    ks, vs = blocks_of(side, k[...], swapped[0]), blocks_of(side, v[...], swapped[1])
     for b in range(2):
-        w, n, *rest, _ = block_prepare(kv[b, 0], kv[b, 1], lg[b : b + 1, :])
+        w, n, *rest, _ = block_prepare(ks[b], vs[b], lg[b : b + 1, :])
         less[b], gain[b] = w, n
         inv[b], sk[b], sv[b], bk[b] = rest
         moves.append((w, n))
@@ -240,8 +250,10 @@
     own[...] = chain_back_matrix(less_of(got), place[0], count)
 
 
-def kernel_outputs(count, place, got, own, lg, kv, qc, less, gain, inv, sk, sv,
+def kernel_outputs(count, place, side, got, own, lg, k, q, ct, swapped, less, gain, inv, sk, sv,
                    out, start, err, draw, back0, give, send):
+    ks, qs = blocks_of(side, k[...], swapped[0]), blocks_of(side, q[...], swapped[2])
+    cs = blocks_of(side, ct[...], swapped[3])
     first = chain_state(less_of(got), gain_of(got), place[0], count)
     before = dot3(first, own[:D]) + own[D:]
     gives = []
@@ -249,7 +261,7 @@
         if b == 1:
             before = step(before, less[0]) + gain[0]
         normed, e, dr, b0, g = block_outputs(
-            qc[b, 0], kv[b, 0], qc[b, 1], lg[b : b + 1, :], before, inv[b], sk[b], sv[b]
+            qs[b], ks[b], cs[b], lg[b : b + 1, :], before, inv[b], sk[b], sv[b]
         )
         out[b] = normed.astype(BF16)
         start[b], err[b], draw[b], back0[b] = before, e, dr, b0
@@ -258,13 +270,17 @@
     send[0:D], send[D : D + 16] = packed(step(gives[1], less[0], NT) + gives[0])
 
 
-def kernel_early(lg, kv, qc, start, err, draw, dq, dkp):
+def kernel_early(side, lg, k, q, swapped, start, err, draw, out, mine, theirs, dkp):
+    ks, qs = blocks_of(side, k[...], swapped[0]), blocks_of(side, q[...], swapped[2])
+    dqs = []
     for b in range(2):
-        x, y = block_grads_early(
-            qc[b, 0], kv[b, 0], lg[b : b + 1, :], start[b], err[b], draw[b]
+        dq, dkp[b] = block_grads_early(
+            qs[b], ks[b], lg[b : b + 1, :], start[b], err[b], draw[b]
         )
-        dq[b] = x.astype(BF16)
-        dkp[b] = y
+        dqs.append(dq)
+    mine[0], theirs[0] = in_order(side, out[0], out[1])
+    dqs = in_order(side, *dqs)
+    mine[1], theirs[1] = dqs[0].astype(BF16), dqs[1].astype(BF16)
 
 
 def kernel_row_back(count, place, got, gives, send, own):
@@ -273,18 +289,27 @@
     own[...] = after
 
 
-def kernel_grads(count, place, got, gives, matrix, own, lg, kv, less, give, start, err,
-                 back0, bk, dkp, dkv, dlog):
+def kernel_grads(count, place, side, got, gives, matrix, own, lg, k, swapped, less, give, start,
+                 err, back0, bk, dkp, mine, theirs, rows, bias):
+    ks = blocks_of(side, k[...], swapped[0])
     _, row_after = chain_back(less_of(got), give_of(gives), place[0], count, total=False)
     end_grad = dot3(row_after, matrix[...]) + own[...]
-    for b in (1, 0):
-        if b == 0:
-            end_grad = step(end_grad, less[1], NT) + give[...]
-        x, y, z = block_grads(
-            kv[b, 0], lg[b : b + 1, :], start[b], end_grad, err[b], back0[b], bk[b], dkp[b]
-        )
-        dkv[b, 0], dkv[b, 1] = x.astype(BF16), y.astype(BF16)
-        dlog[b : b + 1, :] = z
+    later = block_grads(
+        ks[1], lg[1:2, :], start[1], end_grad, err[1], back0[1], bk[1], dkp[1]
+    )
+    end_grad = step(end_grad, less[1], NT) + give[...]
+    earlier = block_grads(
+        ks[0], lg[0:1, :], start[0], end_grad, err[0], back0[0], bk[0], dkp[0]
+    )
+    for i in range(2):
+        x, y = in_order(side, earlier[i], later[i])
+        mine[i], theirs[i] = x.astype(BF16), y.astype(BF16)
+    odd = lax.broadcasted_iota(jnp.int32, (16, L), 0) % 2
+    rows[...] = jnp.where(odd == 0, earlier[2], later[2]).astype(BF16)
+    part = jnp.sum(earlier[2] + later[2], axis=1, keepdims=True)
+    row = lax.broadcasted_iota(jnp.int32, (8, 2 * D), 0)
+    col = lax.broadcasted_iota(jnp.int32, (8, 2 * D), 1)
+    bias[...] = jnp.where((row == 0) & (col == side[0]), part, 0.0)
 
 
 VM = pl.BlockSpec(memory_space=pltpu.VMEM)
@@ -313,39 +338,47 @@
     return copies(x.astype(jnp.float16), axis).astype(F32)
 
 
-def to_heads(*arrays):
-    parts = jnp.stack([a.reshape(L, 2, D).transpose(1, 0, 2) for a in arrays], axis=1)
-    return lax.all_to_all(parts, "zl", 0, 0)
-
-
-def to_blocks(parts):
-    heads = lax.all_to_all(parts, "zl", 0, 0)
-    return [heads[:, i].transpose(1, 0, 2).reshape(L, 2 * D) for i in range(heads.shape[1])]
+def swap(x):
+    return lax.ppermute(x, "zl", [(0, 1), (1, 0)])
+
+
+def joined(side, mine, theirs):
+    return jnp.where(
+        side == 0,
+        jnp.concatenate([mine, theirs], axis=1),
+        jnp.concatenate([theirs, mine], axis=1),
+    )
 
 
 HALF = ((D, D), F32)
 PAIR = ((2, D, D), F32)
-ALL = ("zl", "head")
+PAIRB = ((2, L, D), BF16)
+ALL = ("head", "zl")
 
 
 def per_device(hidden, beta_weight, beta_bias, queries, keys, values, cotangent):
     rows, pairs = lax.axis_size("y"), lax.axis_size("zh")
-    side = lax.axis_index("zl")
+    side = lax.axis_index("zl").astype(jnp.int32)
     at_y = lax.axis_index("y").astype(jnp.int32).reshape(1)
     at_z = lax.axis_index("zh").astype(jnp.int32).reshape(1)
-
+    at_s = side.reshape(1)
+
+    swapped = swap(
+        jnp.stack([
+            jnp.where(side == 0, a[:, D:], a[:, :D])
+            for a in (keys, values, queries, cotangent)
+        ])
+    )
     part = lax.dot_general(
         beta_weight, hidden, (((0,), (1,)), ((), ())), preferred_element_type=F32
     )
-    part = part.reshape(8, 2, L).transpose(1, 0, 2).reshape(16, L)
     part = lax.all_to_all(part, ALL, 0, 0, tiled=True)
     bias = jnp.where(side == 0, beta_bias[0], beta_bias[1])
-    logits = jnp.sum(part.reshape(2, 8, L), axis=1) + bias
-    kv = to_heads(keys, values)
-    qc = to_heads(queries, cotangent)
+    logits = jnp.sum(part.reshape(8, 2, L), axis=0) + bias
 
     send1, less, gain, inv, sk, sv, bk = call(
-        kernel_prepare, [((2 * D + 16, D), F32)] + [PAIR] * 6, logits, kv
+        kernel_prepare, [((2 * D + 16, D), F32)] + [PAIR] * 6,
+        at_s, logits, keys, values, swapped,
     )
     got1 = spread(send1, "zh")
     send2, own1 = call(
@@ -356,41 +389,41 @@
     (matrix,) = call(functools.partial(kernel_row_matrix, pairs), [HALF], at_z, got1)
     out, start, err, draw, back0, give, send3 = call(
         functools.partial(kernel_outputs, rows),
-        [((2, L, D), BF16)] + [PAIR] * 4 + [HALF, ((D + 16, D), F32)],
-        at_y, got2, own1, logits, kv, qc, less, gain, inv, sk, sv,
+        [PAIRB] + [PAIR] * 4 + [HALF, ((D + 16, D), F32)],
+        at_y, at_s, got2, own1, logits, keys, queries, cotangent, swapped,
+        less, gain, inv, sk, sv,
     )
     got3 = spread(send3, "zh")
-    dq, dkp = call(
-        kernel_early, [((2, L, D), BF16), PAIR], logits, kv, qc, start, err, draw
+    mine, theirs, dkp = call(
+        kernel_early, [PAIRB, PAIRB, PAIR],
+        at_s, logits, keys, queries, swapped, start, err, draw, out,
     )
     send4, own2 = call(
         functools.partial(kernel_row_back, pairs), [((D + 16, D), F32), HALF], at_z, got1, got3
     )
     got4 = spread(send4, "y")
-    out, dq = to_blocks(jnp.stack([out, dq], axis=1))
-    dkv, d_logits = call(
-        functools.partial(kernel_grads, rows), [((2, 2, L, D), BF16), ((2, L), F32)],
-        at_y, got2, got4, matrix, own2, logits, kv, less, give, start, err, back0, bk, dkp,
-    )
-
-    grads = jnp.repeat(d_logits.astype(BF16), 8, axis=0)
-    grads = lax.all_to_all(grads, ALL, 0, 0, tiled=True)
-    grads, dkv = lax.optimization_barrier((grads, dkv))
-    all_grads = grads.reshape(2, 8, L).transpose(1, 0, 2).reshape(16, L)
+    theirs = swap(theirs)
+    mine_kv, theirs_kv, grad_rows, bias_part = call(
+        functools.partial(kernel_grads, rows),
+        [PAIRB, PAIRB, ((16, L), BF16), ((8, 2 * D), F32)],
+        at_y, at_s, got2, got4, matrix, own2, logits, keys, swapped, less, give, start, err,
+        back0, bk, dkp,
+    )
+
+    all_grads = lax.all_to_all(grad_rows, ALL, 0, 0, tiled=True)
+    all_grads, theirs_kv = lax.optimization_barrier((all_grads, theirs_kv))
     weight_part = lax.dot_general(
         all_grads, hidden, (((1,), (0,)), ((), ())), preferred_element_type=F32
     )
-    bias_part = jnp.sum(d_logits)
-    slot = lax.broadcasted_iota(jnp.int32, (8, 2 * D), 0) * (2 * D) + lax.broadcasted_iota(
-        jnp.int32, (8, 2 * D), 1
-    )
-    total = jnp.concatenate([weight_part, jnp.where(slot == side, bias_part, 0.0)], axis=0)
+    total = jnp.concatenate([weight_part, bias_part], axis=0)
     total = jnp.sum(copies(total, ("zh", "zl")), axis=0)
     total = jnp.sum(copies(total, "y"), axis=0)
-    dk, dv = to_blocks(dkv)
+    theirs_kv = swap(theirs_kv)
     d_hidden = lax.dot_general(
         all_grads, beta_weight, (((0,), (1,)), ((), ())), preferred_element_type=F32
     )
+    out, dq = [joined(side, mine[i], theirs[i]) for i in range(2)]
+    dk, dv = [joined(side, mine_kv[i], theirs_kv[i]) for i in range(2)]
     return (out, dq, dk, dv, d_hidden.astype(BF16), total[:16].T, total[16, 0:2])
 
 

time: 204 us -> 183 us (0.90)
  blocking collectives: 40.6 us -> 33.1 us
  starting transfers between devices: 54.7 us -> 48.4 us
  local copies, waits for them, and re-layouts: 15.4 us -> 9.52 us
  waiting for transfers between devices: 66.8 us -> 64.1 us
    all_to_all x2 -> x1, blocking collectives: 40.6 us -> 21.2 us  [copies(): lax.all_to_all(jnp.broadcast_to(x[None], (count,) + x.shape), axis, 0, 0)]
    all_to_all x5 -> x0, starting transfers between devices: 19.1 us -> none  [the longest x2 6.89 us: to_blocks(): heads = lax.all_to_all(parts, 'zl', 0, 0)]
    all_to_all x5 -> x0, waiting for transfers between devices: 18.6 us -> none  [the longest x2 7.74 us: to_heads(): return lax.all_to_all(parts, 'zl', 0, 0)]
    all_to_all x0 -> x1, blocking collectives: none -> 11.9 us  [per_device(): all_grads = lax.all_to_all(grad_rows, ALL, 0, 0, tiled=True)]
    ppermute x0 -> x3, waiting for transfers between devices: none -> 10.2 us  [swap(): return lax.ppermute(x, 'zl', [(0, 1), (1, 0)])]
    ppermute x0 -> x3, starting transfers between devices: none -> 9.17 us  [swap(): return lax.ppermute(x, 'zl', [(0, 1), (1, 0)])]
    all_to_all x4 -> x5, waiting for transfers between devices: 48.2 us -> 53.9 us  [copies(): lax.all_to_all(jnp.broadcast_to(x[None], (count,) + x.shape), axis, 0, 0)]
    unnamed x37 -> x31, local copies, waits for them, and re-layouts: 7.15 us -> 3.14 us
  transfers between devices with their start and end apart: 10 -> 9, of which waited for: 9 -> 7; matrix products, arithmetic and copies ran while one was open for 6% -> 4% of each run, Pallas kernels for 1% -> 1%
where the time goes in v2:
time: 183 us; the launch traced here: 182 us
  waiting for transfers between devices  64.1 us (35%)
  starting transfers between devices  48.4 us (26%)
  blocking collectives  33.1 us (18%)
  Pallas kernels  15.4 us (8%)
  local copies, waits for them, and re-layouts  9.52 us (5%)
  other arithmetic  6.88 us (4%)
  matrix products  2.4 us (1%)
  between operations  2.3 us (1%)
    all_to_all x5, waiting for transfers between devices, copies(): lax.all_to_all(jnp.broadcast_to(x[None], (count,) + x.shape), axis, 0, 0)  53.9 us
    all_to_all x5, starting transfers between devices, copies(): lax.all_to_all(jnp.broadcast_to(x[None], (count,) + x.shape), axis, 0, 0)  26.4 us
    all_to_all x1, blocking collectives, copies(): lax.all_to_all(jnp.broadcast_to(x[None], (count,) + x.shape), axis, 0, 0)  21.2 us
    pallas_call x7, Pallas kernels, call(): pl.pallas_call(body, out_shape=[jax.ShapeDtypeStruct(s, t) for s, t in ou...  15.4 us
    all_to_all x1, starting transfers between devices, per_device(): part = lax.all_to_all(part, ALL, 0, 0, tiled=True)  12.8 us
    all_to_all x1, blocking collectives, per_device(): all_grads = lax.all_to_all(grad_rows, ALL, 0, 0, tiled=True)  11.9 us
    ppermute x3, waiting for transfers between devices, swap(): return lax.ppermute(x, 'zl', [(0, 1), (1, 0)])  10.2 us
    ppermute x3, starting transfers between devices, swap(): return lax.ppermute(x, 'zl', [(0, 1), (1, 0)])  9.17 us
  transfers between devices with their start and end apart: 9, of which 7 were waited for; matrix products, arithmetic and copies ran while one was open for 4% of the time, Pallas kernels for 1%

profile of v2, /device:TPU:2, one launch (start us, length us, event | category | flops | bytes accessed | tf_op | source)
XLA Modules:
  0.0 182.0 jit_solution(16921070701336222773)
XLA Ops:
  0.6 0.0 copy-start
  0.6 0.8 copy-done
  1.5 1.4 fusion.1
  2.9 12.8 %all-to-all-start = ((f32[16,1,128]{2,1,0:T(1,128)}), f32[16,1,128]{2,1,0:T(1,128)S(1)}, u32[]{:S(2)}, u32[]{:S(2)}) async-start(f32[16,1,128]{2,1,0:T(1,128)} %bitcast.2), calls=%async_computation | async-start | bytes 16384 | tf_op jit(solution)/shard_map/all_to_all | solution.py:375
  15.7 0.8 select_bitcast_fusion.2
  16.5 0.8 select_bitcast_fusion
  17.3 0.8 select_bitcast_fusion.1
  18.1 0.8 select_bitcast_fusion.3
  18.9 3.4 %collective-permute-start = (bf16[4,128,128]{2,1,0:T(8,128)(2,1)S(1)}, bf16[4,128,128]{2,1,0:T(8,128)(2,1)S(1)}, u32[]{:S(2)}, u32[]{:S(2)}) collective-permute-start(bf16[4,128,128]{2,1,0:T(8,128)(2,1)S(1)} %pad_maximum_fusion), channel_id=1, source_target_pairs={{0,8},{8,0},{1,9},{9,1},{2,10},{10,2},{3,11},{11,3},{4,12},{12,4},... | collective-permute-start | bytes 393224 | tf_op jit(solution)/shard_map/ppermute | solution.py:342
  22.3 1.3 fusion
  24.9 0.0 all-to-all-done
  24.9 1.4 collective-permute-done.swapped
  26.3 0.8 copy-done.1
  27.2 0.8 copy-done.13
  28.0 5.5 %shard_map.126 = (f32[272,128]{1,0:T(8,128)S(1)}, f32[2,128,128]{2,1,0:T(8,128)S(1)}, f32[2,128,128]{2,1,0:T(8,128)S(1)}, f32[2,128,128]{2,1,0:T(8,128)S(1)}, f3...) custom-call(s32[1]{0:T(128)} %bitcast.side, f32[2,128]{1,0:T(2,128)S(1)} %broadcast_add_fusion.lg, ...), custom_call_target="tpu_custom_call" | custom-call | flops 100000000 | bytes 263172 | tf_op jit(solution)/shard_map/pallas_call | solution.py:322
  33.5 0.8 broadcast_in_dim.12
  34.3 8.0 %all-to-all-start.1 = ((f16[6,272,128]{2,1,0:T(8,128)(2,1)}), f16[6,272,128]{2,1,0:T(8,128)(2,1)S(1)}, u32[]{:S(2)}, u32[]{:S(2)}) async-start(f16[6,272,128]{2,1,0:T(8,128)(2,1)} %broadcast_in_dim.12), calls=%async_computation.1 | async-start | bytes 835584 | tf_op jit(solution)/shard_map/all_to_all | solution.py:334
  42.4 19.0 %all-to-all-done.1 = f16[6,272,128]{2,1,0:T(8,128)(2,1)S(1)} async-done(((f16[6,272,128]{2,1,0:T(8,128)(2,1)}), f16[6,272,128]{2,1,0:T(8,128)(2,1)S(1)}, u32[]{:S(2)}, u32[]{:S(2)}) %all-to-all-start.1) | async-done | bytes 417824 | tf_op jit(solution)/shard_map/all_to_all | solution.py:334
  61.4 0.1 convert_element_type.28.got
  61.4 1.1 shard_map.127
  62.5 0.0 copy-start.7
  62.5 0.9 broadcast_in_dim.13
  63.4 0.0 copy-done.7
  63.4 7.1 %all-to-all-start.2 = ((f16[8,272,128]{2,1,0:T(8,128)(2,1)}), f16[8,272,128]{2,1,0:T(8,128)(2,1)}, u32[]{:S(2)}, u32[]{:S(2)}) async-start(f16[8,272,128]{2,1,0:T(8,128)(2,1)} %broadcast_in_dim.13), calls=%async_computation.2 | async-start | bytes 1114112 | tf_op jit(solution)/shard_map/all_to_all | solution.py:334
  70.5 0.0 copy-start.3
  70.5 0.0 copy-start.4
  70.5 14.3 %all-to-all-done.2 = f16[8,272,128]{2,1,0:T(8,128)(2,1)} async-done(((f16[8,272,128]{2,1,0:T(8,128)(2,1)}), f16[8,272,128]{2,1,0:T(8,128)(2,1)}, u32[]{:S(2)}, u32[]{:S(2)}) %all-to-all-start.2) | async-done | bytes 557088 | tf_op jit(solution)/shard_map/all_to_all | solution.py:334
  84.8 1.2 convert_element_type.30.got
  86.0 0.0 copy-done.2
  86.0 0.0 copy-done.3
  86.0 0.0 copy-done.4
  86.0 3.5 %shard_map.128 = (bf16[2,128,128]{2,1,0:T(8,128)(2,1)S(1)}, f32[2,128,128]{2,1,0:T(8,128)S(1)}, f32[2,128,128]{2,1,0:T(8,128)S(1)}, f32[2,128,128]{2,1,0:T(8,128...) custom-call(s32[1]{0:T(128)} %bitcast.10.place, s32[1]{0:T(128)} %bitcast.side, ...), custom_call_target="tpu_custom_call" | custom-call | flops 100000000 | bytes 2229256 | tf_op jit(solution)/shard_map/pallas_call | solution.py:322
  89.5 0.0 copy-start.9
  89.5 0.0 copy-start.11
  89.6 0.5 copy-done.9
  90.1 0.0 copy-done.11
  90.2 21.2 %all_to_all.51 = f16[6,144,128]{2,1,0:T(8,128)(2,1)S(1)} all-to-all(f16[6,144,128]{2,1,0:T(8,128)(2,1)S(1)} %broadcast_in_dim.14), channel_id=1, replica_groups=mesh['y'=8,'zh'=6,'zl'=2,'head'=8] {'zh'}, dimensions={0} | all-to-all | bytes 442368 | tf_op jit(solution)/shard_map/all_to_all | solution.py:334
  111.4 1.1 shard_map.130
  112.5 0.0 copy-start.12
  112.5 0.8 broadcast_in_dim.15
  113.3 4.1 %all-to-all-start.4 = ((f16[8,144,128]{2,1,0:T(8,128)(2,1)}), f16[8,144,128]{2,1,0:T(8,128)(2,1)}, u32[]{:S(2)}, u32[]{:S(2)}) async-start(f16[8,144,128]{2,1,0:T(8,128)(2,1)} %broadcast_in_dim.15), calls=%async_computation.4 | async-start | bytes 589824 | tf_op jit(solution)/shard_map/all_to_all | solution.py:334
  117.4 0.0 copy-start.10
  117.4 1.0 shard_map.131.matrix
  118.4 0.7 shard_map.129
  119.1 9.1 %all-to-all-done.4 = f16[8,144,128]{2,1,0:T(8,128)(2,1)} async-done(((f16[8,144,128]{2,1,0:T(8,128)(2,1)}), f16[8,144,128]{2,1,0:T(8,128)(2,1)}, u32[]{:S(2)}, u32[]{:S(2)}) %all-to-all-start.4) | async-done | bytes 294944 | tf_op jit(solution)/shard_map/all_to_all | solution.py:334
  128.2 1.0 convert_element_type.34.gives
  129.2 2.6 %shard_map.132 = (bf16[2,128,128]{2,1,0:T(8,128)(2,1)S(1)}, bf16[2,128,128]{2,1,0:T(8,128)(2,1)S(1)}, bf16[16,128]{1,0:T(8,128)(2,1)S(1)}, f32[8,256]{1,0:T(8,128)S(1)}) custom-call(s32[1]{0:T(128)} %bitcast.10.place, s32[1]{0:T(128)} %bitcast.side, f32[8,272,128]{2,1,0:T(8,128)S(1)} %convert_element_type.30.got, ...), custom_call_target="tpu_custom_call" | custom-call | flops 100000000 | bytes 2884616 | tf_op jit(solution)/shard_map/pallas_call | solution.py:322
  131.9 11.9 %all_to_all.52 = bf16[16,1,128]{2,1,0:T(2,128)(2,1)S(1)} all-to-all(bf16[16,1,128]{2,1,0:T(2,128)(2,1)S(1)} %copy.19), channel_id=1, replica_groups=mesh['y'=8,'zh'=6,'zl'=2,'head'=8] {'head','zl'}, dimensions={0} | all-to-all | bytes 8192 | tf_op jit(solution)/shard_map/all_to_all | solution.py:413
  143.8 0.1 fusion.2
  143.9 0.7 broadcast_in_dim.16
  144.6 3.8 %all-to-all-start.6 = ((f32[12,24,256]{2,1,0:T(8,128)}), f32[12,24,256]{2,1,0:T(8,128)S(1)}, u32[]{:S(2)}, u32[]{:S(2)}) async-start(f32[12,24,256]{2,1,0:T(8,128)} %broadcast_in_dim.16), calls=%async_computation.6 | async-start | bytes 589824 | tf_op jit(solution)/shard_map/all_to_all | solution.py:334
  148.4 3.9 %collective-permute-start.1 = (bf16[2,128,128]{2,1,0:T(8,128)(2,1)S(1)}, bf16[2,128,128]{2,1,0:T(8,128)(2,1)S(1)}, u32[]{:S(2)}, u32[]{:S(2)}) collective-permute-start(bf16[2,128,128]{2,1,0:T(8,128)(2,1)S(1)} %get-tuple-element.47), channel_id=1, source_target_pairs={{0,8},{8,0},{1,9},{9,1},{2,10},{10,2},{3,11},{11,3},{4,12},{12,4},... | collective-permute-start | bytes 196616 | tf_op jit(solution)/shard_map/ppermute | solution.py:342
  152.3 8.8 %collective-permute-done.1 = bf16[2,128,128]{2,1,0:T(8,128)(2,1)S(1)} collective-permute-done((bf16[2,128,128]{2,1,0:T(8,128)(2,1)S(1)}, bf16[2,128,128]{2,1,0:T(8,128)(2,1)S(1)}, u32[]{:S(2)}, u32[]{:S(2)}) %collective-permute-start.1) | collective-permute-done | bytes 65568 | tf_op jit(solution)/shard_map/ppermute | solution.py:342
  161.1 0.7 maximum_select_fusion
  161.8 1.9 %collective-permute-start.2 = (bf16[2,128,128]{2,1,0:T(8,128)(2,1)S(1)}, bf16[2,128,128]{2,1,0:T(8,128)(2,1)S(1)}, u32[]{:S(2)}, u32[]{:S(2)}) collective-permute-start(bf16[2,128,128]{2,1,0:T(8,128)(2,1)S(1)} %get-tuple-element.58), channel_id=1, source_target_pairs={{0,8},{8,0},{1,9},{9,1},{2,10},{10,2},{3,11},{11,3},{4,12},{12,4},... | collective-permute-start | bytes 196616 | tf_op jit(solution)/shard_map/ppermute | solution.py:342
  163.7 3.4 %all-to-all-done.6 = f32[12,24,256]{2,1,0:T(8,128)S(1)} async-done(((f32[12,24,256]{2,1,0:T(8,128)}), f32[12,24,256]{2,1,0:T(8,128)S(1)}, u32[]{:S(2)}, u32[]{:S(2)}) %all-to-all-start.6) | async-done | bytes 294944 | tf_op jit(solution)/shard_map/all_to_all | solution.py:334
  167.1 0.7 broadcast_in_dim.17
  167.8 3.4 %all-to-all-start.7 = ((f32[8,24,256]{2,1,0:T(8,128)}), f32[8,24,256]{2,1,0:T(8,128)S(1)}, u32[]{:S(2)}, u32[]{:S(2)}) async-start(f32[8,24,256]{2,1,0:T(8,128)} %broadcast_in_dim.17), calls=%async_computation.7 | async-start | bytes 393216 | tf_op jit(solution)/shard_map/all_to_all | solution.py:334
  171.2 0.8 convolution_convert_fusion
  172.1 0.0 collective-permute-done.2
  172.1 0.7 maximum_select_fusion.2
  172.8 8.1 %all-to-all-done.7 = f32[8,24,256]{2,1,0:T(8,128)S(1)} async-done(((f32[8,24,256]{2,1,0:T(8,128)}), f32[8,24,256]{2,1,0:T(8,128)S(1)}, u32[]{:S(2)}, u32[]{:S(2)}) %all-to-all-start.7) | async-done | bytes 196640 | tf_op jit(solution)/shard_map/all_to_all | solution.py:334
  180.9 0.5 slice_bitcast_fusion.9
  181.4 0.6 slice_bitcast_fusion.8
  (31 shorter events, 0.3 us)
Async XLA Ops:
  0.6 0.8 copy-start
  2.9 22.0 %all-to-all-start = ((f32[16,1,128]{2,1,0:T(1,128)}), f32[16,1,128]{2,1,0:T(1,128)S(1)}, u32[]{:S(2)}, u32[]{:S(2)}) async-start(f32[16,1,128]{2,1,0:T(1,128)} %bitcast.2), calls=%async_computation | async-start | bytes 16384 | tf_op jit(solution)/shard_map/all_to_all | solution.py:375
  18.9 7.4 %collective-permute-start = (bf16[4,128,128]{2,1,0:T(8,128)(2,1)S(1)}, bf16[4,128,128]{2,1,0:T(8,128)(2,1)S(1)}, u32[]{:S(2)}, u32[]{:S(2)}) collective-permute-start(bf16[4,128,128]{2,1,0:T(8,128)(2,1)S(1)} %pad_maximum_fusion), channel_id=1, source_target_pairs={{0,8},{8,0},{1,9},{9,1},{2,10},{10,2},{3,11},{11,3},{4,12},{12,4},... | collective-permute-start | bytes 393224 | tf_op jit(solution)/shard_map/ppermute | solution.py:342
  26.3 0.8 copy-start.1
  27.2 0.8 copy-start.13
  34.3 27.0 %all-to-all-start.1 = ((f16[6,272,128]{2,1,0:T(8,128)(2,1)}), f16[6,272,128]{2,1,0:T(8,128)(2,1)S(1)}, u32[]{:S(2)}, u32[]{:S(2)}) async-start(f16[6,272,128]{2,1,0:T(8,128)(2,1)} %broadcast_in_dim.12), calls=%async_computation.1 | async-start | bytes 835584 | tf_op jit(solution)/shard_map/all_to_all | solution.py:334
  62.5 0.9 copy-start.7
  63.4 21.4 %all-to-all-start.2 = ((f16[8,272,128]{2,1,0:T(8,128)(2,1)}), f16[8,272,128]{2,1,0:T(8,128)(2,1)}, u32[]{:S(2)}, u32[]{:S(2)}) async-start(f16[8,272,128]{2,1,0:T(8,128)(2,1)} %broadcast_in_dim.13), calls=%async_computation.2 | async-start | bytes 1114112 | tf_op jit(solution)/shard_map/all_to_all | solution.py:334
  70.5 15.5 %copy-start.2 = (bf16[128,256]{1,0:T(8,128)(2,1)S(1)}, bf16[128,256]{1,0:T(8,128)(2,1)}, u32[]{:S(2)}) copy-start(bf16[128,256]{1,0:T(8,128)(2,1)} %k.7) | copy-start | bytes 196612
  70.5 15.5 %copy-start.3 = (bf16[128,256]{1,0:T(8,128)(2,1)S(1)}, bf16[128,256]{1,0:T(8,128)(2,1)}, u32[]{:S(2)}) copy-start(bf16[128,256]{1,0:T(8,128)(2,1)} %q.3) | copy-start | bytes 196612
  70.5 15.5 %copy-start.4 = (bf16[128,256]{1,0:T(8,128)(2,1)S(1)}, bf16[128,256]{1,0:T(8,128)(2,1)}, u32[]{:S(2)}) copy-start(bf16[128,256]{1,0:T(8,128)(2,1)} %ct.1) | copy-start | bytes 196612
  84.8 1.2 copy-start.8
  89.5 0.6 copy-start.9
  89.5 0.6 copy-start.11
  89.5 23.0 %copy-start.5 = (f32[2,128,128]{2,1,0:T(8,128)}, f32[2,128,128]{2,1,0:T(8,128)S(1)}, u32[]{:S(2)}) copy-start(f32[2,128,128]{2,1,0:T(8,128)S(1)} %get-tuple-element.44.draw) | copy-start | bytes 393220
  112.5 5.8 %copy-start.12 = (bf16[2,128,128]{2,1,0:T(8,128)(2,1)S(1)}, bf16[2,128,128]{2,1,0:T(8,128)(2,1)}, u32[]{:S(2)}) copy-start(bf16[2,128,128]{2,1,0:T(8,128)(2,1)} %copy-done.11) | copy-start | bytes 196612
  112.5 5.8 %copy-start.6 = (f32[2,128,128]{2,1,0:T(8,128)S(1)}, f32[2,128,128]{2,1,0:T(8,128)}, u32[]{:S(2)}) copy-start(f32[2,128,128]{2,1,0:T(8,128)} %copy-done.5) | copy-start | bytes 393220
  113.3 14.9 %all-to-all-start.4 = ((f16[8,144,128]{2,1,0:T(8,128)(2,1)}), f16[8,144,128]{2,1,0:T(8,128)(2,1)}, u32[]{:S(2)}, u32[]{:S(2)}) async-start(f16[8,144,128]{2,1,0:T(8,128)(2,1)} %broadcast_in_dim.15), calls=%async_computation.4 | async-start | bytes 589824 | tf_op jit(solution)/shard_map/all_to_all | solution.py:334
  117.4 11.8 %copy-start.10 = (f32[128,128]{1,0:T(8,128)S(1)}, f32[128,128]{1,0:T(8,128)}, u32[]{:S(2)}) copy-start(f32[128,128]{1,0:T(8,128)} %copy-done.9) | copy-start | bytes 196612
  144.6 26.6 %copy-start.14 = (bf16[256,16]{0,1:T(8,128)(2,1)S(1)}, bf16[256,16]{0,1:T(8,128)(2,1)}, u32[]{:S(2)}) copy-start(bf16[256,16]{0,1:T(8,128)(2,1)} %param.8) | copy-start | bytes 24580
  144.6 22.5 %all-to-all-start.6 = ((f32[12,24,256]{2,1,0:T(8,128)}), f32[12,24,256]{2,1,0:T(8,128)S(1)}, u32[]{:S(2)}, u32[]{:S(2)}) async-start(f32[12,24,256]{2,1,0:T(8,128)} %broadcast_in_dim.16), calls=%async_computation.6 | async-start | bytes 589824 | tf_op jit(solution)/shard_map/all_to_all | solution.py:334
  148.4 12.7 %collective-permute-start.1 = (bf16[2,128,128]{2,1,0:T(8,128)(2,1)S(1)}, bf16[2,128,128]{2,1,0:T(8,128)(2,1)S(1)}, u32[]{:S(2)}, u32[]{:S(2)}) collective-permute-start(bf16[2,128,128]{2,1,0:T(8,128)(2,1)S(1)} %get-tuple-element.47), channel_id=1, source_target_pairs={{0,8},{8,0},{1,9},{9,1},{2,10},{10,2},{3,11},{11,3},{4,12},{12,4},... | collective-permute-start | bytes 196616 | tf_op jit(solution)/shard_map/ppermute | solution.py:342
  161.8 10.3 %collective-permute-start.2 = (bf16[2,128,128]{2,1,0:T(8,128)(2,1)S(1)}, bf16[2,128,128]{2,1,0:T(8,128)(2,1)S(1)}, u32[]{:S(2)}, u32[]{:S(2)}) collective-permute-start(bf16[2,128,128]{2,1,0:T(8,128)(2,1)S(1)} %get-tuple-element.58), channel_id=1, source_target_pairs={{0,8},{8,0},{1,9},{9,1},{2,10},{10,2},{3,11},{11,3},{4,12},{12,4},... | collective-permute-start | bytes 196616 | tf_op jit(solution)/shard_map/ppermute | solution.py:342
  167.8 13.1 %all-to-all-start.7 = ((f32[8,24,256]{2,1,0:T(8,128)}), f32[8,24,256]{2,1,0:T(8,128)S(1)}, u32[]{:S(2)}, u32[]{:S(2)}) async-start(f32[8,24,256]{2,1,0:T(8,128)} %broadcast_in_dim.17), calls=%async_computation.7 | async-start | bytes 393216 | tf_op jit(solution)/shard_map/all_to_all | solution.py:334

commit v3 on v2

--- a/solution.py
+++ b/solution.py
@@ -222,15 +222,35 @@
     return jnp.where(first, mine, theirs), jnp.where(first, theirs, mine)
 
 
-def blocks_of(side, own, swapped):
-    return in_order(side, jnp.where(side[0] == 0, own[:, :D], own[:, D:]), swapped)
-
-
-def kernel_prepare(side, lg, k, v, swapped, send, less, gain, inv, sk, sv, bk):
+def kernel_first(side, slot, bias, weight, hidden, k, v, q, ct, part, mine, theirs,
+                 offset, narrow, held, done):
+    small = pltpu.make_async_copy(bias, offset, done.at[6])
+    small.start()
+    copies = [pltpu.make_async_copy(weight, narrow, done.at[5])] + [
+        pltpu.make_async_copy(x, held.at[i], done.at[i])
+        for i, x in enumerate((hidden, k, v, q, ct))
+    ]
+    for copy in copies:
+        copy.start()
+    copies[0].wait()
+    copies[1].wait()
+    small.wait()
+    head = lax.broadcasted_iota(jnp.int32, (16, L), 0) - 2 * slot[0]
+    own = jnp.where(head == 0, offset[0], jnp.where(head == 1, offset[1], 0.0))
+    part[...] = dot1(narrow[...], held[0], NT) + own
+    for i in range(4):
+        copies[i + 2].wait()
+        mine[i], theirs[i] = in_order(side, held[i + 1, :, :D], held[i + 1, :, D:])
+
+
+def kernel_prepare(side, part, mine, swapped, send, lg, less, gain, inv, sk, sv, bk):
+    odd = lax.broadcasted_iota(jnp.int32, (16, L), 0) % 2
     moves = []
-    ks, vs = blocks_of(side, k[...], swapped[0]), blocks_of(side, v[...], swapped[1])
+    ks, vs = in_order(side, mine[0], swapped[0]), in_order(side, mine[1], swapped[1])
     for b in range(2):
-        w, n, *rest, _ = block_prepare(ks[b], vs[b], lg[b : b + 1, :])
+        logit = jnp.sum(jnp.where(odd == b, part[...], 0.0), axis=0, keepdims=True)
+        lg[b : b + 1, :] = logit
+        w, n, *rest, _ = block_prepare(ks[b], vs[b], logit)
         less[b], gain[b] = w, n
         inv[b], sk[b], sv[b], bk[b] = rest
         moves.append((w, n))
@@ -250,10 +270,10 @@
     own[...] = chain_back_matrix(less_of(got), place[0], count)
 
 
-def kernel_outputs(count, place, side, got, own, lg, k, q, ct, swapped, less, gain, inv, sk, sv,
+def kernel_outputs(count, place, side, got, own, lg, mine, swapped, less, gain, inv, sk, sv,
                    out, start, err, draw, back0, give, send):
-    ks, qs = blocks_of(side, k[...], swapped[0]), blocks_of(side, q[...], swapped[2])
-    cs = blocks_of(side, ct[...], swapped[3])
+    ks, qs = in_order(side, mine[0], swapped[0]), in_order(side, mine[2], swapped[2])
+    cs = in_order(side, mine[3], swapped[3])
     first = chain_state(less_of(got), gain_of(got), place[0], count)
     before = dot3(first, own[:D]) + own[D:]
     gives = []
@@ -270,8 +290,8 @@
     send[0:D], send[D : D + 16] = packed(step(gives[1], less[0], NT) + gives[0])
 
 
-def kernel_early(side, lg, k, q, swapped, start, err, draw, out, mine, theirs, dkp):
-    ks, qs = blocks_of(side, k[...], swapped[0]), blocks_of(side, q[...], swapped[2])
+def kernel_early(side, lg, own, swapped, start, err, draw, out, mine, theirs, dkp):
+    ks, qs = in_order(side, own[0], swapped[0]), in_order(side, own[2], swapped[2])
     dqs = []
     for b in range(2):
         dq, dkp[b] = block_grads_early(
@@ -289,9 +309,9 @@
     own[...] = after
 
 
-def kernel_grads(count, place, side, got, gives, matrix, own, lg, k, swapped, less, give, start,
-                 err, back0, bk, dkp, mine, theirs, rows, bias):
-    ks = blocks_of(side, k[...], swapped[0])
+def kernel_grads(count, place, side, got, gives, matrix, own, lg, held, swapped, less, give,
+                 start, err, back0, bk, dkp, mine, theirs, message):
+    ks = in_order(side, held[0], swapped[0])
     _, row_after = chain_back(less_of(got), give_of(gives), place[0], count, total=False)
     end_grad = dot3(row_after, matrix[...]) + own[...]
     later = block_grads(
@@ -304,12 +324,35 @@
     for i in range(2):
         x, y = in_order(side, earlier[i], later[i])
         mine[i], theirs[i] = x.astype(BF16), y.astype(BF16)
-    odd = lax.broadcasted_iota(jnp.int32, (16, L), 0) % 2
-    rows[...] = jnp.where(odd == 0, earlier[2], later[2]).astype(BF16)
-    part = jnp.sum(earlier[2] + later[2], axis=1, keepdims=True)
-    row = lax.broadcasted_iota(jnp.int32, (8, 2 * D), 0)
-    col = lax.broadcasted_iota(jnp.int32, (8, 2 * D), 1)
-    bias[...] = jnp.where((row == 0) & (col == side[0]), part, 0.0)
+    odd = lax.broadcasted_iota(jnp.int32, (192, L), 0) % 2
+    message[...] = jnp.where(odd == 0, earlier[2], later[2])
+
+
+def kernel_weight(pairs, place, side, slot, got, hidden, total, grads, held, done):
+    copies = [
+        pltpu.make_async_copy(hidden.at[pl.ds(2 * j, 2)], held.at[pl.ds(2 * j, 2)], done.at[j])
+        for j in range(pairs)
+    ]
+    for copy in copies:
+        copy.start()
+    weight = jnp.zeros((16, 2 * D), F32)
+    bias = jnp.zeros((16, 1), F32)
+    for j in range(pairs):
+        copies[j].wait()
+        for b in range(2):
+            rows = got[pl.ds(32 * j + b, 16, stride=2), :]
+            weight = weight + dot1(rows.astype(BF16), held[2 * j + b].astype(BF16))
+            bias = bias + jnp.sum(rows, axis=1, keepdims=True)
+    row = lax.broadcasted_iota(jnp.int32, (16, 2 * D), 0)
+    col = lax.broadcasted_iota(jnp.int32, (16, 2 * D), 1)
+    line = jnp.sum(
+        jnp.where((row - 2 * slot[0] == col) & (col < 2), bias, 0.0), axis=0, keepdims=True
+    )
+    for i in range(total.shape[0]):
+        total[i, 0:16] = weight
+        total[i, 16:24] = jnp.broadcast_to(line, (8, 2 * D))
+    here = [got[pl.ds(32 * place[0] + b, 16, stride=2), :] for b in range(2)]
+    grads[...] = in_order(side, *here)[0].astype(BF16)
 
 
 VM = pl.BlockSpec(memory_space=pltpu.VMEM)
@@ -317,14 +360,14 @@
 
 
 def call(body, outs, *args, flops=1e8):
-    specs = [SM if a.dtype == jnp.int32 else VM for a in args]
+    specs = [SM if a.ndim == 1 else VM for a in args]
     total = sum(a.size * a.dtype.itemsize for a in args)
     return pl.pallas_call(
         body,
         out_shape=[jax.ShapeDtypeStruct(s, t) for s, t in outs],
         in_specs=specs,
         out_specs=[VM] * len(outs),
-        compiler_params=pltpu.CompilerParams(vmem_limit_bytes=40 * 2**20),
+        compiler_params=pltpu.CompilerParams(vmem_limit_bytes=16 * 2**20),
         cost_estimate=pl.CostEstimate(flops=int(flops), bytes_accessed=total, transcendentals=0),
     )(*args)
 
@@ -353,7 +396,6 @@
 HALF = ((D, D), F32)
 PAIR = ((2, D, D), F32)
 PAIRB = ((2, L, D), BF16)
-ALL = ("head", "zl")
 
 
 def per_device(hidden, beta_weight, beta_bias, queries, keys, values, cotangent):
@@ -363,64 +405,79 @@
     at_z = lax.axis_index("zh").astype(jnp.int32).reshape(1)
     at_s = side.reshape(1)
 
-    swapped = swap(
-        jnp.stack([
-            jnp.where(side == 0, a[:, D:], a[:, :D])
-            for a in (keys, values, queries, cotangent)
-        ])
-    )
-    part = lax.dot_general(
-        beta_weight, hidden, (((0,), (1,)), ((), ())), preferred_element_type=F32
-    )
-    part = lax.all_to_all(part, ALL, 0, 0, tiled=True)
-    bias = jnp.where(side == 0, beta_bias[0], beta_bias[1])
-    logits = jnp.sum(part.reshape(8, 2, L), axis=0) + bias
-
-    send1, less, gain, inv, sk, sv, bk = call(
-        kernel_prepare, [((2 * D + 16, D), F32)] + [PAIR] * 6,
-        at_s, logits, keys, values, swapped,
+    at_h = lax.axis_index("head").astype(jnp.int32).reshape(1)
+
+    four = jax.ShapeDtypeStruct((4, L, D), BF16)
+    part, held, theirs = pl.pallas_call(
+        kernel_first,
+        out_shape=[jax.ShapeDtypeStruct((16, L), F32), four, four],
+        in_specs=[SM] * 2 + [pl.BlockSpec(memory_space=pl.ANY)] * 7,
+        out_specs=[VM] * 3,
+        scratch_shapes=[
+            pltpu.SMEM((2,), F32),
+            pltpu.VMEM((16, 2 * D), BF16),
+            pltpu.VMEM((5, L, 2 * D), BF16),
+            pltpu.SemaphoreType.DMA((7,)),
+        ],
+        compiler_params=pltpu.CompilerParams(vmem_limit_bytes=60 * 2**20),
+        cost_estimate=pl.CostEstimate(flops=10**7, bytes_accessed=10**6, transcendentals=0),
+    )(at_s, at_h, beta_bias, beta_weight.T, hidden, keys, values, queries, cotangent)
+    part = lax.all_to_all(part, ("head", "zl"), 0, 0, tiled=True)
+    swapped = swap(theirs)
+
+    send1, logits, less, gain, inv, sk, sv, bk = call(
+        kernel_prepare, [((2 * D + 16, D), F32), ((2, L), F32)] + [PAIR] * 6,
+        at_s, part, held, swapped,
     )
     got1 = spread(send1, "zh")
     send2, own1 = call(
         functools.partial(kernel_row_forward, pairs),
         [((2 * D + 16, D), F32), ((2 * D, D), F32)], at_z, got1,
     )
+    send2, hidden_f = lax.optimization_barrier((send2, hidden))
+    hidden_row = lax.all_gather(hidden_f.astype(F32), ("zh", "zl"))
     got2 = spread(send2, "y")
     (matrix,) = call(functools.partial(kernel_row_matrix, pairs), [HALF], at_z, got1)
     out, start, err, draw, back0, give, send3 = call(
         functools.partial(kernel_outputs, rows),
         [PAIRB] + [PAIR] * 4 + [HALF, ((D + 16, D), F32)],
-        at_y, at_s, got2, own1, logits, keys, queries, cotangent, swapped,
-        less, gain, inv, sk, sv,
+        at_y, at_s, got2, own1, logits, held, swapped, less, gain, inv, sk, sv,
     )
     got3 = spread(send3, "zh")
     mine, theirs, dkp = call(
         kernel_early, [PAIRB, PAIRB, PAIR],
-        at_s, logits, keys, queries, swapped, start, err, draw, out,
+        at_s, logits, held, swapped, start, err, draw, out,
     )
     send4, own2 = call(
         functools.partial(kernel_row_back, pairs), [((D + 16, D), F32), HALF], at_z, got1, got3
     )
     got4 = spread(send4, "y")
     theirs = swap(theirs)
-    mine_kv, theirs_kv, grad_rows, bias_part = call(
-        functools.partial(kernel_grads, rows),
-        [PAIRB, PAIRB, ((16, L), BF16), ((8, 2 * D), F32)],
-        at_y, at_s, got2, got4, matrix, own2, logits, keys, swapped, less, give, start, err,
+    mine_kv, theirs_kv, message = call(
+        functools.partial(kernel_grads, rows), [PAIRB, PAIRB, ((192, L), F32)],
+        at_y, at_s, got2, got4, matrix, own2, logits, held, swapped, less, give, start, err,
         back0, bk, dkp,
     )
 
-    all_grads = lax.all_to_all(grad_rows, ALL, 0, 0, tiled=True)
-    all_grads, theirs_kv = lax.optimization_barrier((all_grads, theirs_kv))
-    weight_part = lax.dot_general(
-        all_grads, hidden, (((1,), (0,)), ((), ())), preferred_element_type=F32
-    )
-    total = jnp.concatenate([weight_part, bias_part], axis=0)
-    total = jnp.sum(copies(total, ("zh", "zl")), axis=0)
-    total = jnp.sum(copies(total, "y"), axis=0)
+    message = lax.all_to_all(message.reshape(96, 2, L), ("zh", "head", "zl"), 0, 0)
+    message, theirs_kv = lax.optimization_barrier((message, theirs_kv))
+    total, grads = pl.pallas_call(
+        functools.partial(kernel_weight, pairs),
+        out_shape=[
+            jax.ShapeDtypeStruct((rows, 24, 2 * D), F32), jax.ShapeDtypeStruct((16, L), BF16)
+        ],
+        in_specs=[SM] * 3 + [VM, pl.BlockSpec(memory_space=pl.ANY)],
+        out_specs=[VM] * 2,
+        scratch_shapes=[
+            pltpu.VMEM((2 * pairs, L, 2 * D), F32), pltpu.SemaphoreType.DMA((pairs,))
+        ],
+        compiler_params=pltpu.CompilerParams(vmem_limit_bytes=60 * 2**20),
+        cost_estimate=pl.CostEstimate(flops=10**8, bytes_accessed=10**6, transcendentals=0),
+    )(at_z, at_s, at_h, message.reshape(192, L), hidden_row)
+    total = jnp.sum(lax.all_to_all(total, "y", 0, 0), axis=0)
     theirs_kv = swap(theirs_kv)
     d_hidden = lax.dot_general(
-        all_grads, beta_weight, (((0,), (1,)), ((), ())), preferred_element_type=F32
+        grads, beta_weight, (((0,), (1,)), ((), ())), preferred_element_type=F32
     )
     out, dq = [joined(side, mine[i], theirs[i]) for i in range(2)]
     dk, dv = [joined(side, mine_kv[i], theirs_kv[i]) for i in range(2)]

time: 183 us -> 190 us (1.038)
  the two profiles are of different devices: /device:TPU:2 before, /device:TPU:7 now
where the time goes in v3:
time: 190 us; the launch traced here: 189 us
  waiting for transfers between devices  57.4 us (30%)
  blocking collectives  42.3 us (22%)
  starting transfers between devices  41 us (22%)
  Pallas kernels  21 us (11%)
  between operations  14.4 us (8%)
  local copies, waits for them, and re-layouts  6.9 us (4%)
  other arithmetic  4.36 us (2%)
    all_to_all x3, waiting for transfers between devices, copies(): lax.all_to_all(jnp.broadcast_to(x[None], (count,) + x.shape), axis, 0, 0)  37.4 us
    all_to_all x1, blocking collectives, copies(): lax.all_to_all(jnp.broadcast_to(x[None], (count,) + x.shape), axis, 0, 0)  27.6 us
    all_to_all x3, starting transfers between devices, copies(): lax.all_to_all(jnp.broadcast_to(x[None], (count,) + x.shape), axis, 0, 0)  19.3 us
    pallas_call x7, Pallas kernels, call(): pl.pallas_call(body, out_shape=[jax.ShapeDtypeStruct(s, t) for s, t in ou...  16 us
    all_to_all x1, blocking collectives, per_device(): part = lax.all_to_all(part, ('head', 'zl'), 0, 0, tiled=True)  14.7 us
    all_to_all x1, waiting for transfers between devices, per_device(): lax.all_to_all(message.reshape(96, 2, L), ('zh', 'head', 'zl'), 0, 0)  11.2 us
    all_to_all x1, starting transfers between devices, per_device(): lax.all_to_all(message.reshape(96, 2, L), ('zh', 'head', 'zl'), 0, 0)  9.6 us
    all_to_all x1, waiting for transfers between devices, per_device(): total = jnp.sum(lax.all_to_all(total, 'y', 0, 0), axis=0)  8.69 us
  transfers between devices with their start and end apart: 9, of which 5 were waited for; matrix products, arithmetic and copies ran while one was open for 4% of the time, Pallas kernels for 7%

profile of v3, /device:TPU:7, one launch (start us, length us, event | category | flops | bytes accessed | tf_op | source)
XLA Modules:
  0.0 188.8 jit_solution(13547472516759954804)
XLA Ops:
  7.2 1.8 shard_map.126
  9.0 4.0 %collective-permute-start = (bf16[4,128,128]{2,1,0:T(8,128)(2,1)}, bf16[4,128,128]{2,1,0:T(8,128)(2,1)S(1)}, u32[]{:S(2)}, u32[]{:S(2)}) collective-permute-start(bf16[4,128,128]{2,1,0:T(8,128)(2,1)} %get-tuple-element.43), channel_id=1, source_target_pairs={{0,8},{8,0},{1,9},{9,1},{2,10},{10,2},{3,11},{11,3},{4,12},{12,4},... | collective-permute-start | bytes 393224 | tf_op jit(solution)/shard_map/ppermute | solution.py:385
  13.0 14.7 %all_to_all.41 = f32[16,1,128]{2,1,0:T(1,128)S(1)} all-to-all(f32[16,1,128]{2,1,0:T(1,128)} %bitcast.38), channel_id=1, replica_groups=mesh['y'=8,'zh'=6,'zl'=2,'head'=8] {'head','zl'}, dimensions={0} | all-to-all | bytes 16384 | tf_op jit(solution)/shard_map/all_to_all | solution.py:425
  27.7 0.0 collective-permute-done.swapped
  27.7 0.0 copy-start
  27.7 0.9 copy-done
  28.7 5.5 %shard_map.127 = (f32[272,128]{1,0:T(8,128)S(1)}, f32[2,128]{1,0:T(2,128)S(1)}, f32[2,128,128]{2,1,0:T(8,128)S(1)}, f32[2,128,128]{2,1,0:T(8,128)S(1)}, f32[2,12...) custom-call(s32[1]{0:T(128)} %bitcast.side, ...), custom_call_target="tpu_custom_call" | custom-call | flops 100000000 | bytes 270340 | tf_op jit(solution)/shard_map/pallas_call | solution.py:365
  34.1 0.8 broadcast_in_dim.8
  35.0 0.0 copy-start.9
  35.0 8.4 %all-to-all-start.1 = ((f16[6,272,128]{2,1,0:T(8,128)(2,1)}), f16[6,272,128]{2,1,0:T(8,128)(2,1)S(1)}, u32[]{:S(2)}, u32[]{:S(2)}) async-start(f16[6,272,128]{2,1,0:T(8,128)(2,1)} %broadcast_in_dim.8), calls=%async_computation.1 | async-start | bytes 835584 | tf_op jit(solution)/shard_map/all_to_all | solution.py:377
  43.4 0.0 all-gather.3.cloned.1.call-start
  43.4 16.4 %all-to-all-done.1 = f16[6,272,128]{2,1,0:T(8,128)(2,1)S(1)} async-done(((f16[6,272,128]{2,1,0:T(8,128)(2,1)}), f16[6,272,128]{2,1,0:T(8,128)(2,1)S(1)}, u32[]{:S(2)}, u32[]{:S(2)}) %all-to-all-start.1) | async-done | bytes 417824 | tf_op jit(solution)/shard_map/all_to_all | solution.py:377
  59.8 0.1 convert_element_type.29.got
  59.9 1.1 shard_map.128
  61.0 0.0 copy-start.2
  61.0 0.0 copy-done.9
  61.0 0.7 all_gather.12
  61.7 0.0 all-gather.3.cloned.1.call-update
  61.7 0.0 copy-start.1
  61.7 0.9 broadcast_in_dim.9
  62.6 6.8 %all-to-all-start.2 = ((f16[8,272,128]{2,1,0:T(8,128)(2,1)}), f16[8,272,128]{2,1,0:T(8,128)(2,1)}, u32[]{:S(2)}, u32[]{:S(2)}) async-start(f16[8,272,128]{2,1,0:T(8,128)(2,1)} %broadcast_in_dim.9), calls=%async_computation.2 | async-start | bytes 1114112 | tf_op jit(solution)/shard_map/all_to_all | solution.py:377
  69.4 15.4 %all-to-all-done.2 = f16[8,272,128]{2,1,0:T(8,128)(2,1)} async-done(((f16[8,272,128]{2,1,0:T(8,128)(2,1)}), f16[8,272,128]{2,1,0:T(8,128)(2,1)}, u32[]{:S(2)}, u32[]{:S(2)}) %all-to-all-start.2) | async-done | bytes 557088 | tf_op jit(solution)/shard_map/all_to_all | solution.py:377
  84.8 1.1 convert_element_type.31.got
  86.0 0.0 copy-done.2
  86.0 0.0 copy-done.1
  86.0 0.0 copy-start.3
  86.0 0.9 copy-done.3
  86.9 3.5 %shard_map.129 = (bf16[2,128,128]{2,1,0:T(8,128)(2,1)S(1)}, f32[2,128,128]{2,1,0:T(8,128)S(1)}, f32[2,128,128]{2,1,0:T(8,128)S(1)}, f32[2,128,128]{2,1,0:T(8,128...) custom-call(s32[1]{0:T(128)} %bitcast.6.place, s32[1]{0:T(128)} %bitcast.side, ...), custom_call_target="tpu_custom_call" | custom-call | flops 100000000 | bytes 2163720 | tf_op jit(solution)/shard_map/pallas_call | solution.py:365
  90.4 0.0 copy-start.4
  90.4 0.0 copy-start.6
  90.5 0.6 copy-done.4
  91.0 27.6 %all_to_all.42 = f16[6,144,128]{2,1,0:T(8,128)(2,1)S(1)} all-to-all(f16[6,144,128]{2,1,0:T(8,128)(2,1)S(1)} %broadcast_in_dim.10), channel_id=1, replica_groups=mesh['y'=8,'zh'=6,'zl'=2,'head'=8] {'zh'}, dimensions={0} | all-to-all | bytes 442368 | tf_op jit(solution)/shard_map/all_to_all | solution.py:377
  118.7 0.0 copy-start.5
  118.7 1.1 shard_map.131
  119.8 0.8 broadcast_in_dim.11
  120.6 0.0 copy-done.6
  120.6 4.1 %all-to-all-start.4 = ((f16[8,144,128]{2,1,0:T(8,128)(2,1)}), f16[8,144,128]{2,1,0:T(8,128)(2,1)}, u32[]{:S(2)}, u32[]{:S(2)}) async-start(f16[8,144,128]{2,1,0:T(8,128)(2,1)} %broadcast_in_dim.11), calls=%async_computation.4 | async-start | bytes 589824 | tf_op jit(solution)/shard_map/all_to_all | solution.py:377
  124.6 1.0 shard_map.132.matrix
  125.6 0.0 copy-done.5
  125.6 0.0 copy-start.7
  125.6 0.8 copy-done.7
  126.5 0.7 shard_map.130
  127.2 2.4 %collective-permute-start.1 = (bf16[2,128,128]{2,1,0:T(8,128)(2,1)S(1)}, bf16[2,128,128]{2,1,0:T(8,128)(2,1)S(1)}, u32[]{:S(2)}, u32[]{:S(2)}) collective-permute-start(bf16[2,128,128]{2,1,0:T(8,128)(2,1)S(1)} %get-tuple-element.59), channel_id=1, source_target_pairs={{0,8},{8,0},{1,9},{9,1},{2,10},{10,2},{3,11},{11,3},{4,12},{12,4},... | collective-permute-start | bytes 196616 | tf_op jit(solution)/shard_map/ppermute | solution.py:385
  129.7 5.6 %all-to-all-done.4 = f16[8,144,128]{2,1,0:T(8,128)(2,1)} async-done(((f16[8,144,128]{2,1,0:T(8,128)(2,1)}), f16[8,144,128]{2,1,0:T(8,128)(2,1)}, u32[]{:S(2)}, u32[]{:S(2)}) %all-to-all-start.4) | async-done | bytes 294944 | tf_op jit(solution)/shard_map/all_to_all | solution.py:377
  135.2 1.0 convert_element_type.35.gives
  136.2 3.2 %shard_map.133 = (bf16[2,128,128]{2,1,0:T(8,128)(2,1)S(1)}, bf16[2,128,128]{2,1,0:T(8,128)(2,1)S(1)}, f32[192,128]{1,0:T(8,128)}) custom-call(s32[1]{0:T(128)} %bitcast.6.place, s32[1]{0:T(128)} %bitcast.side, f32[8,272,128]{2,1,0:T(8,128)S(1)} %convert_element_type.31.got, f32[8,144,128]{2,1,0:T(8,128)S(1)} %convert_element_type.35.gives, ...), custom_call_target="tpu_custom_call" | custom-call | flops 100000000 | bytes 2950152 | tf_op jit(solution)/shard_map/pallas_call | solution.py:365
  139.4 0.0 copy-start.10
  139.4 9.6 %all-to-all-start.5 = ((f32[96,2,128]{2,1,0:T(2,128)}), f32[96,2,128]{2,1,0:T(2,128)S(1)}, u32[]{:S(2)}, u32[]{:S(2)}) async-start(f32[96,2,128]{2,1,0:T(2,128)} %bitcast.13), calls=%async_computation.5 | async-start | bytes 196608 | tf_op jit(solution)/shard_map/all_to_all | solution.py:462
  149.0 0.0 collective-permute-done.1
  149.0 0.7 maximum_select_fusion
  149.7 11.2 %all-to-all-done.5 = f32[96,2,128]{2,1,0:T(2,128)S(1)} async-done(((f32[96,2,128]{2,1,0:T(2,128)}), f32[96,2,128]{2,1,0:T(2,128)S(1)}, u32[]{:S(2)}, u32[]{:S(2)}) %all-to-all-start.5) | async-done | bytes 98336 | tf_op jit(solution)/shard_map/all_to_all | solution.py:462
  161.0 0.0 copy-start.8
  161.0 2.2 %collective-permute-start.2 = (bf16[2,128,128]{2,1,0:T(8,128)(2,1)S(1)}, bf16[2,128,128]{2,1,0:T(8,128)(2,1)S(1)}, u32[]{:S(2)}, u32[]{:S(2)}) collective-permute-start(bf16[2,128,128]{2,1,0:T(8,128)(2,1)S(1)} %get-tuple-element.70), channel_id=1, source_target_pairs={{0,8},{8,0},{1,9},{9,1},{2,10},{10,2},{3,11},{11,3},{4,12},{12,4},... | collective-permute-start | bytes 196616 | tf_op jit(solution)/shard_map/ppermute | solution.py:385
  163.2 0.0 all-gather.3.cloned.1.call-done
  163.3 0.0 copy-done.8
  163.3 3.2 %shard_map.134 = (f32[8,24,256]{2,1,0:T(8,128)}, bf16[16,128]{1,0:T(8,128)(2,1)}) custom-call(s32[1]{0:T(128)} %bitcast.7.place, s32[1]{0:T(128)} %bitcast.side, s32[1]{0:T(128)} %bitcast.1.slot, f32[192,128]{1,0:T(8,128)} %bitcast.36, f32[12,128,256]{2,1,0:T(8,128)} %bitcast.35), custom_call_target="tpu_custom_call" | custom-call | flops 100000000 | bytes 1000000 | tf_op jit(solution)/shard_map/pallas_call | solution.py:464
  166.5 3.4 %all-to-all-start.6 = ((f32[8,24,256]{2,1,0:T(8,128)}), f32[8,24,256]{2,1,0:T(8,128)S(1)}, u32[]{:S(2)}, u32[]{:S(2)}) async-start(f32[8,24,256]{2,1,0:T(8,128)} %get-tuple-element.74), calls=%async_computation.6 | async-start | bytes 393216 | tf_op jit(solution)/shard_map/all_to_all | solution.py:477
  169.9 0.0 collective-permute-done.2
  169.9 0.7 maximum_select_fusion.2
  170.6 0.0 copy-done.10
  170.6 1.5 convolution_convert_fusion
  172.1 8.7 %all-to-all-done.6 = f32[8,24,256]{2,1,0:T(8,128)S(1)} async-done(((f32[8,24,256]{2,1,0:T(8,128)}), f32[8,24,256]{2,1,0:T(8,128)S(1)}, u32[]{:S(2)}, u32[]{:S(2)}) %all-to-all-start.6) | async-done | bytes 196640 | tf_op jit(solution)/shard_map/all_to_all | solution.py:477
  180.8 0.6 slice_bitcast_fusion.8
  181.4 0.5 slice_bitcast_fusion.9
  (11 shorter events, 0.2 us)
Async XLA Ops:
  9.0 18.7 %collective-permute-start = (bf16[4,128,128]{2,1,0:T(8,128)(2,1)}, bf16[4,128,128]{2,1,0:T(8,128)(2,1)S(1)}, u32[]{:S(2)}, u32[]{:S(2)}) collective-permute-start(bf16[4,128,128]{2,1,0:T(8,128)(2,1)} %get-tuple-element.43), channel_id=1, source_target_pairs={{0,8},{8,0},{1,9},{9,1},{2,10},{10,2},{3,11},{11,3},{4,12},{12,4},... | collective-permute-start | bytes 393224 | tf_op jit(solution)/shard_map/ppermute | solution.py:385
  27.7 0.9 copy-start
  35.0 26.0 %copy-start.9 = (bf16[128,256]{1,0:T(8,128)(2,1)S(1)}, bf16[128,256]{1,0:T(8,128)(2,1)}, u32[]{:S(2)}) copy-start(bf16[128,256]{1,0:T(8,128)(2,1)} %hidden.1) | copy-start | bytes 196612
  35.0 24.9 %all-to-all-start.1 = ((f16[6,272,128]{2,1,0:T(8,128)(2,1)}), f16[6,272,128]{2,1,0:T(8,128)(2,1)S(1)}, u32[]{:S(2)}, u32[]{:S(2)}) async-start(f16[6,272,128]{2,1,0:T(8,128)(2,1)} %broadcast_in_dim.8), calls=%async_computation.1 | async-start | bytes 835584 | tf_op jit(solution)/shard_map/all_to_all | solution.py:377
  43.4 119.9 %all-gather.3.cloned.1.call-start = ((), (), s32[]{:S(2)}) async-start(), calls=%async_computation.7 | async-start | bytes 1703936 | tf_op jit(solution)/shard_map/all_gather | solution.py:438
  61.0 25.0 %copy-start.2 = (f32[256,128]{1,0:T(8,128)}, f32[256,128]{1,0:T(8,128)S(1)}, u32[]{:S(2)}) copy-start(f32[256,128]{1,0:T(8,128)S(1)} %get-tuple-element.48.own) | copy-start | bytes 393220
  61.7 24.3 %copy-start.1 = (bf16[4,128,128]{2,1,0:T(8,128)(2,1)S(1)}, bf16[4,128,128]{2,1,0:T(8,128)(2,1)}, u32[]{:S(2)}) copy-start(bf16[4,128,128]{2,1,0:T(8,128)(2,1)} %get-tuple-element.42.mine.own.held) | copy-start | bytes 393220
  62.6 22.2 %all-to-all-start.2 = ((f16[8,272,128]{2,1,0:T(8,128)(2,1)}), f16[8,272,128]{2,1,0:T(8,128)(2,1)}, u32[]{:S(2)}, u32[]{:S(2)}) async-start(f16[8,272,128]{2,1,0:T(8,128)(2,1)} %broadcast_in_dim.9), calls=%async_computation.2 | async-start | bytes 1114112 | tf_op jit(solution)/shard_map/all_to_all | solution.py:377
  86.0 0.9 copy-start.3
  90.4 0.7 copy-start.4
  90.4 30.2 %copy-start.6 = (bf16[2,128,128]{2,1,0:T(8,128)(2,1)}, bf16[2,128,128]{2,1,0:T(8,128)(2,1)S(1)}, u32[]{:S(2)}) copy-start(bf16[2,128,128]{2,1,0:T(8,128)(2,1)S(1)} %get-tuple-element.57.out) | copy-start | bytes 196612
  118.7 6.9 %copy-start.5 = (f32[2,128,128]{2,1,0:T(8,128)S(1)}, f32[2,128,128]{2,1,0:T(8,128)}, u32[]{:S(2)}) copy-start(f32[2,128,128]{2,1,0:T(8,128)} %copy-done.4) | copy-start | bytes 393220
  120.6 14.7 %all-to-all-start.4 = ((f16[8,144,128]{2,1,0:T(8,128)(2,1)}), f16[8,144,128]{2,1,0:T(8,128)(2,1)}, u32[]{:S(2)}, u32[]{:S(2)}) async-start(f16[8,144,128]{2,1,0:T(8,128)(2,1)} %broadcast_in_dim.11), calls=%async_computation.4 | async-start | bytes 589824 | tf_op jit(solution)/shard_map/all_to_all | solution.py:377
  125.6 0.8 copy-start.7
  127.2 21.8 %collective-permute-start.1 = (bf16[2,128,128]{2,1,0:T(8,128)(2,1)S(1)}, bf16[2,128,128]{2,1,0:T(8,128)(2,1)S(1)}, u32[]{:S(2)}, u32[]{:S(2)}) collective-permute-start(bf16[2,128,128]{2,1,0:T(8,128)(2,1)S(1)} %get-tuple-element.59), channel_id=1, source_target_pairs={{0,8},{8,0},{1,9},{9,1},{2,10},{10,2},{3,11},{11,3},{4,12},{12,4},... | collective-permute-start | bytes 196616 | tf_op jit(solution)/shard_map/ppermute | solution.py:385
  139.4 31.2 %copy-start.10 = (bf16[256,16]{0,1:T(8,128)(2,1)S(1)}, bf16[256,16]{0,1:T(8,128)(2,1)}, u32[]{:S(2)}) copy-start(bf16[256,16]{0,1:T(8,128)(2,1)} %param.8) | copy-start | bytes 24580
  139.4 21.6 %all-to-all-start.5 = ((f32[96,2,128]{2,1,0:T(2,128)}), f32[96,2,128]{2,1,0:T(2,128)S(1)}, u32[]{:S(2)}, u32[]{:S(2)}) async-start(f32[96,2,128]{2,1,0:T(2,128)} %bitcast.13), calls=%async_computation.5 | async-start | bytes 196608 | tf_op jit(solution)/shard_map/all_to_all | solution.py:462
  161.0 2.3 %copy-start.8 = (f32[96,2,128]{2,1,0:T(2,128)}, f32[96,2,128]{2,1,0:T(2,128)S(1)}, u32[]{:S(2)}) copy-start(f32[96,2,128]{2,1,0:T(2,128)S(1)} %all-to-all-done.5) | copy-start | bytes 294916
  161.0 8.9 %collective-permute-start.2 = (bf16[2,128,128]{2,1,0:T(8,128)(2,1)S(1)}, bf16[2,128,128]{2,1,0:T(8,128)(2,1)S(1)}, u32[]{:S(2)}, u32[]{:S(2)}) collective-permute-start(bf16[2,128,128]{2,1,0:T(8,128)(2,1)S(1)} %get-tuple-element.70), channel_id=1, source_target_pairs={{0,8},{8,0},{1,9},{9,1},{2,10},{10,2},{3,11},{11,3},{4,12},{12,4},... | collective-permute-start | bytes 196616 | tf_op jit(solution)/shard_map/ppermute | solution.py:385
  166.5 14.3 %all-to-all-start.6 = ((f32[8,24,256]{2,1,0:T(8,128)}), f32[8,24,256]{2,1,0:T(8,128)S(1)}, u32[]{:S(2)}, u32[]{:S(2)}) async-start(f32[8,24,256]{2,1,0:T(8,128)} %get-tuple-element.74), calls=%async_computation.6 | async-start | bytes 393216 | tf_op jit(solution)/shard_map/all_to_all | solution.py:477
Sparse Core Ops, SparseCore 0:
  61.8 55.9 all-gather.2

commit v4 on v3

--- a/solution.py
+++ b/solution.py
@@ -324,25 +324,16 @@
     for i in range(2):
         x, y = in_order(side, earlier[i], later[i])
         mine[i], theirs[i] = x.astype(BF16), y.astype(BF16)
-    odd = lax.broadcasted_iota(jnp.int32, (192, L), 0) % 2
+    odd = lax.broadcasted_iota(jnp.int32, (32, L), 0) % 2
     message[...] = jnp.where(odd == 0, earlier[2], later[2])
 
 
-def kernel_weight(pairs, place, side, slot, got, hidden, total, grads, held, done):
-    copies = [
-        pltpu.make_async_copy(hidden.at[pl.ds(2 * j, 2)], held.at[pl.ds(2 * j, 2)], done.at[j])
-        for j in range(pairs)
-    ]
-    for copy in copies:
-        copy.start()
-    weight = jnp.zeros((16, 2 * D), F32)
-    bias = jnp.zeros((16, 1), F32)
-    for j in range(pairs):
-        copies[j].wait()
-        for b in range(2):
-            rows = got[pl.ds(32 * j + b, 16, stride=2), :]
-            weight = weight + dot1(rows.astype(BF16), held[2 * j + b].astype(BF16))
-            bias = bias + jnp.sum(rows, axis=1, keepdims=True)
+def kernel_weight(side, slot, got, hidden, swapped, total, grads):
+    rows = [got[pl.ds(b, 16, stride=2), :] for b in range(2)]
+    here, there = in_order(side, *rows)
+    grads[...] = here.astype(BF16)
+    weight = dot1(here.astype(BF16), hidden[...]) + dot1(there.astype(BF16), swapped[...])
+    bias = jnp.sum(rows[0] + rows[1], axis=1, keepdims=True)
     row = lax.broadcasted_iota(jnp.int32, (16, 2 * D), 0)
     col = lax.broadcasted_iota(jnp.int32, (16, 2 * D), 1)
     line = jnp.sum(
@@ -351,8 +342,6 @@
     for i in range(total.shape[0]):
         total[i, 0:16] = weight
         total[i, 16:24] = jnp.broadcast_to(line, (8, 2 * D))
-    here = [got[pl.ds(32 * place[0] + b, 16, stride=2), :] for b in range(2)]
-    grads[...] = in_order(side, *here)[0].astype(BF16)
 
 
 VM = pl.BlockSpec(memory_space=pltpu.VMEM)
@@ -434,9 +423,9 @@
         functools.partial(kernel_row_forward, pairs),
         [((2 * D + 16, D), F32), ((2 * D, D), F32)], at_z, got1,
     )
-    send2, hidden_f = lax.optimization_barrier((send2, hidden))
-    hidden_row = lax.all_gather(hidden_f.astype(F32), ("zh", "zl"))
-    got2 = spread(send2, "y")
+    send2, hidden_s = lax.optimization_barrier((send2, hidden))
+    hidden_s = swap(hidden_s)
+    got2, hidden_s = lax.optimization_barrier((spread(send2, "y"), hidden_s))
     (matrix,) = call(functools.partial(kernel_row_matrix, pairs), [HALF], at_z, got1)
     out, start, err, draw, back0, give, send3 = call(
         functools.partial(kernel_outputs, rows),
@@ -454,27 +443,19 @@
     got4 = spread(send4, "y")
     theirs = swap(theirs)
     mine_kv, theirs_kv, message = call(
-        functools.partial(kernel_grads, rows), [PAIRB, PAIRB, ((192, L), F32)],
+        functools.partial(kernel_grads, rows), [PAIRB, PAIRB, ((32, L), F32)],
         at_y, at_s, got2, got4, matrix, own2, logits, held, swapped, less, give, start, err,
         back0, bk, dkp,
     )
 
-    message = lax.all_to_all(message.reshape(96, 2, L), ("zh", "head", "zl"), 0, 0)
-    message, theirs_kv = lax.optimization_barrier((message, theirs_kv))
-    total, grads = pl.pallas_call(
-        functools.partial(kernel_weight, pairs),
-        out_shape=[
-            jax.ShapeDtypeStruct((rows, 24, 2 * D), F32), jax.ShapeDtypeStruct((16, L), BF16)
-        ],
-        in_specs=[SM] * 3 + [VM, pl.BlockSpec(memory_space=pl.ANY)],
-        out_specs=[VM] * 2,
-        scratch_shapes=[
-            pltpu.VMEM((2 * pairs, L, 2 * D), F32), pltpu.SemaphoreType.DMA((pairs,))
-        ],
-        compiler_params=pltpu.CompilerParams(vmem_limit_bytes=60 * 2**20),
-        cost_estimate=pl.CostEstimate(flops=10**8, bytes_accessed=10**6, transcendentals=0),
-    )(at_z, at_s, at_h, message.reshape(192, L), hidden_row)
-    total = jnp.sum(lax.all_to_all(total, "y", 0, 0), axis=0)
+    message = lax.all_to_all(message.reshape(16, 2, L), ("head", "zl"), 0, 0)
+    total, grads = call(
+        kernel_weight, [((pairs, 24, 2 * D), F32), ((16, L), BF16)],
+        at_s, at_h, message.reshape(32, L), hidden, hidden_s,
+    )
+    total, theirs_kv = lax.optimization_barrier((total, theirs_kv))
+    total = jnp.sum(lax.all_to_all(total, "zh", 0, 0), axis=0)
+    total = jnp.sum(copies(total, "y"), axis=0)
     theirs_kv = swap(theirs_kv)
     d_hidden = lax.dot_general(
         grads, beta_weight, (((0,), (1,)), ((), ())), preferred_element_type=F32

time: 190 us -> 175 us (0.921)
  the two profiles are of different devices: /device:TPU:7 before, /device:TPU:64 now
where the time goes in v4:
time: 175 us; the launch traced here: 174 us
  waiting for transfers between devices  56.8 us (32%)
  starting transfers between devices  51.7 us (30%)
  blocking collectives  34.4 us (20%)
  Pallas kernels  18.5 us (11%)
  local copies, waits for them, and re-layouts  7.4 us (4%)
  other arithmetic  3.67 us (2%)
    all_to_all x4, waiting for transfers between devices, copies(): lax.all_to_all(jnp.broadcast_to(x[None], (count,) + x.shape), axis, 0, 0)  42.6 us
    all_to_all x1, blocking collectives, copies(): lax.all_to_all(jnp.broadcast_to(x[None], (count,) + x.shape), axis, 0, 0)  26.5 us
    all_to_all x4, starting transfers between devices, copies(): lax.all_to_all(jnp.broadcast_to(x[None], (count,) + x.shape), axis, 0, 0)  22.5 us
    ppermute x4, starting transfers between devices, swap(): return lax.ppermute(x, 'zl', [(0, 1), (1, 0)])  20.5 us
    pallas_call x8, Pallas kernels, call(): pl.pallas_call(body, out_shape=[jax.ShapeDtypeStruct(s, t) for s, t in ou...  16.7 us
    all_to_all x1, waiting for transfers between devices, per_device(): total = jnp.sum(lax.all_to_all(total, 'zh', 0, 0), axis=0)  9.41 us
    all_to_all x1, blocking collectives, per_device(): part = lax.all_to_all(part, ('head', 'zl'), 0, 0, tiled=True)  7.96 us
    all_to_all x1, waiting for transfers between devices, per_device(): message = lax.all_to_all(message.reshape(16, 2, L), ('head', 'zl'), 0, 0)  4.77 us
  transfers between devices with their start and end apart: 10, of which 6 were waited for; matrix products, arithmetic and copies ran while one was open for 3% of the time, Pallas kernels for 3%

profile of v4, /device:TPU:64, one launch (start us, length us, event | category | flops | bytes accessed | tf_op | source)
XLA Modules:
  0.0 174.3 jit_solution(18242585845532200672)
XLA Ops:
  0.6 1.8 %shard_map.126 = (f32[16,128]{1,0:T(8,128)}, bf16[4,128,128]{2,1,0:T(8,128)(2,1)}, bf16[4,128,128]{2,1,0:T(8,128)(2,1)}) custom-call(s32[1]{0:T(128)} %bitcast.side, s32[1]{0:T(128)} %bitcast.1.slot, f32[2]{0:T(128)} %bias.1, bf16[16,256]{1,0:T(8,128)(2,1)} %bitcast.35, bf16[128,256]{1,0:T(8,128)(2,1)} %hidden.3, bf16[128,256]{1,0:T(8,128)(2,1)} %k.1, ...), custom_call_target="tpu_custom_call" | custom-call | flops 10000000 | bytes 1000000 | tf_op jit(solution)/shard_map/pallas_call | solution.py:400
  2.5 10.6 %collective-permute-start = (bf16[4,128,128]{2,1,0:T(8,128)(2,1)}, bf16[4,128,128]{2,1,0:T(8,128)(2,1)S(1)}, u32[]{:S(2)}, u32[]{:S(2)}) collective-permute-start(bf16[4,128,128]{2,1,0:T(8,128)(2,1)} %get-tuple-element.45), channel_id=1, source_target_pairs={{0,8},{8,0},{1,9},{9,1},{2,10},{10,2},{3,11},{11,3},{4,12},{12,4},... | collective-permute-start | bytes 393224 | tf_op jit(solution)/shard_map/ppermute | solution.py:374
  13.0 8.0 %all_to_all.46 = f32[16,1,128]{2,1,0:T(1,128)S(1)} all-to-all(f32[16,1,128]{2,1,0:T(1,128)} %bitcast.36), channel_id=1, replica_groups=mesh['y'=8,'zh'=6,'zl'=2,'head'=8] {'head','zl'}, dimensions={0} | all-to-all | bytes 16384 | tf_op jit(solution)/shard_map/all_to_all | solution.py:414
  21.0 0.0 collective-permute-done.swapped
  21.0 0.9 copy-done
  21.9 5.5 %shard_map.127 = (f32[272,128]{1,0:T(8,128)S(1)}, f32[2,128]{1,0:T(2,128)S(1)}, f32[2,128,128]{2,1,0:T(8,128)S(1)}, f32[2,128,128]{2,1,0:T(8,128)S(1)}, f32[2,12...) custom-call(s32[1]{0:T(128)} %bitcast.side, ...), custom_call_target="tpu_custom_call" | custom-call | flops 100000000 | bytes 270340 | tf_op jit(solution)/shard_map/pallas_call | solution.py:354
  27.4 0.8 broadcast_in_dim.10
  28.2 8.0 %all-to-all-start.1 = ((f16[6,272,128]{2,1,0:T(8,128)(2,1)}), f16[6,272,128]{2,1,0:T(8,128)(2,1)S(1)}, u32[]{:S(2)}, u32[]{:S(2)}) async-start(f16[6,272,128]{2,1,0:T(8,128)(2,1)} %broadcast_in_dim.10), calls=%async_computation.1 | async-start | bytes 835584 | tf_op jit(solution)/shard_map/all_to_all | solution.py:366
  36.2 18.0 %all-to-all-done.1 = f16[6,272,128]{2,1,0:T(8,128)(2,1)S(1)} async-done(((f16[6,272,128]{2,1,0:T(8,128)(2,1)}), f16[6,272,128]{2,1,0:T(8,128)(2,1)S(1)}, u32[]{:S(2)}, u32[]{:S(2)}) %all-to-all-start.1) | async-done | bytes 417824 | tf_op jit(solution)/shard_map/all_to_all | solution.py:366
  54.2 0.1 convert_element_type.28.got
  54.2 1.1 shard_map.128
  55.3 0.0 copy-start.2
  55.3 0.0 copy-start.8
  55.3 0.9 broadcast_in_dim.11
  56.2 7.1 %all-to-all-start.2 = ((f16[8,272,128]{2,1,0:T(8,128)(2,1)}), f16[8,272,128]{2,1,0:T(8,128)(2,1)}, u32[]{:S(2)}, u32[]{:S(2)}) async-start(f16[8,272,128]{2,1,0:T(8,128)(2,1)} %broadcast_in_dim.11), calls=%async_computation.2 | async-start | bytes 1114112 | tf_op jit(solution)/shard_map/all_to_all | solution.py:366
  63.4 0.0 copy-done.8
  63.4 0.0 copy-start.1
  63.4 4.3 %collective-permute-start.1 = (bf16[128,256]{1,0:T(8,128)(2,1)S(1)}, bf16[128,256]{1,0:T(8,128)(2,1)S(1)}, u32[]{:S(2)}, u32[]{:S(2)}) collective-permute-start(bf16[128,256]{1,0:T(8,128)(2,1)S(1)} %copy-done.8), channel_id=1, source_target_pairs={{0,8},{8,0},{1,9},{9,1},{2,10},{10,2},{3,11},{11,3},{4,12},{12,4},... | collective-permute-start | bytes 196616 | tf_op jit(solution)/shard_map/ppermute | solution.py:374
  67.7 9.4 %all-to-all-done.2 = f16[8,272,128]{2,1,0:T(8,128)(2,1)} async-done(((f16[8,272,128]{2,1,0:T(8,128)(2,1)}), f16[8,272,128]{2,1,0:T(8,128)(2,1)}, u32[]{:S(2)}, u32[]{:S(2)}) %all-to-all-start.2) | async-done | bytes 557088 | tf_op jit(solution)/shard_map/all_to_all | solution.py:366
  77.2 1.1 convert_element_type.30.got
  78.3 0.0 copy-done.2
  78.3 0.0 collective-permute-done.1.swapped
  78.3 0.0 copy-start.10
  78.3 0.6 copy-done.10
  79.0 0.0 copy-done.1
  79.0 0.9 copy-done.3
  79.9 3.5 %shard_map.129 = (bf16[2,128,128]{2,1,0:T(8,128)(2,1)S(1)}, f32[2,128,128]{2,1,0:T(8,128)S(1)}, f32[2,128,128]{2,1,0:T(8,128)S(1)}, f32[2,128,128]{2,1,0:T(8,128...) custom-call(s32[1]{0:T(128)} %bitcast.6.place, s32[1]{0:T(128)} %bitcast.side, ...), custom_call_target="tpu_custom_call" | custom-call | flops 100000000 | bytes 2163720 | tf_op jit(solution)/shard_map/pallas_call | solution.py:354
  83.4 0.0 copy-start.4
  83.4 0.0 copy-start.6
  83.4 0.6 copy-done.4
  84.0 26.5 %all_to_all.47 = f16[6,144,128]{2,1,0:T(8,128)(2,1)S(1)} all-to-all(f16[6,144,128]{2,1,0:T(8,128)(2,1)S(1)} %broadcast_in_dim.12), channel_id=1, replica_groups=mesh['y'=8,'zh'=6,'zl'=2,'head'=8] {'zh'}, dimensions={0} | all-to-all | bytes 442368 | tf_op jit(solution)/shard_map/all_to_all | solution.py:366
  110.5 1.1 shard_map.131
  111.6 0.0 copy-done.6
  111.6 0.0 copy-start.5
  111.6 0.0 copy-start.7
  111.6 0.7 broadcast_in_dim.13
  112.4 4.1 %all-to-all-start.4 = ((f16[8,144,128]{2,1,0:T(8,128)(2,1)}), f16[8,144,128]{2,1,0:T(8,128)(2,1)}, u32[]{:S(2)}, u32[]{:S(2)}) async-start(f16[8,144,128]{2,1,0:T(8,128)(2,1)} %broadcast_in_dim.13), calls=%async_computation.4 | async-start | bytes 589824 | tf_op jit(solution)/shard_map/all_to_all | solution.py:366
  116.5 1.0 shard_map.132.matrix
  117.4 0.0 copy-done.5
  117.4 0.0 copy-done.7
  117.5 0.7 shard_map.130
  118.2 2.0 %collective-permute-start.2 = (bf16[2,128,128]{2,1,0:T(8,128)(2,1)S(1)}, bf16[2,128,128]{2,1,0:T(8,128)(2,1)S(1)}, u32[]{:S(2)}, u32[]{:S(2)}) collective-permute-start(bf16[2,128,128]{2,1,0:T(8,128)(2,1)S(1)} %get-tuple-element.63), channel_id=1, source_target_pairs={{0,8},{8,0},{1,9},{9,1},{2,10},{10,2},{3,11},{11,3},{4,12},{12,4},... | collective-permute-start | bytes 196616 | tf_op jit(solution)/shard_map/ppermute | solution.py:374
  120.2 7.1 %all-to-all-done.4 = f16[8,144,128]{2,1,0:T(8,128)(2,1)} async-done(((f16[8,144,128]{2,1,0:T(8,128)(2,1)}), f16[8,144,128]{2,1,0:T(8,128)(2,1)}, u32[]{:S(2)}, u32[]{:S(2)}) %all-to-all-start.4) | async-done | bytes 294944 | tf_op jit(solution)/shard_map/all_to_all | solution.py:366
  127.3 1.0 convert_element_type.34.gives
  128.3 0.0 copy-start.9
  128.3 0.0 copy-start.11
  128.3 3.2 %shard_map.133 = (bf16[2,128,128]{2,1,0:T(8,128)(2,1)S(1)}, bf16[2,128,128]{2,1,0:T(8,128)(2,1)S(1)}, f32[32,128]{1,0:T(8,128)}) custom-call(s32[1]{0:T(128)} %bitcast.6.place, s32[1]{0:T(128)} %bitcast.side, f32[8,272,128]{2,1,0:T(8,128)S(1)} %convert_element_type.30.got, f32[8,144,128]{2,1,0:T(8,128)S(1)} %convert_element_type.34.gives, ...), custom_call_target="tpu_custom_call" | custom-call | flops 100000000 | bytes 2950152 | tf_op jit(solution)/shard_map/pallas_call | solution.py:354
  131.5 4.0 %all-to-all-start.5 = ((f32[16,2,128]{2,1,0:T(2,128)}), f32[16,2,128]{2,1,0:T(2,128)S(1)}, u32[]{:S(2)}, u32[]{:S(2)}) async-start(f32[16,2,128]{2,1,0:T(2,128)} %bitcast.13), calls=%async_computation.5 | async-start | bytes 32768 | tf_op jit(solution)/shard_map/all_to_all | solution.py:451
  135.5 4.8 %all-to-all-done.5 = f32[16,2,128]{2,1,0:T(2,128)S(1)} async-done(((f32[16,2,128]{2,1,0:T(2,128)}), f32[16,2,128]{2,1,0:T(2,128)S(1)}, u32[]{:S(2)}, u32[]{:S(2)}) %all-to-all-start.5) | async-done | bytes 16416 | tf_op jit(solution)/shard_map/all_to_all | solution.py:451
  140.3 0.0 copy-done.9
  140.3 0.8 shard_map.134
  141.1 4.7 %all-to-all-start.6 = ((f32[6,24,256]{2,1,0:T(8,128)}), f32[6,24,256]{2,1,0:T(8,128)S(1)}, u32[]{:S(2)}, u32[]{:S(2)}) async-start(f32[6,24,256]{2,1,0:T(8,128)} %get-tuple-element.78), calls=%async_computation.6 | async-start | bytes 294912 | tf_op jit(solution)/shard_map/all_to_all | solution.py:457
  145.8 0.0 collective-permute-done.2
  145.8 0.7 maximum_select_fusion
  146.5 3.5 %collective-permute-start.3 = (bf16[2,128,128]{2,1,0:T(8,128)(2,1)S(1)}, bf16[2,128,128]{2,1,0:T(8,128)(2,1)S(1)}, u32[]{:S(2)}, u32[]{:S(2)}) collective-permute-start(bf16[2,128,128]{2,1,0:T(8,128)(2,1)S(1)} %get-tuple-element.76), channel_id=1, source_target_pairs={{0,8},{8,0},{1,9},{9,1},{2,10},{10,2},{3,11},{11,3},{4,12},{12,4},... | collective-permute-start | bytes 196616 | tf_op jit(solution)/shard_map/ppermute | solution.py:374
  150.0 9.4 %all-to-all-done.6 = f32[6,24,256]{2,1,0:T(8,128)S(1)} async-done(((f32[6,24,256]{2,1,0:T(8,128)}), f32[6,24,256]{2,1,0:T(8,128)S(1)}, u32[]{:S(2)}, u32[]{:S(2)}) %all-to-all-start.6) | async-done | bytes 147488 | tf_op jit(solution)/shard_map/all_to_all | solution.py:457
  159.4 0.7 broadcast_in_dim.14
  160.1 3.4 %all-to-all-start.7 = ((f32[8,24,256]{2,1,0:T(8,128)}), f32[8,24,256]{2,1,0:T(8,128)S(1)}, u32[]{:S(2)}, u32[]{:S(2)}) async-start(f32[8,24,256]{2,1,0:T(8,128)} %broadcast_in_dim.14), calls=%async_computation.7 | async-start | bytes 393216 | tf_op jit(solution)/shard_map/all_to_all | solution.py:366
  163.5 0.8 convolution_convert_fusion
  164.3 0.0 collective-permute-done.3
  164.4 0.7 maximum_select_fusion.2
  165.0 8.1 %all-to-all-done.7 = f32[8,24,256]{2,1,0:T(8,128)S(1)} async-done(((f32[8,24,256]{2,1,0:T(8,128)}), f32[8,24,256]{2,1,0:T(8,128)S(1)}, u32[]{:S(2)}, u32[]{:S(2)}) %all-to-all-start.7) | async-done | bytes 196640 | tf_op jit(solution)/shard_map/all_to_all | solution.py:366
  173.2 0.5 slice_bitcast_fusion.9
  173.7 0.6 slice_bitcast_fusion.8
  (17 shorter events, 0.2 us)
Async XLA Ops:
  2.5 18.5 %collective-permute-start = (bf16[4,128,128]{2,1,0:T(8,128)(2,1)}, bf16[4,128,128]{2,1,0:T(8,128)(2,1)S(1)}, u32[]{:S(2)}, u32[]{:S(2)}) collective-permute-start(bf16[4,128,128]{2,1,0:T(8,128)(2,1)} %get-tuple-element.45), channel_id=1, source_target_pairs={{0,8},{8,0},{1,9},{9,1},{2,10},{10,2},{3,11},{11,3},{4,12},{12,4},... | collective-permute-start | bytes 393224 | tf_op jit(solution)/shard_map/ppermute | solution.py:374
  21.0 0.9 copy-start
  28.2 25.9 %all-to-all-start.1 = ((f16[6,272,128]{2,1,0:T(8,128)(2,1)}), f16[6,272,128]{2,1,0:T(8,128)(2,1)S(1)}, u32[]{:S(2)}, u32[]{:S(2)}) async-start(f16[6,272,128]{2,1,0:T(8,128)(2,1)} %broadcast_in_dim.10), calls=%async_computation.1 | async-start | bytes 835584 | tf_op jit(solution)/shard_map/all_to_all | solution.py:366
  55.3 23.0 %copy-start.2 = (f32[256,128]{1,0:T(8,128)}, f32[256,128]{1,0:T(8,128)S(1)}, u32[]{:S(2)}) copy-start(f32[256,128]{1,0:T(8,128)S(1)} %get-tuple-element.52.own) | copy-start | bytes 393220
  55.3 8.1 %copy-start.8 = (bf16[128,256]{1,0:T(8,128)(2,1)S(1)}, bf16[128,256]{1,0:T(8,128)(2,1)}, u32[]{:S(2)}) copy-start(bf16[128,256]{1,0:T(8,128)(2,1)} %hidden.3) | copy-start | bytes 196612
  56.2 20.9 %all-to-all-start.2 = ((f16[8,272,128]{2,1,0:T(8,128)(2,1)}), f16[8,272,128]{2,1,0:T(8,128)(2,1)}, u32[]{:S(2)}, u32[]{:S(2)}) async-start(f16[8,272,128]{2,1,0:T(8,128)(2,1)} %broadcast_in_dim.11), calls=%async_computation.2 | async-start | bytes 1114112 | tf_op jit(solution)/shard_map/all_to_all | solution.py:366
  63.4 15.6 %copy-start.1 = (bf16[4,128,128]{2,1,0:T(8,128)(2,1)S(1)}, bf16[4,128,128]{2,1,0:T(8,128)(2,1)}, u32[]{:S(2)}) copy-start(bf16[4,128,128]{2,1,0:T(8,128)(2,1)} %get-tuple-element.44.mine.own.held) | copy-start | bytes 393220
  63.4 14.9 %collective-permute-start.1 = (bf16[128,256]{1,0:T(8,128)(2,1)S(1)}, bf16[128,256]{1,0:T(8,128)(2,1)S(1)}, u32[]{:S(2)}, u32[]{:S(2)}) collective-permute-start(bf16[128,256]{1,0:T(8,128)(2,1)S(1)} %copy-done.8), channel_id=1, source_target_pairs={{0,8},{8,0},{1,9},{9,1},{2,10},{10,2},{3,11},{11,3},{4,12},{12,4},... | collective-permute-start | bytes 196616 | tf_op jit(solution)/shard_map/ppermute | solution.py:374
  78.3 0.6 copy-start.10
  79.0 0.9 copy-start.3
  83.4 0.7 copy-start.4
  83.4 28.2 %copy-start.6 = (bf16[2,128,128]{2,1,0:T(8,128)(2,1)}, bf16[2,128,128]{2,1,0:T(8,128)(2,1)S(1)}, u32[]{:S(2)}) copy-start(bf16[2,128,128]{2,1,0:T(8,128)(2,1)S(1)} %get-tuple-element.61.out) | copy-start | bytes 196612
  111.6 5.8 %copy-start.5 = (f32[2,128,128]{2,1,0:T(8,128)S(1)}, f32[2,128,128]{2,1,0:T(8,128)}, u32[]{:S(2)}) copy-start(f32[2,128,128]{2,1,0:T(8,128)} %copy-done.4) | copy-start | bytes 393220
  111.6 5.8 %copy-start.7 = (bf16[2,128,128]{2,1,0:T(8,128)(2,1)S(1)}, bf16[2,128,128]{2,1,0:T(8,128)(2,1)}, u32[]{:S(2)}) copy-start(bf16[2,128,128]{2,1,0:T(8,128)(2,1)} %copy-done.6) | copy-start | bytes 196612
  112.4 14.9 %all-to-all-start.4 = ((f16[8,144,128]{2,1,0:T(8,128)(2,1)}), f16[8,144,128]{2,1,0:T(8,128)(2,1)}, u32[]{:S(2)}, u32[]{:S(2)}) async-start(f16[8,144,128]{2,1,0:T(8,128)(2,1)} %broadcast_in_dim.13), calls=%async_computation.4 | async-start | bytes 589824 | tf_op jit(solution)/shard_map/all_to_all | solution.py:366
  118.2 27.6 %collective-permute-start.2 = (bf16[2,128,128]{2,1,0:T(8,128)(2,1)S(1)}, bf16[2,128,128]{2,1,0:T(8,128)(2,1)S(1)}, u32[]{:S(2)}, u32[]{:S(2)}) collective-permute-start(bf16[2,128,128]{2,1,0:T(8,128)(2,1)S(1)} %get-tuple-element.63), channel_id=1, source_target_pairs={{0,8},{8,0},{1,9},{9,1},{2,10},{10,2},{3,11},{11,3},{4,12},{12,4},... | collective-permute-start | bytes 196616 | tf_op jit(solution)/shard_map/ppermute | solution.py:374
  128.3 12.0 %copy-start.9 = (bf16[128,256]{1,0:T(8,128)(2,1)S(1)}, bf16[128,256]{1,0:T(8,128)(2,1)}, u32[]{:S(2)}) copy-start(bf16[128,256]{1,0:T(8,128)(2,1)} %hidden.3) | copy-start | bytes 196612
  128.3 12.0 %copy-start.11 = (bf16[128,256]{1,0:T(8,128)(2,1)S(1)}, bf16[128,256]{1,0:T(8,128)(2,1)}, u32[]{:S(2)}) copy-start(bf16[128,256]{1,0:T(8,128)(2,1)} %copy-done.10) | copy-start | bytes 196612
  131.5 32.0 %copy-start.12 = (bf16[256,16]{0,1:T(8,128)(2,1)S(1)}, bf16[256,16]{0,1:T(8,128)(2,1)}, u32[]{:S(2)}) copy-start(bf16[256,16]{0,1:T(8,128)(2,1)} %param.8) | copy-start | bytes 24580
  131.5 8.8 %all-to-all-start.5 = ((f32[16,2,128]{2,1,0:T(2,128)}), f32[16,2,128]{2,1,0:T(2,128)S(1)}, u32[]{:S(2)}, u32[]{:S(2)}) async-start(f32[16,2,128]{2,1,0:T(2,128)} %bitcast.13), calls=%async_computation.5 | async-start | bytes 32768 | tf_op jit(solution)/shard_map/all_to_all | solution.py:451
  141.1 18.3 %all-to-all-start.6 = ((f32[6,24,256]{2,1,0:T(8,128)}), f32[6,24,256]{2,1,0:T(8,128)S(1)}, u32[]{:S(2)}, u32[]{:S(2)}) async-start(f32[6,24,256]{2,1,0:T(8,128)} %get-tuple-element.78), calls=%async_computation.6 | async-start | bytes 294912 | tf_op jit(solution)/shard_map/all_to_all | solution.py:457
  146.5 17.9 %collective-permute-start.3 = (bf16[2,128,128]{2,1,0:T(8,128)(2,1)S(1)}, bf16[2,128,128]{2,1,0:T(8,128)(2,1)S(1)}, u32[]{:S(2)}, u32[]{:S(2)}) collective-permute-start(bf16[2,128,128]{2,1,0:T(8,128)(2,1)S(1)} %get-tuple-element.76), channel_id=1, source_target_pairs={{0,8},{8,0},{1,9},{9,1},{2,10},{10,2},{3,11},{11,3},{4,12},{12,4},... | collective-permute-start | bytes 196616 | tf_op jit(solution)/shard_map/ppermute | solution.py:374
  160.1 13.1 %all-to-all-start.7 = ((f32[8,24,256]{2,1,0:T(8,128)}), f32[8,24,256]{2,1,0:T(8,128)S(1)}, u32[]{:S(2)}, u32[]{:S(2)}) async-start(f32[8,24,256]{2,1,0:T(8,128)} %broadcast_in_dim.14), calls=%async_computation.7 | async-start | bytes 393216 | tf_op jit(solution)/shard_map/all_to_all | solution.py:366

commit v5 on v4

--- a/solution.py
+++ b/solution.py
@@ -86,26 +86,30 @@
     scale = beta * rk
     less = dot2(solved_k * scale, kr, TN)
     gain = dot2(solved_v * scale, kr, TN)
+    return less, gain, inv, solved_k, solved_v
+
+
+def block_side(qr, kr, logit_row, inv, solved_k, solved_v):
+    row, col = index_grids()
+    beta_row = 2.0 * jax.nn.sigmoid(logit_row)
+    beta = to_col(beta_row, row, col)
+    rk, rq = inv_norm(kr), inv_norm(qr)
+    attend = jnp.where(row >= col, dot1(qr, kr, NT) * rq * to_row(rk, row, col), 0.0)
+    attend = attend * beta_row
+    read = qr.astype(F32) * rq - dot3(attend, solved_k)
+    fixed = dot3(attend, solved_v)
+    back_out = dot3(attend, inv)
     back_k = dot3(inv, beta * (kr.astype(F32) * rk), TN)
-    return less, gain, inv, solved_k, solved_v, back_k, gram
-
-
-def block_outputs(qr, kr, ct, logit_row, start, inv, solved_k, solved_v):
-    row, col = index_grids()
-    beta = to_col(2.0 * jax.nn.sigmoid(logit_row), row, col)
-    rk, rq = inv_norm(kr), inv_norm(qr)
-    rk_row = to_row(rk, row, col)
-    attend = jnp.where(row >= col, dot1(qr, kr, NT) * rq * rk_row, 0.0)
-    errors = solved_v - dot3(solved_k, start, NT)
-    scaled = beta * errors
-    raw = rq * dot2r(qr, start, NT) + dot3(attend, scaled)
+    return read, fixed, back_out, back_k
+
+
+def block_outputs(ct, start, read, fixed):
+    raw = fixed + dot3(read, start, NT)
     rn = lax.rsqrt(jnp.mean(raw * raw, axis=1, keepdims=True) + 1e-05)
     normed = raw * rn
     cotan = ct.astype(F32)
     d_raw = rn * (cotan - normed * jnp.mean(normed * cotan, axis=1, keepdims=True))
-    back0 = dot3(inv, beta * dot3(attend, d_raw, TN), TN)
-    give = dot2(d_raw * rq, qr, TN) - dot2(back0 * rk, kr, TN)
-    return normed, errors, d_raw, back0, give
+    return normed, d_raw, dot3(d_raw, read, TN)
 
 
 def block_grads_early(qr, kr, logit_row, start, errors, d_raw):
@@ -122,21 +126,24 @@
     return dq, dk_part
 
 
-def block_grads(kr, logit_row, start, end_grad, errors, back0, back_k, dk_part):
+def block_logit_grads(logit_row, end_grad, errors, back0, back_k):
+    row, col = index_grids()
+    keep = to_col(jax.nn.sigmoid(-logit_row), row, col)
+    back = back0 + dot3(back_k, end_grad, NT)
+    return back, to_row(jnp.sum(errors * back, axis=1, keepdims=True) * keep, row, col)
+
+
+def block_key_grads(kr, logit_row, start, end_grad, errors, back, dk_part):
     row, col = index_grids()
     beta = to_col(2.0 * jax.nn.sigmoid(logit_row), row, col)
-    keep = to_col(jax.nn.sigmoid(-logit_row), row, col)
     rk = inv_norm(kr)
     rk_row = to_row(rk, row, col)
     scaled = beta * errors
-    back = back0 + dot3(back_k, end_grad, NT)
-    d_logit = to_row(jnp.sum(errors * back, axis=1, keepdims=True) * keep, row, col)
     d_gram = jnp.where(row > col, -dot3(back, scaled, NT), 0.0)
     d_gram = d_gram + jnp.where(row < col, -dot3(scaled, back, NT), 0.0)
     dk_unit = dk_part - dot3(back, start) + dot3(scaled, end_grad) + dot2(d_gram * rk_row, kr)
     k_unit = kr.astype(F32) * rk
-    dk = rk * (dk_unit - k_unit * jnp.sum(k_unit * dk_unit, axis=1, keepdims=True))
-    return dk, back, d_logit
+    return rk * (dk_unit - k_unit * jnp.sum(k_unit * dk_unit, axis=1, keepdims=True))
 
 
 def level_of(x):
@@ -163,7 +170,10 @@
     state = jnp.concatenate([eye, zero], axis=0)
     own = state
     for j in range(count):
-        own = jnp.where(place == j, state, own)
+        if place is not None:
+            own = jnp.where(place == j, state, own)
+            if j == count - 1:
+                break
         if j == 0:
             state = jnp.concatenate([eye - less(j), gain(j)], axis=0)
         else:
@@ -241,38 +251,44 @@
     for i in range(4):
         copies[i + 2].wait()
         mine[i], theirs[i] = in_order(side, held[i + 1, :, :D], held[i + 1, :, D:])
-
-
-def kernel_prepare(side, part, mine, swapped, send, lg, less, gain, inv, sk, sv, bk):
+    theirs[4], theirs[5] = held[0, :, :D], held[0, :, D:]
+
+
+def kernel_prepare(side, part, mine, swapped, send, lg, less, gain, inv, sk, sv):
     odd = lax.broadcasted_iota(jnp.int32, (16, L), 0) % 2
     moves = []
     ks, vs = in_order(side, mine[0], swapped[0]), in_order(side, mine[1], swapped[1])
     for b in range(2):
         logit = jnp.sum(jnp.where(odd == b, part[...], 0.0), axis=0, keepdims=True)
         lg[b : b + 1, :] = logit
-        w, n, *rest, _ = block_prepare(ks[b], vs[b], logit)
+        w, n, *rest = block_prepare(ks[b], vs[b], logit)
         less[b], gain[b] = w, n
-        inv[b], sk[b], sv[b], bk[b] = rest
+        inv[b], sk[b], sv[b] = rest
         moves.append((w, n))
     (w0, n0), (w1, n1) = moves
     both = step(jnp.concatenate([w0, n0], axis=0), w1)
     put(send, both[:D] + w1, both[D:] + n1)
 
 
-def kernel_row_forward(count, place, got, send, own):
-    state, before = chain_forward(less_of(got), gain_of(got), place[0], count)
+def kernel_row_forward(count, got, send):
+    state, _ = chain_forward(less_of(got), gain_of(got), None, count)
     row, col = index_grids()
     put(send, jnp.where(row == col, 1.0, 0.0) - state[:D], state[D:])
-    own[...] = before
-
-
-def kernel_row_matrix(count, place, got, own):
-    own[...] = chain_back_matrix(less_of(got), place[0], count)
-
-
-def kernel_outputs(count, place, side, got, own, lg, mine, swapped, less, gain, inv, sk, sv,
-                   out, start, err, draw, back0, give, send):
+
+
+def kernel_side(count, place, side, lg, mine, swapped, got, inv, sk, sv,
+                own, matrix, read, fixed, bo, bk):
     ks, qs = in_order(side, mine[0], swapped[0]), in_order(side, mine[2], swapped[2])
+    for b in range(2):
+        read[b], fixed[b], bo[b], bk[b] = block_side(
+            qs[b], ks[b], lg[b : b + 1, :], inv[b], sk[b], sv[b]
+        )
+    own[...] = chain_forward(less_of(got), gain_of(got), place[0], count)[1]
+    matrix[...] = chain_back_matrix(less_of(got), place[0], count)
+
+
+def kernel_outputs(count, place, side, got, own, mine, swapped, less, gain, read, fixed,
+                   out, start, draw, give, send):
     cs = in_order(side, mine[3], swapped[3])
     first = chain_state(less_of(got), gain_of(got), place[0], count)
     before = dot3(first, own[:D]) + own[D:]
@@ -280,22 +296,24 @@
     for b in range(2):
         if b == 1:
             before = step(before, less[0]) + gain[0]
-        normed, e, dr, b0, g = block_outputs(
-            qs[b], ks[b], cs[b], lg[b : b + 1, :], before, inv[b], sk[b], sv[b]
-        )
+        normed, draw[b], g = block_outputs(cs[b], before, read[b], fixed[b])
         out[b] = normed.astype(BF16)
-        start[b], err[b], draw[b], back0[b] = before, e, dr, b0
+        start[b] = before
         gives.append(g)
     give[...] = gives[1]
     send[0:D], send[D : D + 16] = packed(step(gives[1], less[0], NT) + gives[0])
 
 
-def kernel_early(side, lg, own, swapped, start, err, draw, out, mine, theirs, dkp):
+def kernel_early(side, lg, own, swapped, start, draw, sk, sv, bo, out,
+                 mine, theirs, dkp, err, back0):
     ks, qs = in_order(side, own[0], swapped[0]), in_order(side, own[2], swapped[2])
     dqs = []
     for b in range(2):
+        errors = sv[b] - dot3(sk[b], start[b], NT)
+        err[b] = errors
+        back0[b] = dot3(bo[b], draw[b], TN)
         dq, dkp[b] = block_grads_early(
-            qs[b], ks[b], lg[b : b + 1, :], start[b], err[b], draw[b]
+            qs[b], ks[b], lg[b : b + 1, :], start[b], errors, draw[b]
         )
         dqs.append(dq)
     mine[0], theirs[0] = in_order(side, out[0], out[1])
@@ -309,30 +327,37 @@
     own[...] = after
 
 
-def kernel_grads(count, place, side, got, gives, matrix, own, lg, held, swapped, less, give,
-                 start, err, back0, bk, dkp, mine, theirs, message):
-    ks = in_order(side, held[0], swapped[0])
+def kernel_grads(count, place, got, gives, matrix, own, lg, less, give, err, back0, bk,
+                 ends, back, message):
     _, row_after = chain_back(less_of(got), give_of(gives), place[0], count, total=False)
     end_grad = dot3(row_after, matrix[...]) + own[...]
-    later = block_grads(
-        ks[1], lg[1:2, :], start[1], end_grad, err[1], back0[1], bk[1], dkp[1]
-    )
-    end_grad = step(end_grad, less[1], NT) + give[...]
-    earlier = block_grads(
-        ks[0], lg[0:1, :], start[0], end_grad, err[0], back0[0], bk[0], dkp[0]
-    )
-    for i in range(2):
-        x, y = in_order(side, earlier[i], later[i])
+    ends[1] = end_grad
+    ends[0] = step(end_grad, less[1], NT) + give[...]
+    rows = []
+    for b in range(2):
+        back[b], row = block_logit_grads(lg[b : b + 1, :], ends[b], err[b], back0[b], bk[b])
+        rows.append(row)
+    odd = lax.broadcasted_iota(jnp.int32, (32, L), 0) % 2
+    message[...] = jnp.where(odd == 0, rows[0], rows[1])
+
+
+def kernel_keys(side, lg, held, swapped, start, ends, err, back, dkp, mine, theirs):
+    ks = in_order(side, held[0], swapped[0])
+    dks = [
+        block_key_grads(ks[b], lg[b : b + 1, :], start[b], ends[b], err[b], back[b], dkp[b])
+        for b in range(2)
+    ]
+    for i, pair in enumerate((dks, (back[0], back[1]))):
+        x, y = in_order(side, *pair)
         mine[i], theirs[i] = x.astype(BF16), y.astype(BF16)
-    odd = lax.broadcasted_iota(jnp.int32, (32, L), 0) % 2
-    message[...] = jnp.where(odd == 0, earlier[2], later[2])
 
 
 def kernel_weight(side, slot, got, hidden, swapped, total, grads):
     rows = [got[pl.ds(b, 16, stride=2), :] for b in range(2)]
     here, there = in_order(side, *rows)
     grads[...] = here.astype(BF16)
-    weight = dot1(here.astype(BF16), hidden[...]) + dot1(there.astype(BF16), swapped[...])
+    theirs = jnp.concatenate([swapped[4], swapped[5]], axis=1)
+    weight = dot1(here.astype(BF16), hidden[...]) + dot1(there.astype(BF16), theirs)
     bias = jnp.sum(rows[0] + rows[1], axis=1, keepdims=True)
     row = lax.broadcasted_iota(jnp.int32, (16, 2 * D), 0)
     col = lax.broadcasted_iota(jnp.int32, (16, 2 * D), 1)
@@ -396,10 +421,10 @@
 
     at_h = lax.axis_index("head").astype(jnp.int32).reshape(1)
 
-    four = jax.ShapeDtypeStruct((4, L, D), BF16)
+    four, six = [jax.ShapeDtypeStruct((n, L, D), BF16) for n in (4, 6)]
     part, held, theirs = pl.pallas_call(
         kernel_first,
-        out_shape=[jax.ShapeDtypeStruct((16, L), F32), four, four],
+        out_shape=[jax.ShapeDtypeStruct((16, L), F32), four, six],
         in_specs=[SM] * 2 + [pl.BlockSpec(memory_space=pl.ANY)] * 7,
         out_specs=[VM] * 3,
         scratch_shapes=[
@@ -414,44 +439,47 @@
     part = lax.all_to_all(part, ("head", "zl"), 0, 0, tiled=True)
     swapped = swap(theirs)
 
-    send1, logits, less, gain, inv, sk, sv, bk = call(
-        kernel_prepare, [((2 * D + 16, D), F32), ((2, L), F32)] + [PAIR] * 6,
+    send1, logits, less, gain, inv, sk, sv = call(
+        kernel_prepare, [((2 * D + 16, D), F32), ((2, L), F32)] + [PAIR] * 5,
         at_s, part, held, swapped,
     )
     got1 = spread(send1, "zh")
-    send2, own1 = call(
-        functools.partial(kernel_row_forward, pairs),
-        [((2 * D + 16, D), F32), ((2 * D, D), F32)], at_z, got1,
-    )
-    send2, hidden_s = lax.optimization_barrier((send2, hidden))
-    hidden_s = swap(hidden_s)
-    got2, hidden_s = lax.optimization_barrier((spread(send2, "y"), hidden_s))
-    (matrix,) = call(functools.partial(kernel_row_matrix, pairs), [HALF], at_z, got1)
-    out, start, err, draw, back0, give, send3 = call(
+    (send2,) = call(
+        functools.partial(kernel_row_forward, pairs), [((2 * D + 16, D), F32)], got1
+    )
+    got2 = spread(send2, "y")
+    own1, matrix, read, fixed, bo, bk = call(
+        functools.partial(kernel_side, pairs), [((2 * D, D), F32), HALF] + [PAIR] * 4,
+        at_z, at_s, logits, held, swapped, got1, inv, sk, sv,
+    )
+    out, start, draw, give, send3 = call(
         functools.partial(kernel_outputs, rows),
-        [PAIRB] + [PAIR] * 4 + [HALF, ((D + 16, D), F32)],
-        at_y, at_s, got2, own1, logits, held, swapped, less, gain, inv, sk, sv,
+        [PAIRB] + [PAIR] * 2 + [HALF, ((D + 16, D), F32)],
+        at_y, at_s, got2, own1, held, swapped, less, gain, read, fixed,
     )
     got3 = spread(send3, "zh")
-    mine, theirs, dkp = call(
-        kernel_early, [PAIRB, PAIRB, PAIR],
-        at_s, logits, held, swapped, start, err, draw, out,
+    mine, theirs, dkp, err, back0 = call(
+        kernel_early, [PAIRB, PAIRB] + [PAIR] * 3,
+        at_s, logits, held, swapped, start, draw, sk, sv, bo, out,
     )
     send4, own2 = call(
         functools.partial(kernel_row_back, pairs), [((D + 16, D), F32), HALF], at_z, got1, got3
     )
     got4 = spread(send4, "y")
     theirs = swap(theirs)
-    mine_kv, theirs_kv, message = call(
-        functools.partial(kernel_grads, rows), [PAIRB, PAIRB, ((32, L), F32)],
-        at_y, at_s, got2, got4, matrix, own2, logits, held, swapped, less, give, start, err,
-        back0, bk, dkp,
+    ends, back, message = call(
+        functools.partial(kernel_grads, rows), [PAIR, PAIR, ((32, L), F32)],
+        at_y, got2, got4, matrix, own2, logits, less, give, err, back0, bk,
+    )
+    mine_kv, theirs_kv = call(
+        kernel_keys, [PAIRB, PAIRB],
+        at_s, logits, held, swapped, start, ends, err, back, dkp,
     )
 
     message = lax.all_to_all(message.reshape(16, 2, L), ("head", "zl"), 0, 0)
     total, grads = call(
         kernel_weight, [((pairs, 24, 2 * D), F32), ((16, L), BF16)],
-        at_s, at_h, message.reshape(32, L), hidden, hidden_s,
+        at_s, at_h, message.reshape(32, L), hidden, swapped,
     )
     total, theirs_kv = lax.optimization_barrier((total, theirs_kv))
     total = jnp.sum(lax.all_to_all(total, "zh", 0, 0), axis=0)

time: 175 us -> 167 us (0.954)
  blocking collectives: 34.4 us -> 55.9 us
  waiting for transfers between devices: 56.8 us -> 36 us
  starting transfers between devices: 51.7 us -> 43.7 us
    all_to_all x1 -> x2, blocking collectives: 26.5 us -> 47.9 us  [copies(): lax.all_to_all(jnp.broadcast_to(x[None], (count,) + x.shape), axis, 0, 0)]
    all_to_all x4 -> x3, waiting for transfers between devices: 42.6 us -> 22.5 us  [copies(): lax.all_to_all(jnp.broadcast_to(x[None], (count,) + x.shape), axis, 0, 0)]
    all_to_all x4 -> x3, starting transfers between devices: 22.5 us -> 13.9 us  [copies(): lax.all_to_all(jnp.broadcast_to(x[None], (count,) + x.shape), axis, 0, 0)]
    all_to_all x1, starting transfers between devices: 4.04 us -> 6.88 us  [per_device(): message = lax.all_to_all(message.reshape(16, 2, L), ('head', 'zl'), 0, 0)]
    ppermute x4 -> x3, starting transfers between devices: 20.5 us -> 19.3 us  [swap(): return lax.ppermute(x, 'zl', [(0, 1), (1, 0)])]
    pallas_call x8 -> x9, Pallas kernels: 16.7 us -> 17.6 us  [call(): pl.pallas_call(body, out_shape=[jax.ShapeDtypeStruct(s, t) for s, t in ou...]
  transfers between devices with their start and end apart: 10 -> 8, of which waited for: 6 -> 5; matrix products, arithmetic and copies ran while one was open for 3% -> 2% of each run, Pallas kernels for 3% -> 4%
where the time goes in v5:
time: 167 us; the launch traced here: 166 us
  blocking collectives  55.9 us (33%)
  starting transfers between devices  43.7 us (26%)
  waiting for transfers between devices  36 us (22%)
  Pallas kernels  19.4 us (12%)
  local copies, waits for them, and re-layouts  6.91 us (4%)
  other arithmetic  2.75 us (2%)
    all_to_all x2, blocking collectives, copies(): lax.all_to_all(jnp.broadcast_to(x[None], (count,) + x.shape), axis, 0, 0)  47.9 us
    all_to_all x3, waiting for transfers between devices, copies(): lax.all_to_all(jnp.broadcast_to(x[None], (count,) + x.shape), axis, 0, 0)  22.5 us
    ppermute x3, starting transfers between devices, swap(): return lax.ppermute(x, 'zl', [(0, 1), (1, 0)])  19.3 us
    pallas_call x9, Pallas kernels, call(): pl.pallas_call(body, out_shape=[jax.ShapeDtypeStruct(s, t) for s, t in ou...  17.6 us
    all_to_all x3, starting transfers between devices, copies(): lax.all_to_all(jnp.broadcast_to(x[None], (count,) + x.shape), axis, 0, 0)  13.9 us
    all_to_all x1, waiting for transfers between devices, per_device(): total = jnp.sum(lax.all_to_all(total, 'zh', 0, 0), axis=0)  9.63 us
    all_to_all x1, blocking collectives, per_device(): part = lax.all_to_all(part, ('head', 'zl'), 0, 0, tiled=True)  7.96 us
    all_to_all x1, starting transfers between devices, per_device(): message = lax.all_to_all(message.reshape(16, 2, L), ('head', 'zl'), 0, 0)  6.88 us
  transfers between devices with their start and end apart: 8, of which 5 were waited for; matrix products, arithmetic and copies ran while one was open for 2% of the time, Pallas kernels for 4%

profile of v5, /device:TPU:64, one launch (start us, length us, event | category | flops | bytes accessed | tf_op | source)
XLA Modules:
  0.0 166.5 jit_solution(14840691974350693321)
XLA Ops:
  0.6 1.9 %shard_map.126 = (f32[16,128]{1,0:T(8,128)}, bf16[4,128,128]{2,1,0:T(8,128)(2,1)}, bf16[6,128,128]{2,1,0:T(8,128)(2,1)}) custom-call(s32[1]{0:T(128)} %bitcast.side, s32[1]{0:T(128)} %bitcast.1.slot, f32[2]{0:T(128)} %bias.1, bf16[16,256]{1,0:T(8,128)(2,1)} %bitcast.35, bf16[128,256]{1,0:T(8,128)(2,1)} %hidden.3, bf16[128,256]{1,0:T(8,128)(2,1)} %k.1, ...), custom_call_target="tpu_custom_call" | custom-call | flops 10000000 | bytes 1000000 | tf_op jit(solution)/shard_map/pallas_call | solution.py:425
  2.5 10.6 %collective-permute-start = (bf16[6,128,128]{2,1,0:T(8,128)(2,1)}, bf16[6,128,128]{2,1,0:T(8,128)(2,1)S(1)}, u32[]{:S(2)}, u32[]{:S(2)}) collective-permute-start(bf16[6,128,128]{2,1,0:T(8,128)(2,1)} %get-tuple-element.46), channel_id=1, source_target_pairs={{0,8},{8,0},{1,9},{9,1},{2,10},{10,2},{3,11},{11,3},{4,12},{12,4},... | collective-permute-start | bytes 589832 | tf_op jit(solution)/shard_map/ppermute | solution.py:399
  13.1 8.0 %all_to_all.46 = f32[16,1,128]{2,1,0:T(1,128)S(1)} all-to-all(f32[16,1,128]{2,1,0:T(1,128)} %bitcast.36), channel_id=1, replica_groups=mesh['y'=8,'zh'=6,'zl'=2,'head'=8] {'head','zl'}, dimensions={0} | all-to-all | bytes 16384 | tf_op jit(solution)/shard_map/all_to_all | solution.py:439
  21.1 0.0 collective-permute-done.swapped
  21.1 0.0 copy-start
  21.1 0.9 copy-done
  22.0 5.4 %shard_map.127 = (f32[272,128]{1,0:T(8,128)S(1)}, f32[2,128]{1,0:T(2,128)S(1)}, f32[2,128,128]{2,1,0:T(8,128)S(1)}, f32[2,128,128]{2,1,0:T(8,128)S(1)}, f32[2,12...) custom-call(s32[1]{0:T(128)} %bitcast.side, f32[16,128]{1,0:T(8,128)S(1)} %bitcast.34, ...), custom_call_target="tpu_custom_call" | custom-call | flops 100000000 | bytes 335876 | tf_op jit(solution)/shard_map/pallas_call | solution.py:379
  27.4 0.1 broadcast_in_dim.10
  27.5 29.7 %all_to_all.47 = f16[6,272,128]{2,1,0:T(8,128)(2,1)S(1)} all-to-all(f16[6,272,128]{2,1,0:T(8,128)(2,1)S(1)} %broadcast_in_dim.10), channel_id=1, replica_groups=mesh['y'=8,'zh'=6,'zl'=2,'head'=8] {'zh'}, dimensions={0} | all-to-all | bytes 835584 | tf_op jit(solution)/shard_map/all_to_all | solution.py:391
  57.2 0.1 convert_element_type.28.got
  57.3 1.1 shard_map.128
  58.3 0.0 copy-start.1
  58.4 0.9 broadcast_in_dim.11
  59.2 7.1 %all-to-all-start.2 = ((f16[8,272,128]{2,1,0:T(8,128)(2,1)}), f16[8,272,128]{2,1,0:T(8,128)(2,1)}, u32[]{:S(2)}, u32[]{:S(2)}) async-start(f16[8,272,128]{2,1,0:T(8,128)(2,1)} %broadcast_in_dim.11), calls=%async_computation.2 | async-start | bytes 1114112 | tf_op jit(solution)/shard_map/all_to_all | solution.py:391
  66.3 0.0 copy-done.1
  66.3 2.0 %shard_map.129 = (f32[256,128]{1,0:T(8,128)S(1)}, f32[128,128]{1,0:T(8,128)S(1)}, f32[2,128,128]{2,1,0:T(8,128)S(1)}, f32[2,128,128]{2,1,0:T(8,128)S(1)}, f32[2,...) custom-call(s32[1]{0:T(128)} %bitcast.7.place, s32[1]{0:T(128)} %bitcast.side, f32[2,128]{1,0:T(2,128)S(1)} %get-tuple-element.47.lg, ...), custom_call_target="tpu_custom_call" | custom-call | flops 100000000 | bytes 1557512 | tf_op jit(solution)/shard_map/pallas_call | solution.py:379
  68.4 0.0 copy-start.2
  68.4 0.6 copy-done.2
  69.0 0.0 copy-start.4
  69.0 11.1 %all-to-all-done.2 = f16[8,272,128]{2,1,0:T(8,128)(2,1)} async-done(((f16[8,272,128]{2,1,0:T(8,128)(2,1)}), f16[8,272,128]{2,1,0:T(8,128)(2,1)}, u32[]{:S(2)}, u32[]{:S(2)}) %all-to-all-start.2) | async-done | bytes 557088 | tf_op jit(solution)/shard_map/all_to_all | solution.py:391
  80.1 0.0 copy-start.3
  80.1 1.2 convert_element_type.30.got
  81.3 0.0 copy-done.4
  81.3 0.0 copy-done.3
  81.3 0.0 copy-start.5
  81.3 0.9 copy-done.5
  82.2 2.6 %shard_map.130 = (bf16[2,128,128]{2,1,0:T(8,128)(2,1)S(1)}, f32[2,128,128]{2,1,0:T(8,128)S(1)}, f32[2,128,128]{2,1,0:T(8,128)S(1)}, f32[128,128]{1,0:T(8,128)S(1)}, f32[144,128]{1,0:T(8,128)S(1)}) custom-call(s32[1]{0:T(128)} %bitcast.6.place, s32[1]{0:T(128)} %bitcast.side, f32[8,272,128]{2,1,0:T(8,128)S(1)} %convert_element_type.30.got, ...), custom_call_target="tpu_custom_call" | custom-call | flops 100000000 | bytes 2097160 | tf_op jit(solution)/shard_map/pallas_call | solution.py:379
  84.8 0.0 copy-start.6
  84.8 0.0 copy-start.8
  84.9 18.2 %all_to_all.48 = f16[6,144,128]{2,1,0:T(8,128)(2,1)S(1)} all-to-all(f16[6,144,128]{2,1,0:T(8,128)(2,1)S(1)} %broadcast_in_dim.12), channel_id=1, replica_groups=mesh['y'=8,'zh'=6,'zl'=2,'head'=8] {'zh'}, dimensions={0} | all-to-all | bytes 442368 | tf_op jit(solution)/shard_map/all_to_all | solution.py:391
  103.2 1.1 shard_map.132
  104.2 0.0 copy-done.6
  104.2 0.0 copy-done.8
  104.3 0.7 broadcast_in_dim.13
  105.0 3.4 %all-to-all-start.4 = ((f16[8,144,128]{2,1,0:T(8,128)(2,1)}), f16[8,144,128]{2,1,0:T(8,128)(2,1)S(1)}, u32[]{:S(2)}, u32[]{:S(2)}) async-start(f16[8,144,128]{2,1,0:T(8,128)(2,1)} %broadcast_in_dim.13), calls=%async_computation.4 | async-start | bytes 589824 | tf_op jit(solution)/shard_map/all_to_all | solution.py:391
  108.4 0.0 copy-start.7
  108.5 0.0 copy-start.9
  108.5 0.9 copy-done.9
  109.3 1.2 shard_map.131
  110.6 5.4 %collective-permute-start.1 = (bf16[2,128,128]{2,1,0:T(8,128)(2,1)S(1)}, bf16[2,128,128]{2,1,0:T(8,128)(2,1)S(1)}, u32[]{:S(2)}, u32[]{:S(2)}) collective-permute-start(bf16[2,128,128]{2,1,0:T(8,128)(2,1)S(1)} %get-tuple-element.62), channel_id=1, source_target_pairs={{0,8},{8,0},{1,9},{9,1},{2,10},{10,2},{3,11},{11,3},{4,12},{12,4},... | collective-permute-start | bytes 196616 | tf_op jit(solution)/shard_map/ppermute | solution.py:399
  115.9 3.3 %all-to-all-done.4 = f16[8,144,128]{2,1,0:T(8,128)(2,1)S(1)} async-done(((f16[8,144,128]{2,1,0:T(8,128)(2,1)}), f16[8,144,128]{2,1,0:T(8,128)(2,1)S(1)}, u32[]{:S(2)}, u32[]{:S(2)}) %all-to-all-start.4) | async-done | bytes 294944 | tf_op jit(solution)/shard_map/all_to_all | solution.py:391
  119.2 0.0 copy-done.7
  119.2 2.5 %shard_map.133 = (f32[2,128,128]{2,1,0:T(8,128)S(1)}, f32[2,128,128]{2,1,0:T(8,128)S(1)}, f32[32,128]{1,0:T(8,128)}) custom-call(s32[1]{0:T(128)} %bitcast.6.place, f32[8,272,128]{2,1,0:T(8,128)S(1)} %convert_element_type.30.got, f32[8,144,128]{2,1,0:T(8,128)S(1)} %convert_element_type.34.gives, f32[128,128]{1,0:T(8,128)S(1)} %get-tuple-element.65.matrix, ...), custom_call_target="tpu_custom_call" | custom-call | flops 100000000 | bytes 2425860 | tf_op jit(solution)/shard_map/pallas_call | solution.py:379
  121.7 0.0 copy-start.10
  121.7 6.9 %all-to-all-start.5 = ((f32[16,2,128]{2,1,0:T(2,128)}), f32[16,2,128]{2,1,0:T(2,128)S(1)}, u32[]{:S(2)}, u32[]{:S(2)}) async-start(f32[16,2,128]{2,1,0:T(2,128)} %bitcast.13), calls=%async_computation.5 | async-start | bytes 32768 | tf_op jit(solution)/shard_map/all_to_all | solution.py:479
  128.6 0.9 shard_map.134
  129.5 0.0 copy-start.11
  129.5 3.9 %all-to-all-done.5 = f32[16,2,128]{2,1,0:T(2,128)S(1)} async-done(((f32[16,2,128]{2,1,0:T(2,128)}), f32[16,2,128]{2,1,0:T(2,128)S(1)}, u32[]{:S(2)}, u32[]{:S(2)}) %all-to-all-start.5) | async-done | bytes 16416 | tf_op jit(solution)/shard_map/all_to_all | solution.py:479
  133.4 0.0 copy-done.10
  133.4 0.8 shard_map.135
  134.2 3.6 %all-to-all-start.6 = ((f32[6,24,256]{2,1,0:T(8,128)}), f32[6,24,256]{2,1,0:T(8,128)S(1)}, u32[]{:S(2)}, u32[]{:S(2)}) async-start(f32[6,24,256]{2,1,0:T(8,128)} %get-tuple-element.80), calls=%async_computation.6 | async-start | bytes 294912 | tf_op jit(solution)/shard_map/all_to_all | solution.py:485
  137.8 0.0 collective-permute-done.1
  137.9 0.7 maximum_select_fusion
  138.6 3.3 %collective-permute-start.2 = (bf16[2,128,128]{2,1,0:T(8,128)(2,1)S(1)}, bf16[2,128,128]{2,1,0:T(8,128)(2,1)S(1)}, u32[]{:S(2)}, u32[]{:S(2)}) collective-permute-start(bf16[2,128,128]{2,1,0:T(8,128)(2,1)S(1)} %get-tuple-element.78), channel_id=1, source_target_pairs={{0,8},{8,0},{1,9},{9,1},{2,10},{10,2},{3,11},{11,3},{4,12},{12,4},... | collective-permute-start | bytes 196616 | tf_op jit(solution)/shard_map/ppermute | solution.py:399
  141.9 9.6 %all-to-all-done.6 = f32[6,24,256]{2,1,0:T(8,128)S(1)} async-done(((f32[6,24,256]{2,1,0:T(8,128)}), f32[6,24,256]{2,1,0:T(8,128)S(1)}, u32[]{:S(2)}, u32[]{:S(2)}) %all-to-all-start.6) | async-done | bytes 147488 | tf_op jit(solution)/shard_map/all_to_all | solution.py:485
  151.5 0.7 broadcast_in_dim.14
  152.2 3.4 %all-to-all-start.7 = ((f32[8,24,256]{2,1,0:T(8,128)}), f32[8,24,256]{2,1,0:T(8,128)S(1)}, u32[]{:S(2)}, u32[]{:S(2)}) async-start(f32[8,24,256]{2,1,0:T(8,128)} %broadcast_in_dim.14), calls=%async_computation.7 | async-start | bytes 393216 | tf_op jit(solution)/shard_map/all_to_all | solution.py:391
  155.6 0.0 copy-done.11
  155.6 0.8 convolution_convert_fusion
  156.5 0.0 collective-permute-done.2
  156.5 0.7 maximum_select_fusion.2
  157.2 8.1 %all-to-all-done.7 = f32[8,24,256]{2,1,0:T(8,128)S(1)} async-done(((f32[8,24,256]{2,1,0:T(8,128)}), f32[8,24,256]{2,1,0:T(8,128)S(1)}, u32[]{:S(2)}, u32[]{:S(2)}) %all-to-all-start.7) | async-done | bytes 196640 | tf_op jit(solution)/shard_map/all_to_all | solution.py:391
  165.3 0.5 slice_bitcast_fusion.9
  165.8 0.6 slice_bitcast_fusion.8
  (13 shorter events, 0.2 us)
Async XLA Ops:
  2.5 18.5 %collective-permute-start = (bf16[6,128,128]{2,1,0:T(8,128)(2,1)}, bf16[6,128,128]{2,1,0:T(8,128)(2,1)S(1)}, u32[]{:S(2)}, u32[]{:S(2)}) collective-permute-start(bf16[6,128,128]{2,1,0:T(8,128)(2,1)} %get-tuple-element.46), channel_id=1, source_target_pairs={{0,8},{8,0},{1,9},{9,1},{2,10},{10,2},{3,11},{11,3},{4,12},{12,4},... | collective-permute-start | bytes 589832 | tf_op jit(solution)/shard_map/ppermute | solution.py:399
  21.1 0.9 copy-start
  58.3 8.0 %copy-start.1 = (bf16[4,128,128]{2,1,0:T(8,128)(2,1)S(1)}, bf16[4,128,128]{2,1,0:T(8,128)(2,1)}, u32[]{:S(2)}) copy-start(bf16[4,128,128]{2,1,0:T(8,128)(2,1)} %get-tuple-element.45.mine.own.held) | copy-start | bytes 393220
  59.2 20.8 %all-to-all-start.2 = ((f16[8,272,128]{2,1,0:T(8,128)(2,1)}), f16[8,272,128]{2,1,0:T(8,128)(2,1)}, u32[]{:S(2)}, u32[]{:S(2)}) async-start(f16[8,272,128]{2,1,0:T(8,128)(2,1)} %broadcast_in_dim.11), calls=%async_computation.2 | async-start | bytes 1114112 | tf_op jit(solution)/shard_map/all_to_all | solution.py:391
  68.4 0.7 copy-start.2
  69.0 12.2 %copy-start.4 = (f32[2,128,128]{2,1,0:T(8,128)}, f32[2,128,128]{2,1,0:T(8,128)S(1)}, u32[]{:S(2)}) copy-start(f32[2,128,128]{2,1,0:T(8,128)S(1)} %get-tuple-element.56.fixed) | copy-start | bytes 393220
  80.1 1.2 copy-start.3
  81.3 0.9 copy-start.5
  84.8 19.4 %copy-start.6 = (f32[128,128]{1,0:T(8,128)}, f32[128,128]{1,0:T(8,128)S(1)}, u32[]{:S(2)}) copy-start(f32[128,128]{1,0:T(8,128)S(1)} %get-tuple-element.67.give) | copy-start | bytes 196612
  84.8 19.4 %copy-start.8 = (bf16[2,128,128]{2,1,0:T(8,128)(2,1)}, bf16[2,128,128]{2,1,0:T(8,128)(2,1)S(1)}, u32[]{:S(2)}) copy-start(bf16[2,128,128]{2,1,0:T(8,128)(2,1)S(1)} %get-tuple-element.60.out) | copy-start | bytes 196612
  105.0 14.2 %all-to-all-start.4 = ((f16[8,144,128]{2,1,0:T(8,128)(2,1)}), f16[8,144,128]{2,1,0:T(8,128)(2,1)S(1)}, u32[]{:S(2)}, u32[]{:S(2)}) async-start(f16[8,144,128]{2,1,0:T(8,128)(2,1)} %broadcast_in_dim.13), calls=%async_computation.4 | async-start | bytes 589824 | tf_op jit(solution)/shard_map/all_to_all | solution.py:391
  108.4 10.8 %copy-start.7 = (f32[128,128]{1,0:T(8,128)S(1)}, f32[128,128]{1,0:T(8,128)}, u32[]{:S(2)}) copy-start(f32[128,128]{1,0:T(8,128)} %copy-done.6) | copy-start | bytes 196612
  108.5 0.9 copy-start.9
  110.6 27.3 %collective-permute-start.1 = (bf16[2,128,128]{2,1,0:T(8,128)(2,1)S(1)}, bf16[2,128,128]{2,1,0:T(8,128)(2,1)S(1)}, u32[]{:S(2)}, u32[]{:S(2)}) collective-permute-start(bf16[2,128,128]{2,1,0:T(8,128)(2,1)S(1)} %get-tuple-element.62), channel_id=1, source_target_pairs={{0,8},{8,0},{1,9},{9,1},{2,10},{10,2},{3,11},{11,3},{4,12},{12,4},... | collective-permute-start | bytes 196616 | tf_op jit(solution)/shard_map/ppermute | solution.py:399
  121.7 11.7 %copy-start.10 = (bf16[128,256]{1,0:T(8,128)(2,1)S(1)}, bf16[128,256]{1,0:T(8,128)(2,1)}, u32[]{:S(2)}) copy-start(bf16[128,256]{1,0:T(8,128)(2,1)} %hidden.3) | copy-start | bytes 196612
  121.7 11.7 %all-to-all-start.5 = ((f32[16,2,128]{2,1,0:T(2,128)}), f32[16,2,128]{2,1,0:T(2,128)S(1)}, u32[]{:S(2)}, u32[]{:S(2)}) async-start(f32[16,2,128]{2,1,0:T(2,128)} %bitcast.13), calls=%async_computation.5 | async-start | bytes 32768 | tf_op jit(solution)/shard_map/all_to_all | solution.py:479
  129.5 26.1 %copy-start.11 = (bf16[256,16]{0,1:T(8,128)(2,1)S(1)}, bf16[256,16]{0,1:T(8,128)(2,1)}, u32[]{:S(2)}) copy-start(bf16[256,16]{0,1:T(8,128)(2,1)} %param.8) | copy-start | bytes 24580
  134.2 17.3 %all-to-all-start.6 = ((f32[6,24,256]{2,1,0:T(8,128)}), f32[6,24,256]{2,1,0:T(8,128)S(1)}, u32[]{:S(2)}, u32[]{:S(2)}) async-start(f32[6,24,256]{2,1,0:T(8,128)} %get-tuple-element.80), calls=%async_computation.6 | async-start | bytes 294912 | tf_op jit(solution)/shard_map/all_to_all | solution.py:485
  138.6 17.9 %collective-permute-start.2 = (bf16[2,128,128]{2,1,0:T(8,128)(2,1)S(1)}, bf16[2,128,128]{2,1,0:T(8,128)(2,1)S(1)}, u32[]{:S(2)}, u32[]{:S(2)}) collective-permute-start(bf16[2,128,128]{2,1,0:T(8,128)(2,1)S(1)} %get-tuple-element.78), channel_id=1, source_target_pairs={{0,8},{8,0},{1,9},{9,1},{2,10},{10,2},{3,11},{11,3},{4,12},{12,4},... | collective-permute-start | bytes 196616 | tf_op jit(solution)/shard_map/ppermute | solution.py:399
  152.2 13.1 %all-to-all-start.7 = ((f32[8,24,256]{2,1,0:T(8,128)}), f32[8,24,256]{2,1,0:T(8,128)S(1)}, u32[]{:S(2)}, u32[]{:S(2)}) async-start(f32[8,24,256]{2,1,0:T(8,128)} %broadcast_in_dim.14), calls=%async_computation.7 | async-start | bytes 393216 | tf_op jit(solution)/shard_map/all_to_all | solution.py:391

commit v6 on v5

--- a/solution.py
+++ b/solution.py
@@ -25,20 +25,23 @@
     return hi, (x - hi.astype(F32)).astype(BF16)
 
 
+def along(dims, a_parts, b_parts):
+    return dot1(
+        jnp.concatenate(a_parts, axis=dims[0][0][0]),
+        jnp.concatenate(b_parts, axis=dims[0][1][0]),
+        dims,
+    )
+
+
 def dot2(a, b, dims=NN):
     hi, lo = split(a)
-    return dot1(hi, b, dims) + dot1(lo, b, dims)
-
-
-def dot2r(a, b, dims=NN):
-    hi, lo = split(b)
-    return dot1(a, hi, dims) + dot1(a, lo, dims)
+    return along(dims, [hi, lo], [b, b])
 
 
 def dot3(a, b, dims=NN):
     ah, al = split(a)
     bh, bl = split(b)
-    return dot1(ah, bh, dims) + (dot1(al, bh, dims) + dot1(ah, bl, dims))
+    return along(dims, [ah, al, ah], [bh, bh, bl])
 
 
 def index_grids():

time: 167 us -> 166 us (level)
  Pallas kernels: 19.4 us -> 17 us
    pallas_call x9, Pallas kernels: 17.6 us -> 15.1 us  [call(): pl.pallas_call(body, out_shape=[jax.ShapeDtypeStruct(s, t) for s, t in ou...]
where the time goes in v6:
time: 166 us; the launch traced here: 165 us
  blocking collectives  55.9 us (34%)
  starting transfers between devices  43.7 us (26%)
  waiting for transfers between devices  36.7 us (22%)
  Pallas kernels  17 us (10%)
  local copies, waits for them, and re-layouts  6.91 us (4%)
  other arithmetic  2.75 us (2%)
    all_to_all x2, blocking collectives, copies(): lax.all_to_all(jnp.broadcast_to(x[None], (count,) + x.shape), axis, 0, 0)  48 us
    all_to_all x3, waiting for transfers between devices, copies(): lax.all_to_all(jnp.broadcast_to(x[None], (count,) + x.shape), axis, 0, 0)  23.1 us
    ppermute x3, starting transfers between devices, swap(): return lax.ppermute(x, 'zl', [(0, 1), (1, 0)])  19.3 us
    pallas_call x9, Pallas kernels, call(): pl.pallas_call(body, out_shape=[jax.ShapeDtypeStruct(s, t) for s, t in ou...  15.1 us
    all_to_all x3, starting transfers between devices, copies(): lax.all_to_all(jnp.broadcast_to(x[None], (count,) + x.shape), axis, 0, 0)  13.9 us
    all_to_all x1, waiting for transfers between devices, per_device(): total = jnp.sum(lax.all_to_all(total, 'zh', 0, 0), axis=0)  9.53 us
    all_to_all x1, blocking collectives, per_device(): part = lax.all_to_all(part, ('head', 'zl'), 0, 0, tiled=True)  7.96 us
    all_to_all x1, starting transfers between devices, per_device(): message = lax.all_to_all(message.reshape(16, 2, L), ('head', 'zl'), 0, 0)  6.82 us
  transfers between devices with their start and end apart: 8, of which 5 were waited for; matrix products, arithmetic and copies ran while one was open for 2% of the time, Pallas kernels for 4%

profile of v6, /device:TPU:64, one launch (start us, length us, event | category | flops | bytes accessed | tf_op | source)
XLA Modules:
  0.0 164.8 jit_solution(17301251485355848851)
XLA Ops:
  0.6 1.9 %shard_map.126 = (f32[16,128]{1,0:T(8,128)}, bf16[4,128,128]{2,1,0:T(8,128)(2,1)}, bf16[6,128,128]{2,1,0:T(8,128)(2,1)}) custom-call(s32[1]{0:T(128)} %bitcast.side, s32[1]{0:T(128)} %bitcast.1.slot, f32[2]{0:T(128)} %bias.1, bf16[16,256]{1,0:T(8,128)(2,1)} %bitcast.35, bf16[128,256]{1,0:T(8,128)(2,1)} %hidden.3, bf16[128,256]{1,0:T(8,128)(2,1)} %k.1, ...), custom_call_target="tpu_custom_call" | custom-call | flops 10000000 | bytes 1000000 | tf_op jit(solution)/shard_map/pallas_call | solution.py:428
  2.5 10.6 %collective-permute-start = (bf16[6,128,128]{2,1,0:T(8,128)(2,1)}, bf16[6,128,128]{2,1,0:T(8,128)(2,1)S(1)}, u32[]{:S(2)}, u32[]{:S(2)}) collective-permute-start(bf16[6,128,128]{2,1,0:T(8,128)(2,1)} %get-tuple-element.46), channel_id=1, source_target_pairs={{0,8},{8,0},{1,9},{9,1},{2,10},{10,2},{3,11},{11,3},{4,12},{12,4},... | collective-permute-start | bytes 589832 | tf_op jit(solution)/shard_map/ppermute | solution.py:402
  13.1 8.0 %all_to_all.46 = f32[16,1,128]{2,1,0:T(1,128)S(1)} all-to-all(f32[16,1,128]{2,1,0:T(1,128)} %bitcast.36), channel_id=1, replica_groups=mesh['y'=8,'zh'=6,'zl'=2,'head'=8] {'head','zl'}, dimensions={0} | all-to-all | bytes 16384 | tf_op jit(solution)/shard_map/all_to_all | solution.py:442
  21.1 0.0 collective-permute-done.swapped
  21.1 0.0 copy-start
  21.1 0.9 copy-done
  22.0 5.0 %shard_map.127 = (f32[272,128]{1,0:T(8,128)S(1)}, f32[2,128]{1,0:T(2,128)S(1)}, f32[2,128,128]{2,1,0:T(8,128)S(1)}, f32[2,128,128]{2,1,0:T(8,128)S(1)}, f32[2,12...) custom-call(s32[1]{0:T(128)} %bitcast.side, f32[16,128]{1,0:T(8,128)S(1)} %bitcast.34, ...), custom_call_target="tpu_custom_call" | custom-call | flops 100000000 | bytes 335876 | tf_op jit(solution)/shard_map/pallas_call | solution.py:382
  27.0 0.1 broadcast_in_dim.10
  27.1 29.7 %all_to_all.47 = f16[6,272,128]{2,1,0:T(8,128)(2,1)S(1)} all-to-all(f16[6,272,128]{2,1,0:T(8,128)(2,1)S(1)} %broadcast_in_dim.10), channel_id=1, replica_groups=mesh['y'=8,'zh'=6,'zl'=2,'head'=8] {'zh'}, dimensions={0} | all-to-all | bytes 835584 | tf_op jit(solution)/shard_map/all_to_all | solution.py:394
  56.8 0.1 convert_element_type.28.got
  56.9 0.8 shard_map.128
  57.7 0.0 copy-start.1
  57.7 0.9 broadcast_in_dim.11
  58.6 7.1 %all-to-all-start.2 = ((f16[8,272,128]{2,1,0:T(8,128)(2,1)}), f16[8,272,128]{2,1,0:T(8,128)(2,1)}, u32[]{:S(2)}, u32[]{:S(2)}) async-start(f16[8,272,128]{2,1,0:T(8,128)(2,1)} %broadcast_in_dim.11), calls=%async_computation.2 | async-start | bytes 1114112 | tf_op jit(solution)/shard_map/all_to_all | solution.py:394
  65.7 0.0 copy-done.1
  65.7 1.7 %shard_map.129 = (f32[256,128]{1,0:T(8,128)S(1)}, f32[128,128]{1,0:T(8,128)S(1)}, f32[2,128,128]{2,1,0:T(8,128)S(1)}, f32[2,128,128]{2,1,0:T(8,128)S(1)}, f32[2,...) custom-call(s32[1]{0:T(128)} %bitcast.7.place, s32[1]{0:T(128)} %bitcast.side, f32[2,128]{1,0:T(2,128)S(1)} %get-tuple-element.47.lg, ...), custom_call_target="tpu_custom_call" | custom-call | flops 100000000 | bytes 1557512 | tf_op jit(solution)/shard_map/pallas_call | solution.py:382
  67.4 0.0 copy-start.2
  67.4 0.6 copy-done.2
  68.1 0.0 copy-start.4
  68.1 11.4 %all-to-all-done.2 = f16[8,272,128]{2,1,0:T(8,128)(2,1)} async-done(((f16[8,272,128]{2,1,0:T(8,128)(2,1)}), f16[8,272,128]{2,1,0:T(8,128)(2,1)}, u32[]{:S(2)}, u32[]{:S(2)}) %all-to-all-start.2) | async-done | bytes 557088 | tf_op jit(solution)/shard_map/all_to_all | solution.py:394
  79.5 0.0 copy-start.3
  79.5 1.2 convert_element_type.30.got
  80.6 0.0 copy-done.4
  80.6 0.0 copy-done.3
  80.7 0.0 copy-start.5
  80.7 0.9 copy-done.5
  81.6 2.3 %shard_map.130 = (bf16[2,128,128]{2,1,0:T(8,128)(2,1)S(1)}, f32[2,128,128]{2,1,0:T(8,128)S(1)}, f32[2,128,128]{2,1,0:T(8,128)S(1)}, f32[128,128]{1,0:T(8,128)S(1)}, f32[144,128]{1,0:T(8,128)S(1)}) custom-call(s32[1]{0:T(128)} %bitcast.6.place, s32[1]{0:T(128)} %bitcast.side, f32[8,272,128]{2,1,0:T(8,128)S(1)} %convert_element_type.30.got, ...), custom_call_target="tpu_custom_call" | custom-call | flops 100000000 | bytes 2097160 | tf_op jit(solution)/shard_map/pallas_call | solution.py:382
  83.8 0.0 copy-start.6
  83.9 0.0 copy-start.8
  83.9 18.3 %all_to_all.48 = f16[6,144,128]{2,1,0:T(8,128)(2,1)S(1)} all-to-all(f16[6,144,128]{2,1,0:T(8,128)(2,1)S(1)} %broadcast_in_dim.12), channel_id=1, replica_groups=mesh['y'=8,'zh'=6,'zl'=2,'head'=8] {'zh'}, dimensions={0} | all-to-all | bytes 442368 | tf_op jit(solution)/shard_map/all_to_all | solution.py:394
  102.2 0.8 shard_map.132
  103.0 0.0 copy-done.6
  103.1 0.0 copy-done.8
  103.1 0.7 broadcast_in_dim.13
  103.8 3.4 %all-to-all-start.4 = ((f16[8,144,128]{2,1,0:T(8,128)(2,1)}), f16[8,144,128]{2,1,0:T(8,128)(2,1)S(1)}, u32[]{:S(2)}, u32[]{:S(2)}) async-start(f16[8,144,128]{2,1,0:T(8,128)(2,1)} %broadcast_in_dim.13), calls=%async_computation.4 | async-start | bytes 589824 | tf_op jit(solution)/shard_map/all_to_all | solution.py:394
  107.3 0.0 copy-start.7
  107.3 0.0 copy-start.9
  107.3 0.9 copy-done.9
  108.1 1.0 shard_map.131
  109.2 5.3 %collective-permute-start.1 = (bf16[2,128,128]{2,1,0:T(8,128)(2,1)S(1)}, bf16[2,128,128]{2,1,0:T(8,128)(2,1)S(1)}, u32[]{:S(2)}, u32[]{:S(2)}) collective-permute-start(bf16[2,128,128]{2,1,0:T(8,128)(2,1)S(1)} %get-tuple-element.62), channel_id=1, source_target_pairs={{0,8},{8,0},{1,9},{9,1},{2,10},{10,2},{3,11},{11,3},{4,12},{12,4},... | collective-permute-start | bytes 196616 | tf_op jit(solution)/shard_map/ppermute | solution.py:402
  114.5 3.5 %all-to-all-done.4 = f16[8,144,128]{2,1,0:T(8,128)(2,1)S(1)} async-done(((f16[8,144,128]{2,1,0:T(8,128)(2,1)}), f16[8,144,128]{2,1,0:T(8,128)(2,1)S(1)}, u32[]{:S(2)}, u32[]{:S(2)}) %all-to-all-start.4) | async-done | bytes 294944 | tf_op jit(solution)/shard_map/all_to_all | solution.py:394
  118.0 0.0 copy-done.7
  118.0 2.0 %shard_map.133 = (f32[2,128,128]{2,1,0:T(8,128)S(1)}, f32[2,128,128]{2,1,0:T(8,128)S(1)}, f32[32,128]{1,0:T(8,128)}) custom-call(s32[1]{0:T(128)} %bitcast.6.place, f32[8,272,128]{2,1,0:T(8,128)S(1)} %convert_element_type.30.got, f32[8,144,128]{2,1,0:T(8,128)S(1)} %convert_element_type.34.gives, f32[128,128]{1,0:T(8,128)S(1)} %get-tuple-element.65.matrix, ...), custom_call_target="tpu_custom_call" | custom-call | flops 100000000 | bytes 2425860 | tf_op jit(solution)/shard_map/pallas_call | solution.py:382
  120.0 0.0 copy-start.10
  120.0 6.8 %all-to-all-start.5 = ((f32[16,2,128]{2,1,0:T(2,128)}), f32[16,2,128]{2,1,0:T(2,128)S(1)}, u32[]{:S(2)}, u32[]{:S(2)}) async-start(f32[16,2,128]{2,1,0:T(2,128)} %bitcast.13), calls=%async_computation.5 | async-start | bytes 32768 | tf_op jit(solution)/shard_map/all_to_all | solution.py:482
  126.9 0.7 shard_map.134
  127.6 0.0 copy-start.11
  127.6 4.1 %all-to-all-done.5 = f32[16,2,128]{2,1,0:T(2,128)S(1)} async-done(((f32[16,2,128]{2,1,0:T(2,128)}), f32[16,2,128]{2,1,0:T(2,128)S(1)}, u32[]{:S(2)}, u32[]{:S(2)}) %all-to-all-start.5) | async-done | bytes 16416 | tf_op jit(solution)/shard_map/all_to_all | solution.py:482
  131.7 0.0 copy-done.10
  131.7 0.8 shard_map.135
  132.5 3.7 %all-to-all-start.6 = ((f32[6,24,256]{2,1,0:T(8,128)}), f32[6,24,256]{2,1,0:T(8,128)S(1)}, u32[]{:S(2)}, u32[]{:S(2)}) async-start(f32[6,24,256]{2,1,0:T(8,128)} %get-tuple-element.80), calls=%async_computation.6 | async-start | bytes 294912 | tf_op jit(solution)/shard_map/all_to_all | solution.py:488
  136.2 0.0 collective-permute-done.1
  136.2 0.7 maximum_select_fusion
  136.9 3.4 %collective-permute-start.2 = (bf16[2,128,128]{2,1,0:T(8,128)(2,1)S(1)}, bf16[2,128,128]{2,1,0:T(8,128)(2,1)S(1)}, u32[]{:S(2)}, u32[]{:S(2)}) collective-permute-start(bf16[2,128,128]{2,1,0:T(8,128)(2,1)S(1)} %get-tuple-element.78), channel_id=1, source_target_pairs={{0,8},{8,0},{1,9},{9,1},{2,10},{10,2},{3,11},{11,3},{4,12},{12,4},... | collective-permute-start | bytes 196616 | tf_op jit(solution)/shard_map/ppermute | solution.py:402
  140.3 9.5 %all-to-all-done.6 = f32[6,24,256]{2,1,0:T(8,128)S(1)} async-done(((f32[6,24,256]{2,1,0:T(8,128)}), f32[6,24,256]{2,1,0:T(8,128)S(1)}, u32[]{:S(2)}, u32[]{:S(2)}) %all-to-all-start.6) | async-done | bytes 147488 | tf_op jit(solution)/shard_map/all_to_all | solution.py:488
  149.9 0.7 broadcast_in_dim.14
  150.6 3.4 %all-to-all-start.7 = ((f32[8,24,256]{2,1,0:T(8,128)}), f32[8,24,256]{2,1,0:T(8,128)S(1)}, u32[]{:S(2)}, u32[]{:S(2)}) async-start(f32[8,24,256]{2,1,0:T(8,128)} %broadcast_in_dim.14), calls=%async_computation.7 | async-start | bytes 393216 | tf_op jit(solution)/shard_map/all_to_all | solution.py:394
  154.0 0.0 copy-done.11
  154.0 0.8 convolution_convert_fusion
  154.8 0.0 collective-permute-done.2
  154.8 0.7 maximum_select_fusion.2
  155.5 8.1 %all-to-all-done.7 = f32[8,24,256]{2,1,0:T(8,128)S(1)} async-done(((f32[8,24,256]{2,1,0:T(8,128)}), f32[8,24,256]{2,1,0:T(8,128)S(1)}, u32[]{:S(2)}, u32[]{:S(2)}) %all-to-all-start.7) | async-done | bytes 196640 | tf_op jit(solution)/shard_map/all_to_all | solution.py:394
  163.7 0.5 slice_bitcast_fusion.9
  164.2 0.6 slice_bitcast_fusion.8
  (13 shorter events, 0.2 us)
Async XLA Ops:
  2.5 18.5 %collective-permute-start = (bf16[6,128,128]{2,1,0:T(8,128)(2,1)}, bf16[6,128,128]{2,1,0:T(8,128)(2,1)S(1)}, u32[]{:S(2)}, u32[]{:S(2)}) collective-permute-start(bf16[6,128,128]{2,1,0:T(8,128)(2,1)} %get-tuple-element.46), channel_id=1, source_target_pairs={{0,8},{8,0},{1,9},{9,1},{2,10},{10,2},{3,11},{11,3},{4,12},{12,4},... | collective-permute-start | bytes 589832 | tf_op jit(solution)/shard_map/ppermute | solution.py:402
  21.1 0.9 copy-start
  57.7 8.0 %copy-start.1 = (bf16[4,128,128]{2,1,0:T(8,128)(2,1)S(1)}, bf16[4,128,128]{2,1,0:T(8,128)(2,1)}, u32[]{:S(2)}) copy-start(bf16[4,128,128]{2,1,0:T(8,128)(2,1)} %get-tuple-element.45.mine.own.held) | copy-start | bytes 393220
  58.6 20.9 %all-to-all-start.2 = ((f16[8,272,128]{2,1,0:T(8,128)(2,1)}), f16[8,272,128]{2,1,0:T(8,128)(2,1)}, u32[]{:S(2)}, u32[]{:S(2)}) async-start(f16[8,272,128]{2,1,0:T(8,128)(2,1)} %broadcast_in_dim.11), calls=%async_computation.2 | async-start | bytes 1114112 | tf_op jit(solution)/shard_map/all_to_all | solution.py:394
  67.4 0.7 copy-start.2
  68.1 12.6 %copy-start.4 = (f32[2,128,128]{2,1,0:T(8,128)}, f32[2,128,128]{2,1,0:T(8,128)S(1)}, u32[]{:S(2)}) copy-start(f32[2,128,128]{2,1,0:T(8,128)S(1)} %get-tuple-element.56.fixed) | copy-start | bytes 393220
  79.5 1.2 copy-start.3
  80.7 0.9 copy-start.5
  83.8 19.2 %copy-start.6 = (f32[128,128]{1,0:T(8,128)}, f32[128,128]{1,0:T(8,128)S(1)}, u32[]{:S(2)}) copy-start(f32[128,128]{1,0:T(8,128)S(1)} %get-tuple-element.67.give) | copy-start | bytes 196612
  83.9 19.2 %copy-start.8 = (bf16[2,128,128]{2,1,0:T(8,128)(2,1)}, bf16[2,128,128]{2,1,0:T(8,128)(2,1)S(1)}, u32[]{:S(2)}) copy-start(bf16[2,128,128]{2,1,0:T(8,128)(2,1)S(1)} %get-tuple-element.60.out) | copy-start | bytes 196612
  103.8 14.2 %all-to-all-start.4 = ((f16[8,144,128]{2,1,0:T(8,128)(2,1)}), f16[8,144,128]{2,1,0:T(8,128)(2,1)S(1)}, u32[]{:S(2)}, u32[]{:S(2)}) async-start(f16[8,144,128]{2,1,0:T(8,128)(2,1)} %broadcast_in_dim.13), calls=%async_computation.4 | async-start | bytes 589824 | tf_op jit(solution)/shard_map/all_to_all | solution.py:394
  107.3 10.8 %copy-start.7 = (f32[128,128]{1,0:T(8,128)S(1)}, f32[128,128]{1,0:T(8,128)}, u32[]{:S(2)}) copy-start(f32[128,128]{1,0:T(8,128)} %copy-done.6) | copy-start | bytes 196612
  107.3 0.9 copy-start.9
  109.2 27.0 %collective-permute-start.1 = (bf16[2,128,128]{2,1,0:T(8,128)(2,1)S(1)}, bf16[2,128,128]{2,1,0:T(8,128)(2,1)S(1)}, u32[]{:S(2)}, u32[]{:S(2)}) collective-permute-start(bf16[2,128,128]{2,1,0:T(8,128)(2,1)S(1)} %get-tuple-element.62), channel_id=1, source_target_pairs={{0,8},{8,0},{1,9},{9,1},{2,10},{10,2},{3,11},{11,3},{4,12},{12,4},... | collective-permute-start | bytes 196616 | tf_op jit(solution)/shard_map/ppermute | solution.py:402
  120.0 11.7 %copy-start.10 = (bf16[128,256]{1,0:T(8,128)(2,1)S(1)}, bf16[128,256]{1,0:T(8,128)(2,1)}, u32[]{:S(2)}) copy-start(bf16[128,256]{1,0:T(8,128)(2,1)} %hidden.3) | copy-start | bytes 196612
  120.0 11.7 %all-to-all-start.5 = ((f32[16,2,128]{2,1,0:T(2,128)}), f32[16,2,128]{2,1,0:T(2,128)S(1)}, u32[]{:S(2)}, u32[]{:S(2)}) async-start(f32[16,2,128]{2,1,0:T(2,128)} %bitcast.13), calls=%async_computation.5 | async-start | bytes 32768 | tf_op jit(solution)/shard_map/all_to_all | solution.py:482
  127.6 26.4 %copy-start.11 = (bf16[256,16]{0,1:T(8,128)(2,1)S(1)}, bf16[256,16]{0,1:T(8,128)(2,1)}, u32[]{:S(2)}) copy-start(bf16[256,16]{0,1:T(8,128)(2,1)} %param.8) | copy-start | bytes 24580
  132.5 17.4 %all-to-all-start.6 = ((f32[6,24,256]{2,1,0:T(8,128)}), f32[6,24,256]{2,1,0:T(8,128)S(1)}, u32[]{:S(2)}, u32[]{:S(2)}) async-start(f32[6,24,256]{2,1,0:T(8,128)} %get-tuple-element.80), calls=%async_computation.6 | async-start | bytes 294912 | tf_op jit(solution)/shard_map/all_to_all | solution.py:488
  136.9 17.9 %collective-permute-start.2 = (bf16[2,128,128]{2,1,0:T(8,128)(2,1)S(1)}, bf16[2,128,128]{2,1,0:T(8,128)(2,1)S(1)}, u32[]{:S(2)}, u32[]{:S(2)}) collective-permute-start(bf16[2,128,128]{2,1,0:T(8,128)(2,1)S(1)} %get-tuple-element.78), channel_id=1, source_target_pairs={{0,8},{8,0},{1,9},{9,1},{2,10},{10,2},{3,11},{11,3},{4,12},{12,4},... | collective-permute-start | bytes 196616 | tf_op jit(solution)/shard_map/ppermute | solution.py:402
  150.6 13.1 %all-to-all-start.7 = ((f32[8,24,256]{2,1,0:T(8,128)}), f32[8,24,256]{2,1,0:T(8,128)S(1)}, u32[]{:S(2)}, u32[]{:S(2)}) async-start(f32[8,24,256]{2,1,0:T(8,128)} %broadcast_in_dim.14), calls=%async_computation.7 | async-start | bytes 393216 | tf_op jit(solution)/shard_map/all_to_all | solution.py:394

commit v7 on v6

--- a/solution.py
+++ b/solution.py
@@ -372,6 +372,25 @@
         total[i, 16:24] = jnp.broadcast_to(line, (8, 2 * D))
 
 
+def added(got):
+    parts = [got[i] for i in range(got.shape[0])]
+    while len(parts) > 1:
+        parts = [sum(parts[i : i + 2]) for i in range(0, len(parts), 2)]
+    return parts[0]
+
+
+def kernel_add(got, total):
+    value = added(got)
+    for i in range(total.shape[0]):
+        total[i] = value
+
+
+def kernel_last(got, weight, bias):
+    value = added(got)
+    weight[...] = value[:16]
+    bias[...] = value[16:]
+
+
 VM = pl.BlockSpec(memory_space=pltpu.VMEM)
 SM = pl.BlockSpec(memory_space=pltpu.SMEM)
 
@@ -485,15 +504,20 @@
         at_s, at_h, message.reshape(32, L), hidden, swapped,
     )
     total, theirs_kv = lax.optimization_barrier((total, theirs_kv))
-    total = jnp.sum(lax.all_to_all(total, "zh", 0, 0), axis=0)
-    total = jnp.sum(copies(total, "y"), axis=0)
+    (total,) = call(
+        kernel_add, [((rows, 24, 2 * D), F32)], lax.all_to_all(total, "zh", 0, 0), flops=1e6
+    )
+    d_weight, d_bias = call(
+        kernel_last, [((16, 2 * D), F32), ((8, 2 * D), F32)],
+        lax.all_to_all(total, "y", 0, 0), flops=1e6,
+    )
     theirs_kv = swap(theirs_kv)
     d_hidden = lax.dot_general(
         grads, beta_weight, (((0,), (1,)), ((), ())), preferred_element_type=F32
     )
     out, dq = [joined(side, mine[i], theirs[i]) for i in range(2)]
     dk, dv = [joined(side, mine_kv[i], theirs_kv[i]) for i in range(2)]
-    return (out, dq, dk, dv, d_hidden.astype(BF16), total[:16].T, total[16, 0:2])
+    return (out, dq, dk, dv, d_hidden.astype(BF16), d_weight.T, d_bias[0, 0:2])
 
 
 def solution(mesh):

time: 166 us -> 166 us (level)
    all_to_all x1 -> x2, waiting for transfers between devices: 9.53 us -> 17.7 us  [the longest x1 9.53 us: per_device(): lax.all_to_all(total, 'zh', 0, 0)]
    all_to_all x3 -> x2, waiting for transfers between devices: 23.1 us -> 14.9 us  [copies(): lax.all_to_all(jnp.broadcast_to(x[None], (count,) + x.shape), axis, 0, 0)]
    all_to_all x3 -> x2, starting transfers between devices: 13.9 us -> 10.5 us  [copies(): lax.all_to_all(jnp.broadcast_to(x[None], (count,) + x.shape), axis, 0, 0)]
    all_to_all x1 -> x2, starting transfers between devices: 3.7 us -> 7.09 us  [the longest x1 3.7 us: per_device(): lax.all_to_all(total, 'zh', 0, 0)]
    pallas_call x9 -> x11, Pallas kernels: 15.1 us -> 16.4 us  [call(): pl.pallas_call(body, out_shape=[jax.ShapeDtypeStruct(s, t) for s, t in ou...]
  transfers between devices with their start and end apart: 8 -> 8, of which waited for: 5 -> 5; matrix products, arithmetic and copies ran while one was open for 2% -> 1% of each run, Pallas kernels for 4% -> 4%
where the time goes in v7:
time: 166 us; the launch traced here: 165 us
  blocking collectives  55.9 us (34%)
  starting transfers between devices  43.7 us (26%)
  waiting for transfers between devices  36.7 us (22%)
  Pallas kernels  18.3 us (11%)
  local copies, waits for them, and re-layouts  5.64 us (3%)
  other arithmetic  2.72 us (2%)
    all_to_all x2, blocking collectives, copies(): lax.all_to_all(jnp.broadcast_to(x[None], (count,) + x.shape), axis, 0, 0)  48 us
    ppermute x3, starting transfers between devices, swap(): return lax.ppermute(x, 'zl', [(0, 1), (1, 0)])  19.3 us
    pallas_call x11, Pallas kernels, call(): pl.pallas_call(body, out_shape=[jax.ShapeDtypeStruct(s, t) for s, t in ou...  16.4 us
    all_to_all x2, waiting for transfers between devices, copies(): lax.all_to_all(jnp.broadcast_to(x[None], (count,) + x.shape), axis, 0, 0)  14.9 us
    all_to_all x2, starting transfers between devices, copies(): lax.all_to_all(jnp.broadcast_to(x[None], (count,) + x.shape), axis, 0, 0)  10.5 us
    all_to_all x1, waiting for transfers between devices, per_device(): lax.all_to_all(total, 'zh', 0, 0)  9.53 us
    all_to_all x1, waiting for transfers between devices, per_device(): lax.all_to_all(total, 'y', 0, 0)  8.14 us
    all_to_all x1, blocking collectives, per_device(): part = lax.all_to_all(part, ('head', 'zl'), 0, 0, tiled=True)  7.96 us
  transfers between devices with their start and end apart: 8, of which 5 were waited for; matrix products, arithmetic and copies ran while one was open for 1% of the time, Pallas kernels for 4%

profile of v7, /device:TPU:64, one launch (start us, length us, event | category | flops | bytes accessed | tf_op | source)
XLA Modules:
  0.0 164.8 jit_solution(2440237038919396206)
XLA Ops:
  0.6 1.9 %shard_map.126 = (f32[16,128]{1,0:T(8,128)}, bf16[4,128,128]{2,1,0:T(8,128)(2,1)}, bf16[6,128,128]{2,1,0:T(8,128)(2,1)}) custom-call(s32[1]{0:T(128)} %bitcast.side, s32[1]{0:T(128)} %bitcast.1.slot, f32[2]{0:T(128)} %bias.1, bf16[16,256]{1,0:T(8,128)(2,1)} %bitcast.34, bf16[128,256]{1,0:T(8,128)(2,1)} %hidden.3, bf16[128,256]{1,0:T(8,128)(2,1)} %k.1, ...), custom_call_target="tpu_custom_call" | custom-call | flops 10000000 | bytes 1000000 | tf_op jit(solution)/shard_map/pallas_call | solution.py:447
  2.5 10.6 %collective-permute-start = (bf16[6,128,128]{2,1,0:T(8,128)(2,1)}, bf16[6,128,128]{2,1,0:T(8,128)(2,1)S(1)}, u32[]{:S(2)}, u32[]{:S(2)}) collective-permute-start(bf16[6,128,128]{2,1,0:T(8,128)(2,1)} %get-tuple-element.48), channel_id=1, source_target_pairs={{0,8},{8,0},{1,9},{9,1},{2,10},{10,2},{3,11},{11,3},{4,12},{12,4},... | collective-permute-start | bytes 589832 | tf_op jit(solution)/shard_map/ppermute | solution.py:421
  13.1 8.0 %all_to_all.46 = f32[16,1,128]{2,1,0:T(1,128)S(1)} all-to-all(f32[16,1,128]{2,1,0:T(1,128)} %bitcast.35), channel_id=1, replica_groups=mesh['y'=8,'zh'=6,'zl'=2,'head'=8] {'head','zl'}, dimensions={0} | all-to-all | bytes 16384 | tf_op jit(solution)/shard_map/all_to_all | solution.py:461
  21.1 0.0 collective-permute-done.swapped
  21.1 0.0 copy-start
  21.1 0.9 copy-done
  22.0 5.0 %shard_map.127 = (f32[272,128]{1,0:T(8,128)S(1)}, f32[2,128]{1,0:T(2,128)S(1)}, f32[2,128,128]{2,1,0:T(8,128)S(1)}, f32[2,128,128]{2,1,0:T(8,128)S(1)}, f32[2,12...) custom-call(s32[1]{0:T(128)} %bitcast.side, f32[16,128]{1,0:T(8,128)S(1)} %bitcast.33, ...), custom_call_target="tpu_custom_call" | custom-call | flops 100000000 | bytes 335876 | tf_op jit(solution)/shard_map/pallas_call | solution.py:401
  27.0 0.1 broadcast_in_dim.8
  27.1 29.7 %all_to_all.47 = f16[6,272,128]{2,1,0:T(8,128)(2,1)S(1)} all-to-all(f16[6,272,128]{2,1,0:T(8,128)(2,1)S(1)} %broadcast_in_dim.8), channel_id=1, replica_groups=mesh['y'=8,'zh'=6,'zl'=2,'head'=8] {'zh'}, dimensions={0} | all-to-all | bytes 835584 | tf_op jit(solution)/shard_map/all_to_all | solution.py:413
  56.8 0.1 convert_element_type.28.got
  56.9 0.8 shard_map.128
  57.7 0.0 copy-start.1
  57.7 0.9 broadcast_in_dim.9
  58.6 7.1 %all-to-all-start.2 = ((f16[8,272,128]{2,1,0:T(8,128)(2,1)}), f16[8,272,128]{2,1,0:T(8,128)(2,1)}, u32[]{:S(2)}, u32[]{:S(2)}) async-start(f16[8,272,128]{2,1,0:T(8,128)(2,1)} %broadcast_in_dim.9), calls=%async_computation.2 | async-start | bytes 1114112 | tf_op jit(solution)/shard_map/all_to_all | solution.py:413
  65.7 0.0 copy-done.1
  65.8 1.7 %shard_map.129 = (f32[256,128]{1,0:T(8,128)S(1)}, f32[128,128]{1,0:T(8,128)S(1)}, f32[2,128,128]{2,1,0:T(8,128)S(1)}, f32[2,128,128]{2,1,0:T(8,128)S(1)}, f32[2,...) custom-call(s32[1]{0:T(128)} %bitcast.7.place, s32[1]{0:T(128)} %bitcast.side, f32[2,128]{1,0:T(2,128)S(1)} %get-tuple-element.49.lg, ...), custom_call_target="tpu_custom_call" | custom-call | flops 100000000 | bytes 1557512 | tf_op jit(solution)/shard_map/pallas_call | solution.py:401
  67.4 0.0 copy-start.2
  67.5 0.6 copy-done.2
  68.1 0.0 copy-start.4
  68.1 11.4 %all-to-all-done.2 = f16[8,272,128]{2,1,0:T(8,128)(2,1)} async-done(((f16[8,272,128]{2,1,0:T(8,128)(2,1)}), f16[8,272,128]{2,1,0:T(8,128)(2,1)}, u32[]{:S(2)}, u32[]{:S(2)}) %all-to-all-start.2) | async-done | bytes 557088 | tf_op jit(solution)/shard_map/all_to_all | solution.py:413
  79.5 0.0 copy-start.3
  79.5 1.2 convert_element_type.30.got
  80.7 0.0 copy-done.4
  80.7 0.0 copy-done.3
  80.7 0.0 copy-start.5
  80.7 0.9 copy-done.5
  81.6 2.3 %shard_map.130 = (bf16[2,128,128]{2,1,0:T(8,128)(2,1)S(1)}, f32[2,128,128]{2,1,0:T(8,128)S(1)}, f32[2,128,128]{2,1,0:T(8,128)S(1)}, f32[128,128]{1,0:T(8,128)S(1)}, f32[144,128]{1,0:T(8,128)S(1)}) custom-call(s32[1]{0:T(128)} %bitcast.6.place, s32[1]{0:T(128)} %bitcast.side, f32[8,272,128]{2,1,0:T(8,128)S(1)} %convert_element_type.30.got, ...), custom_call_target="tpu_custom_call" | custom-call | flops 100000000 | bytes 2097160 | tf_op jit(solution)/shard_map/pallas_call | solution.py:401
  83.9 0.0 copy-start.6
  83.9 0.0 copy-start.8
  83.9 18.3 %all_to_all.48 = f16[6,144,128]{2,1,0:T(8,128)(2,1)S(1)} all-to-all(f16[6,144,128]{2,1,0:T(8,128)(2,1)S(1)} %broadcast_in_dim.10), channel_id=1, replica_groups=mesh['y'=8,'zh'=6,'zl'=2,'head'=8] {'zh'}, dimensions={0} | all-to-all | bytes 442368 | tf_op jit(solution)/shard_map/all_to_all | solution.py:413
  102.3 0.8 shard_map.132
  103.1 0.0 copy-done.6
  103.1 0.0 copy-done.8
  103.1 0.8 broadcast_in_dim.11
  103.9 3.4 %all-to-all-start.4 = ((f16[8,144,128]{2,1,0:T(8,128)(2,1)}), f16[8,144,128]{2,1,0:T(8,128)(2,1)S(1)}, u32[]{:S(2)}, u32[]{:S(2)}) async-start(f16[8,144,128]{2,1,0:T(8,128)(2,1)} %broadcast_in_dim.11), calls=%async_computation.4 | async-start | bytes 589824 | tf_op jit(solution)/shard_map/all_to_all | solution.py:413
  107.3 0.0 copy-start.7
  107.3 0.0 copy-start.9
  107.3 0.9 copy-done.9
  108.2 1.0 shard_map.131
  109.2 5.3 %collective-permute-start.1 = (bf16[2,128,128]{2,1,0:T(8,128)(2,1)S(1)}, bf16[2,128,128]{2,1,0:T(8,128)(2,1)S(1)}, u32[]{:S(2)}, u32[]{:S(2)}) collective-permute-start(bf16[2,128,128]{2,1,0:T(8,128)(2,1)S(1)} %get-tuple-element.64), channel_id=1, source_target_pairs={{0,8},{8,0},{1,9},{9,1},{2,10},{10,2},{3,11},{11,3},{4,12},{12,4},... | collective-permute-start | bytes 196616 | tf_op jit(solution)/shard_map/ppermute | solution.py:421
  114.5 3.5 %all-to-all-done.4 = f16[8,144,128]{2,1,0:T(8,128)(2,1)S(1)} async-done(((f16[8,144,128]{2,1,0:T(8,128)(2,1)}), f16[8,144,128]{2,1,0:T(8,128)(2,1)S(1)}, u32[]{:S(2)}, u32[]{:S(2)}) %all-to-all-start.4) | async-done | bytes 294944 | tf_op jit(solution)/shard_map/all_to_all | solution.py:413
  118.1 0.0 copy-done.7
  118.1 2.0 %shard_map.133 = (f32[2,128,128]{2,1,0:T(8,128)S(1)}, f32[2,128,128]{2,1,0:T(8,128)S(1)}, f32[32,128]{1,0:T(8,128)}) custom-call(s32[1]{0:T(128)} %bitcast.6.place, f32[8,272,128]{2,1,0:T(8,128)S(1)} %convert_element_type.30.got, f32[8,144,128]{2,1,0:T(8,128)S(1)} %convert_element_type.34.gives, f32[128,128]{1,0:T(8,128)S(1)} %get-tuple-element.67.matrix, ...), custom_call_target="tpu_custom_call" | custom-call | flops 100000000 | bytes 2425860 | tf_op jit(solution)/shard_map/pallas_call | solution.py:401
  120.1 0.0 copy-start.10
  120.1 6.8 %all-to-all-start.5 = ((f32[16,2,128]{2,1,0:T(2,128)}), f32[16,2,128]{2,1,0:T(2,128)S(1)}, u32[]{:S(2)}, u32[]{:S(2)}) async-start(f32[16,2,128]{2,1,0:T(2,128)} %bitcast.13), calls=%async_computation.5 | async-start | bytes 32768 | tf_op jit(solution)/shard_map/all_to_all | solution.py:501
  126.9 0.7 shard_map.134
  127.6 0.0 copy-start.11
  127.6 4.1 %all-to-all-done.5 = f32[16,2,128]{2,1,0:T(2,128)S(1)} async-done(((f32[16,2,128]{2,1,0:T(2,128)}), f32[16,2,128]{2,1,0:T(2,128)S(1)}, u32[]{:S(2)}, u32[]{:S(2)}) %all-to-all-start.5) | async-done | bytes 16416 | tf_op jit(solution)/shard_map/all_to_all | solution.py:501
  131.7 0.0 copy-done.10
  131.7 0.8 shard_map.135
  132.5 3.7 %all-to-all-start.6 = ((f32[6,24,256]{2,1,0:T(8,128)}), f32[6,24,256]{2,1,0:T(8,128)S(1)}, u32[]{:S(2)}, u32[]{:S(2)}) async-start(f32[6,24,256]{2,1,0:T(8,128)} %get-tuple-element.82), calls=%async_computation.6 | async-start | bytes 294912 | tf_op jit(solution)/shard_map/all_to_all | solution.py:508
  136.2 0.0 collective-permute-done.1
  136.2 0.7 maximum_select_fusion
  136.9 3.4 %collective-permute-start.2 = (bf16[2,128,128]{2,1,0:T(8,128)(2,1)S(1)}, bf16[2,128,128]{2,1,0:T(8,128)(2,1)S(1)}, u32[]{:S(2)}, u32[]{:S(2)}) collective-permute-start(bf16[2,128,128]{2,1,0:T(8,128)(2,1)S(1)} %get-tuple-element.80), channel_id=1, source_target_pairs={{0,8},{8,0},{1,9},{9,1},{2,10},{10,2},{3,11},{11,3},{4,12},{12,4},... | collective-permute-start | bytes 196616 | tf_op jit(solution)/shard_map/ppermute | solution.py:421
  140.4 9.5 %all-to-all-done.6.got = f32[6,24,256]{2,1,0:T(8,128)S(1)} async-done(((f32[6,24,256]{2,1,0:T(8,128)}), f32[6,24,256]{2,1,0:T(8,128)S(1)}, u32[]{:S(2)}, u32[]{:S(2)}) %all-to-all-start.6) | async-done | bytes 147488 | tf_op jit(solution)/shard_map/all_to_all | solution.py:508
  149.9 0.7 shard_map.136
  150.6 3.4 %all-to-all-start.7 = ((f32[8,24,256]{2,1,0:T(8,128)}), f32[8,24,256]{2,1,0:T(8,128)S(1)}, u32[]{:S(2)}, u32[]{:S(2)}) async-start(f32[8,24,256]{2,1,0:T(8,128)} %shard_map.136), calls=%async_computation.7 | async-start | bytes 393216 | tf_op jit(solution)/shard_map/all_to_all | solution.py:512
  154.0 0.0 copy-done.11
  154.0 0.8 convolution_convert_fusion
  154.8 0.0 collective-permute-done.2
  154.8 0.7 maximum_select_fusion.2
  155.5 8.1 %all-to-all-done.7.got = f32[8,24,256]{2,1,0:T(8,128)S(1)} async-done(((f32[8,24,256]{2,1,0:T(8,128)}), f32[8,24,256]{2,1,0:T(8,128)S(1)}, u32[]{:S(2)}, u32[]{:S(2)}) %all-to-all-start.7) | async-done | bytes 196640 | tf_op jit(solution)/shard_map/all_to_all | solution.py:512
  163.7 0.6 shard_map.137
  164.3 0.5 slice_bitcast_fusion.8
  (11 shorter events, 0.2 us)
Async XLA Ops:
  2.5 18.5 %collective-permute-start = (bf16[6,128,128]{2,1,0:T(8,128)(2,1)}, bf16[6,128,128]{2,1,0:T(8,128)(2,1)S(1)}, u32[]{:S(2)}, u32[]{:S(2)}) collective-permute-start(bf16[6,128,128]{2,1,0:T(8,128)(2,1)} %get-tuple-element.48), channel_id=1, source_target_pairs={{0,8},{8,0},{1,9},{9,1},{2,10},{10,2},{3,11},{11,3},{4,12},{12,4},... | collective-permute-start | bytes 589832 | tf_op jit(solution)/shard_map/ppermute | solution.py:421
  21.1 0.9 copy-start
  57.7 8.0 %copy-start.1 = (bf16[4,128,128]{2,1,0:T(8,128)(2,1)S(1)}, bf16[4,128,128]{2,1,0:T(8,128)(2,1)}, u32[]{:S(2)}) copy-start(bf16[4,128,128]{2,1,0:T(8,128)(2,1)} %get-tuple-element.47.mine.own.held) | copy-start | bytes 393220
  58.6 20.8 %all-to-all-start.2 = ((f16[8,272,128]{2,1,0:T(8,128)(2,1)}), f16[8,272,128]{2,1,0:T(8,128)(2,1)}, u32[]{:S(2)}, u32[]{:S(2)}) async-start(f16[8,272,128]{2,1,0:T(8,128)(2,1)} %broadcast_in_dim.9), calls=%async_computation.2 | async-start | bytes 1114112 | tf_op jit(solution)/shard_map/all_to_all | solution.py:413
  67.4 0.6 copy-start.2
  68.1 12.6 %copy-start.4 = (f32[2,128,128]{2,1,0:T(8,128)}, f32[2,128,128]{2,1,0:T(8,128)S(1)}, u32[]{:S(2)}) copy-start(f32[2,128,128]{2,1,0:T(8,128)S(1)} %get-tuple-element.58.fixed) | copy-start | bytes 393220
  79.5 1.2 copy-start.3
  80.7 0.9 copy-start.5
  83.9 19.2 %copy-start.6 = (f32[128,128]{1,0:T(8,128)}, f32[128,128]{1,0:T(8,128)S(1)}, u32[]{:S(2)}) copy-start(f32[128,128]{1,0:T(8,128)S(1)} %get-tuple-element.69.give) | copy-start | bytes 196612
  83.9 19.2 %copy-start.8 = (bf16[2,128,128]{2,1,0:T(8,128)(2,1)}, bf16[2,128,128]{2,1,0:T(8,128)(2,1)S(1)}, u32[]{:S(2)}) copy-start(bf16[2,128,128]{2,1,0:T(8,128)(2,1)S(1)} %get-tuple-element.62.out) | copy-start | bytes 196612
  103.9 14.2 %all-to-all-start.4 = ((f16[8,144,128]{2,1,0:T(8,128)(2,1)}), f16[8,144,128]{2,1,0:T(8,128)(2,1)S(1)}, u32[]{:S(2)}, u32[]{:S(2)}) async-start(f16[8,144,128]{2,1,0:T(8,128)(2,1)} %broadcast_in_dim.11), calls=%async_computation.4 | async-start | bytes 589824 | tf_op jit(solution)/shard_map/all_to_all | solution.py:413
  107.3 10.8 %copy-start.7 = (f32[128,128]{1,0:T(8,128)S(1)}, f32[128,128]{1,0:T(8,128)}, u32[]{:S(2)}) copy-start(f32[128,128]{1,0:T(8,128)} %copy-done.6) | copy-start | bytes 196612
  107.3 0.9 copy-start.9
  109.2 27.0 %collective-permute-start.1 = (bf16[2,128,128]{2,1,0:T(8,128)(2,1)S(1)}, bf16[2,128,128]{2,1,0:T(8,128)(2,1)S(1)}, u32[]{:S(2)}, u32[]{:S(2)}) collective-permute-start(bf16[2,128,128]{2,1,0:T(8,128)(2,1)S(1)} %get-tuple-element.64), channel_id=1, source_target_pairs={{0,8},{8,0},{1,9},{9,1},{2,10},{10,2},{3,11},{11,3},{4,12},{12,4},... | collective-permute-start | bytes 196616 | tf_op jit(solution)/shard_map/ppermute | solution.py:421
  120.1 11.7 %copy-start.10 = (bf16[128,256]{1,0:T(8,128)(2,1)S(1)}, bf16[128,256]{1,0:T(8,128)(2,1)}, u32[]{:S(2)}) copy-start(bf16[128,256]{1,0:T(8,128)(2,1)} %hidden.3) | copy-start | bytes 196612
  120.1 11.7 %all-to-all-start.5 = ((f32[16,2,128]{2,1,0:T(2,128)}), f32[16,2,128]{2,1,0:T(2,128)S(1)}, u32[]{:S(2)}, u32[]{:S(2)}) async-start(f32[16,2,128]{2,1,0:T(2,128)} %bitcast.13), calls=%async_computation.5 | async-start | bytes 32768 | tf_op jit(solution)/shard_map/all_to_all | solution.py:501
  127.6 26.3 %copy-start.11 = (bf16[256,16]{0,1:T(8,128)(2,1)S(1)}, bf16[256,16]{0,1:T(8,128)(2,1)}, u32[]{:S(2)}) copy-start(bf16[256,16]{0,1:T(8,128)(2,1)} %param.8) | copy-start | bytes 24580
  132.5 17.4 %all-to-all-start.6 = ((f32[6,24,256]{2,1,0:T(8,128)}), f32[6,24,256]{2,1,0:T(8,128)S(1)}, u32[]{:S(2)}, u32[]{:S(2)}) async-start(f32[6,24,256]{2,1,0:T(8,128)} %get-tuple-element.82), calls=%async_computation.6 | async-start | bytes 294912 | tf_op jit(solution)/shard_map/all_to_all | solution.py:508
  136.9 17.9 %collective-permute-start.2 = (bf16[2,128,128]{2,1,0:T(8,128)(2,1)S(1)}, bf16[2,128,128]{2,1,0:T(8,128)(2,1)S(1)}, u32[]{:S(2)}, u32[]{:S(2)}) collective-permute-start(bf16[2,128,128]{2,1,0:T(8,128)(2,1)S(1)} %get-tuple-element.80), channel_id=1, source_target_pairs={{0,8},{8,0},{1,9},{9,1},{2,10},{10,2},{3,11},{11,3},{4,12},{12,4},... | collective-permute-start | bytes 196616 | tf_op jit(solution)/shard_map/ppermute | solution.py:421
  150.6 13.1 %all-to-all-start.7 = ((f32[8,24,256]{2,1,0:T(8,128)}), f32[8,24,256]{2,1,0:T(8,128)S(1)}, u32[]{:S(2)}, u32[]{:S(2)}) async-start(f32[8,24,256]{2,1,0:T(8,128)} %shard_map.136), calls=%async_computation.7 | async-start | bytes 393216 | tf_op jit(solution)/shard_map/all_to_all | solution.py:512
